TPU v7x, 256 devices: a whole 4x4x8 slice. The times are simulated.
256 devices in a mesh: grp: 4 (over x), gx: 8 (over z), gy: 8 (over y, core).
Axes of the slice: x: 4, y: 4, z: 8, core: 2. Of those that a mesh axis runs over, the one named last changes fastest.
Arguments:
- air: float32 [3, 80, 512, 1024], P(None, None, ('grp', 'gx'), 'gy'), may hold values from -6 to 6
- level_set: float32 [8192, 128, 128], P(('grp', 'gx', 'gy')), may hold values from -12 to 12
- fuel: int32 [8192, 128, 128], P(('grp', 'gx', 'gy')), may hold values from 0 to 12
- tile_list: int32 [4, 64, 32], P('grp'), may hold values from -1 to 2047, as said below
Outputs:
- air_next: float32 [3, 80, 512, 1024], P(None, None, ('grp', 'gx'), 'gy')
- level_set_next: float32 [8192, 128, 128], P(('grp', 'gx', 'gy'))
Inputs may be any that keep to these rules, and one draw needn't show every extreme that they name: `tile_list`: in each band, every device's live slots come first and name tiles over distinct devices of the band; no tile is named twice; some device of each band has all 32 slots live; a tile t lies over device t // 32 of the band (index gx * 8 + gy).
All inputs are finite; a program needn't handle non-finite values.
Results may differ from a plain program's by a relative error of at most 0.0003.
Values sent between devices are 32-bit elements; how exact they have to be, the bound alone decides.
No kernel may reach another device: no remote copies, remote signals or barrier semaphores. Data moves between devices by JAX's collectives and lax.ppermute only.
A program may use at most 128 MiB of HBM per device.

v0:
```python
import jax
import jax.numpy as jnp
import numpy as np
from jax import lax
from jax.sharding import PartitionSpec as P

SUB = 4


spread_rates = np.array(
    [0.3, 0.5, 0.9, 1.2, 0.6, 0.4, 0.7, 0.35, 0.25, 0.45, 0.55, 0.8, 1.0], np.float32
)
heat_yields = np.array(
    [1.0, 2.5, 4.0, 3.0, 1.5, 2.0, 5.0, 1.2, 0.8, 3.5, 2.2, 4.5, 2.8], np.float32
)
smoke_yields = np.array(
    [0.5, 1.5, 2.5, 1.0, 3.0, 0.8, 2.0, 1.8, 0.6, 2.6, 1.1, 3.4, 1.4], np.float32
)
courant = 0.1
viscosity = 0.1
buoyancy = 0.5
source_step = 0.5
fire_time = 0.1
wind_gain = 0.3


def with_halo(cells, sides, width):
    for axis, dim in sides:
        count = lax.axis_size(axis)
        ends = count - 1
        head = lax.slice_in_dim(cells, 0, width, axis=dim)
        tail = lax.slice_in_dim(cells, cells.shape[dim] - width, cells.shape[dim], axis=dim)
        cells = jnp.concatenate(
            [
                lax.ppermute(tail, axis, [(i, (i + 1) % count) for i in range(ends)]),
                cells,
                lax.ppermute(head, axis, [((i + 1) % count, i) for i in range(ends)]),
            ],
            axis=dim,
        )
    return cells


def lookup(category, table):
    result = jnp.zeros(category.shape, jnp.float32)
    for position in range(13):
        result = jnp.where(category == position, jnp.float32(table[position]), result)
    return result


def weights_table(cells, refine):
    spots = (jnp.arange(cells, dtype=jnp.float32) + 0.5) / refine + 0.5
    knots = jnp.arange(10, dtype=jnp.float32)
    return jnp.maximum(0.0, 1.0 - jnp.abs(spots[:, None] - knots[None, :]))


def fire_advance(phase, category, window, active):
    cells = phase.shape[0]
    refine = cells // 8
    table = weights_table(cells, refine)
    highest = lax.Precision.HIGHEST
    row_wind = jnp.dot(jnp.dot(table, window[0], precision=highest), table.T, precision=highest)
    col_wind = jnp.dot(jnp.dot(table, window[1], precision=highest), table.T, precision=highest)
    base_rate = lookup(category, spread_rates)
    for substep in range(SUB):
        padded = jnp.pad(phase, 1, mode="edge")
        back_row = phase - padded[:-2, 1:-1]
        ahead_row = padded[2:, 1:-1] - phase
        back_col = phase - padded[1:-1, :-2]
        ahead_col = padded[1:-1, 2:] - phase
        upwind = (
            jnp.maximum(back_row, 0.0) ** 2
            + jnp.minimum(ahead_row, 0.0) ** 2
            + jnp.maximum(back_col, 0.0) ** 2
            + jnp.minimum(ahead_col, 0.0) ** 2
        )
        slope_row = 0.5 * (back_row + ahead_row)
        slope_col = 0.5 * (back_col + ahead_col)
        length = jnp.maximum(jnp.sqrt(slope_row * slope_row + slope_col * slope_col), 1.0)
        along = (row_wind * slope_row + col_wind * slope_col) / length
        rate = base_rate * (1.0 + wind_gain * jnp.maximum(along, 0.0))
        phase = phase - fire_time * rate * jnp.sqrt(upwind)
    burning = jax.nn.sigmoid(-phase)
    heat = (lookup(category, heat_yields) * burning).reshape(8, refine, 8, refine).mean(axis=(1, 3))
    smoke = (
        (lookup(category, smoke_yields) * burning).reshape(8, refine, 8, refine).mean(axis=(1, 3))
    )
    return (phase, jnp.concatenate([heat.reshape(64), smoke.reshape(64)]) * active)


def centre(field):
    return field[..., 1:-1, 1:-1]


def laplace(field):
    return (
        field[..., 2:, 1:-1]
        + field[..., :-2, 1:-1]
        + field[..., 1:-1, 2:]
        + field[..., 1:-1, :-2]
        - 4.0 * centre(field)
    )


def atmosphere(padded, heat_padded, emission):
    levels = padded.shape[1]
    profile = jnp.exp(-jnp.arange(levels, dtype=jnp.float32) * 8.0 / levels)[:, None, None]
    row_wind = centre(padded[0])
    col_wind = centre(padded[1])
    tracer = padded[2]
    middle = centre(tracer)
    upwind = (
        jnp.maximum(row_wind, 0.0) * (middle - tracer[:, :-2, 1:-1])
        + jnp.minimum(row_wind, 0.0) * (tracer[:, 2:, 1:-1] - middle)
        + jnp.maximum(col_wind, 0.0) * (middle - tracer[:, 1:-1, :-2])
        + jnp.minimum(col_wind, 0.0) * (tracer[:, 1:-1, 2:] - middle)
    )
    smoke_next = middle - courant * upwind + source_step * profile * emission
    heat_row = 0.5 * (heat_padded[2:, 1:-1] - heat_padded[:-2, 1:-1])
    heat_col = 0.5 * (heat_padded[1:-1, 2:] - heat_padded[1:-1, :-2])
    row_next = row_wind + viscosity * laplace(padded[0]) + buoyancy * profile * heat_row
    col_next = col_wind + viscosity * laplace(padded[1]) + buoyancy * profile * heat_col
    return jnp.stack([row_next, col_next, smoke_next])


def on_device(air, level_set, fuel, tile_list):
    highest = lax.Precision.HIGHEST
    rows_here = air.shape[2]
    cols_here = air.shape[3]
    padded = with_halo(air, ((("grp", "gx"), 2), ("gy", 3)), 1)
    surface = padded[0:2, 0]
    tile_cols = cols_here // 8
    tile_count = rows_here // 8 * tile_cols
    pieces = []
    for tile_at in range(tile_count):
        tile_row = tile_at // tile_cols
        tile_col = tile_at % tile_cols
        pieces.append(
            surface[:, tile_row * 8 : tile_row * 8 + 10, tile_col * 8 : tile_col * 8 + 10].reshape(
                200
            )
        )
    windows_all = jnp.stack(pieces)
    size_gx = lax.axis_size("gx")
    size_gy = lax.axis_size("gy")
    group_size = size_gx * size_gy
    myself = lax.axis_index("gx") * size_gy + lax.axis_index("gy")
    listed = tile_list[0]
    owner = listed // tile_count
    local_tile = listed % tile_count
    is_mine = (owner == myself) & (listed >= 0)
    tile_ids = jnp.arange(tile_count, dtype=jnp.int32)
    chosen = is_mine[:, :, None] & (local_tile[:, :, None] == tile_ids[None, None, :])
    choose = jnp.sum(chosen.astype(jnp.float32), axis=1)
    outgoing = jnp.dot(choose, windows_all, precision=highest)
    received = lax.all_to_all(outgoing, ("gx", "gy"), split_axis=0, concat_axis=0, tiled=True)
    my_slots = lax.dynamic_index_in_dim(listed, myself, 0, keepdims=False)
    slot_live = my_slots >= 0
    device_ids = jnp.arange(group_size, dtype=jnp.int32)
    picker = (
        ((my_slots // tile_count)[:, None] == device_ids[None, :]) & slot_live[:, None]
    ).astype(jnp.float32)
    windows = jnp.dot(picker, received, precision=highest).reshape(-1, 2, 10, 10)
    active = slot_live.astype(jnp.float32)
    phases, fluxes = jax.vmap(fire_advance)(level_set, fuel, windows, active)
    returning = jnp.dot(picker.T, fluxes, precision=highest)
    arrived = lax.all_to_all(returning, ("gx", "gy"), split_axis=0, concat_axis=0, tiled=True)
    per_tile = jnp.dot(choose.T, arrived, precision=highest)
    columns = (
        per_tile.reshape(rows_here // 8, tile_cols, 2, 8, 8)
        .transpose(2, 0, 3, 1, 4)
        .reshape(2, rows_here, cols_here)
    )
    heat_padded = with_halo(columns[0], ((("grp", "gx"), 0), ("gy", 1)), 1)
    return (atmosphere(padded, heat_padded, columns[1]), phases)


def solution(mesh):
    in_specs = (
        P(None, None, ("grp", "gx"), "gy"),
        P(("grp", "gx", "gy"), None, None),
        P(("grp", "gx", "gy"), None, None),
        P("grp", None, None),
    )
    out_specs = (P(None, None, ("grp", "gx"), "gy"), P(("grp", "gx", "gy"), None, None))
    return jax.shard_map(
        on_device, mesh=mesh, in_specs=in_specs, out_specs=out_specs, check_vma=False
    )
```

profile of v0, /device:TPU:2, one launch (start us, length us, event | category | flops | bytes accessed | tf_op | source)
XLA Modules:
  0.0 168.2 jit_solution(7513494441726887270)
XLA Ops:
  0.6 2.2 %copy.91 = f32[3,80,16,128]{1,3,2,0:T(8,128)S(1)} copy(f32[3,80,16,128]{3,2,1,0:T(8,128)} %param.4) | data formatting | bytes 3932160 | tf_op args[0]
  2.8 0.8 fusion.131
  3.6 7.7 %collective-permute-start.1 = (f32[3,80,1,128]{1,3,2,0:T(8,128)}, f32[3,80,1,128]{1,3,2,0:T(8,128)S(1)}, u32[]{:S(2)}, u32[]{:S(2)}) collective-permute-start(f32[3,80,1,128]{1,3,2,0:T(8,128)} %get-tuple-element.31), channel_id=1, source_target_pairs={{8,0},{16,8},{24,16},{32,24},{40,32},{48,40},{56,48},{64,56},{72,6... | collective-permute-start | bytes 368648 | tf_op jit(solution)/shard_map/ppermute | solution.py:37
  11.3 1.9 %collective-permute-start = (f32[3,80,1,128]{1,3,2,0:T(8,128)}, f32[3,80,1,128]{1,3,2,0:T(8,128)S(1)}, u32[]{:S(2)}, u32[]{:S(2)}) collective-permute-start(f32[3,80,1,128]{1,3,2,0:T(8,128)} %get-tuple-element.30), channel_id=1, source_target_pairs={{0,8},{8,16},{16,24},{24,32},{32,40},{40,48},{48,56},{56,64},{64,7... | collective-permute-start | bytes 368648 | tf_op jit(solution)/shard_map/ppermute | solution.py:35
  13.3 0.6 add_select_fusion
  13.9 0.6 fusion.93
  14.7 0.5 fusion.129
  15.2 1.0 fusion.139
  16.2 0.6 copy-done.5
  16.8 1.8 %pad_maximum_fusion.2 = f32[32,130,128]{2,1,0:T(8,128)S(1)} fusion(f32[32,1,128]{2,1,0:T(1,128)S(1)} %get-tuple-element.47, f32[32,128,128]{2,1,0:T(8,128)} %param.5, f32[32,1,128]{2,1,0:T(1,128)S(1)} %get-tuple-element.46), kind=kLoop, calls=%fused_computation.2 | loop fusion | flops 1064960 | bytes 4259840 | tf_op jit(solution)/shard_map/vmap(jit(_pad))/concatenate | solution.py:66
  18.6 2.8 %fusion.135 = (f32[32,130,1]{2,1,0:T(8,128)}, f32[32,130,1]{2,1,0:T(8,128)}) fusion(f32[32,130,128]{2,1,0:T(8,128)S(1)} %pad_maximum_fusion.2), kind=kLoop, calls=%fused_computation.247 | loop fusion | bytes 66560 | tf_op jit(solution)/shard_map/vmap(jit(_pad))/slice | solution.py:66
  21.4 0.5 and_select_fusion
  22.0 1.3 collective-permute-start.3
  23.3 3.0 %collective-permute-start.2 = (f32[3,80,18,1]{1,3,2,0:T(1,128)S(1)}, f32[3,80,18,1]{1,3,2,0:T(1,128)S(1)}, u32[]{:S(2)}, u32[]{:S(2)}) collective-permute-start(f32[3,80,18,1]{1,3,2,0:T(1,128)S(1)} %get-tuple-element.28), channel_id=1, source_target_pairs={{0,1},{1,2},{2,3},{3,4},{4,5},{5,6},{6,7},{8,9},{9,10},{10,11},{11... | collective-permute-start | bytes 51848 | tf_op jit(solution)/shard_map/ppermute | solution.py:35
  26.5 0.7 collective-permute-done.2
  27.1 0.5 pad_maximum_fusion
  27.7 1.8 %copy-done.1 = f32[3,80,18,130]{1,3,2,0:T(8,128)} copy-done((f32[3,80,18,130]{1,3,2,0:T(8,128)}, f32[3,80,18,130]{1,3,2,0:T(8,128)S(1)}, u32[]{:S(2)}) %copy-start.1) | copy-done | bytes 2246424
  29.7 1.3 copy.94
  35.2 0.7 copy.127
  35.9 11.2 %all-to-all-start = ((f32[64,1,200]{2,1,0:T(1,128)}), f32[64,1,200]{2,1,0:T(1,128)S(1)}, u32[]{:S(2)}, u32[]{:S(2)}) async-start(f32[64,1,200]{2,1,0:T(1,128)} %copy.127), calls=%async_computation | async-start | bytes 131072 | tf_op jit(solution)/shard_map/all_to_all | solution.py:156
  47.1 9.8 %all-to-all-done = f32[64,1,200]{2,1,0:T(1,128)S(1)} async-done(((f32[64,1,200]{2,1,0:T(1,128)}), f32[64,1,200]{2,1,0:T(1,128)S(1)}, u32[]{:S(2)}, u32[]{:S(2)}) %all-to-all-start) | async-done | bytes 51232 | tf_op jit(solution)/shard_map/all_to_all | solution.py:156
  57.4 0.5 fusion.80
  57.9 3.5 %fusion.76 = f32[128,32,128]{2,0,1:T(8,128)S(1)} fusion(f32[128,32,10]{0,1,2:T(8,128)S(1)} %fusion.80, f32[128]{0:T(128)S(1)} %multiply_add_fusion), kind=kOutput, calls=%fused_computation.156 | convolution fusion | flops 62919680 | bytes 2261504 | tf_op jit(solution)/shard_map/vmap()/dot_general | solution.py:62
  61.8 17.8 %fusion.24 = (f32[32,128,128]{2,1,0:T(8,128)S(1)}, f32[32,128,128]{2,1,0:T(8,128)S(1)}, pred[32,128,128]{2,1,0:T(8,128)(4,1)S(1)}, pred[32,128,128]{2,1,0:T(8,12...) fusion(f32[32,128,128]{2,1,0:T(8,128)} %param.5, ...), kind=kOutput, calls=%fused_computation.66 | convolution fusion | flops 98571264 | bytes 19629056 | tf_op jit(solution)/shard_map/vmap()/dot_general | solution.py:63
  79.9 0.7 fusion.134
  80.6 5.4 %fusion.33 = f32[32,128,128]{2,1,0:T(8,128)S(1)} fusion(f32[32,128,128]{2,1,0:T(8,128)S(1)} %get-tuple-element.10, f32[32,128,128]{2,1,0:T(8,128)S(1)} %get-tuple-element.11, f32[128,32,128]{2,0,1:T(8,128)S(1)} %get-tuple-element.94, f32[128,32,128]{2,0,1:T(8,128)S(1)} %fusion.76, f32[32,1,128]{2,1,0:T(1,128)S(1)} %get-tuple-element.45, ...), kind=kLoop, calls=%fused_computation.75 | loop fusion | flops 22020096 | bytes 10551808 | tf_op jit(solution)/shard_map/vmap()/sub | solution.py:82
  86.3 0.7 fusion.133
  87.0 5.7 %fusion.42 = f32[32,128,128]{2,1,0:T(8,128)S(1)} fusion(f32[32,128,128]{2,1,0:T(8,128)S(1)} %fusion.33, f32[32,128,128]{2,1,0:T(8,128)S(1)} %get-tuple-element.11, f32[128,32,128]{2,0,1:T(8,128)S(1)} %get-tuple-element.94, f32[128,32,128]{2,0,1:T(8,128)S(1)} %fusion.76, f32[32,1,128]{2,1,0:T(1,128)S(1)} %get-tuple-element.43, ...), kind=kLoop, calls=%fused_computation.84 | loop fusion | flops 22020096 | bytes 10551808 | tf_op jit(solution)/shard_map/vmap()/sub | solution.py:82
  92.9 0.7 fusion.132
  93.6 9.1 %select_multiply_fusion.1 = (f32[32,128,128]{2,1,0:T(8,128)S(1)}, f32[32,128,128]{2,1,0:T(8,128)S(1)}) fusion(pred[32,128,128]{2,1,0:T(8,128)(4,1)} %get-tuple-element.24, pred[32,128,128]{2,1,0:T(8,128)(4,1)S(1)} %get-tuple-element.23, pred[32,128,128]{2,1,0:T(8,128)(4,1)S(1)} %get-tuple-element.22, pred[32,128,128]{2,1,0:T(8,128)(4,1)S(1)} %get-tuple-element.21, ...), kind=kLoop, calls=%fused_computation.101 | loop fusion | flops 30408704 | bytes 19464704 | tf_op jit(solution)/shard_map/vmap()/mul | solution.py:84
  102.7 1.3 copy-done.2
  104.0 5.8 %select_multiply_fusion = f32[32,128,128]{2,1,0:T(8,128)} fusion(pred[32,128,128]{2,1,0:T(8,128)(4,1)} %get-tuple-element.24, pred[32,128,128]{2,1,0:T(8,128)(4,1)S(1)} %get-tuple-element.23, pred[32,128,128]{2,1,0:T(8,128)(4,1)S(1)} %get-tuple-element.22, pred[32,128,128]{2,1,0:T(8,128)(4,1)S(1)} %get-tuple-element.21, ...), kind=kLoop, calls=%fused_computation.98 | loop fusion | flops 8388608 | bytes 11010048 | tf_op jit(solution)/shard_map/vmap()/mul | solution.py:86
  109.8 6.4 %copy.134 = f32[32,128,128]{0,2,1:T(8,128)} copy(f32[32,128,128]{2,1,0:T(8,128)} %select_multiply_fusion) | data formatting | bytes 4194304 | tf_op jit(solution)/shard_map/vmap()/mul | solution.py:86
  116.2 4.4 %reduce_sum.29 = f32[32,8,8]{0,2,1:T(8,128)S(1)} reduce(f32[32,8,16,8,16]{0,4,3,2,1:T(8,128)} %bitcast.197, f32[]{:T(128)} %constant.63.clone.1), dimensions={2,4}, to_apply=%region_2.3 | reduce | flops 522240 | bytes 2105348 | tf_op jit(solution)/shard_map/vmap()/reduce_sum | solution.py:86
  120.7 4.7 %copy.133 = f32[32,128,128]{0,2,1:T(8,128)} copy(f32[32,128,128]{2,1,0:T(8,128)S(1)} %get-tuple-element.8) | data formatting | bytes 4194304 | tf_op jit(solution)/shard_map/vmap()/mul | solution.py:84
  125.4 4.4 %reduce_sum.28 = f32[32,8,8]{0,2,1:T(8,128)S(1)} reduce(f32[32,8,16,8,16]{0,4,3,2,1:T(8,128)} %bitcast.196, f32[]{:T(128)} %constant.63.clone.1), dimensions={2,4}, to_apply=%region_1.2 | reduce | flops 522240 | bytes 2105348 | tf_op jit(solution)/shard_map/vmap()/reduce_sum | solution.py:84
  130.0 0.9 fusion.83
  130.9 4.6 %all-to-all-start.1 = ((f32[64,1,128]{2,1,0:T(1,128)}), f32[64,1,128]{2,1,0:T(1,128)S(1)}, u32[]{:S(2)}, u32[]{:S(2)}) async-start(f32[64,1,128]{2,1,0:T(1,128)} %bitcast.21), calls=%async_computation.1 | async-start | bytes 65536 | tf_op jit(solution)/shard_map/all_to_all | solution.py:167
  135.5 9.5 %all-to-all-done.1 = f32[64,1,128]{2,1,0:T(1,128)S(1)} async-done(((f32[64,1,128]{2,1,0:T(1,128)}), f32[64,1,128]{2,1,0:T(1,128)S(1)}, u32[]{:S(2)}, u32[]{:S(2)}) %all-to-all-start.1) | async-done | bytes 32800 | tf_op jit(solution)/shard_map/all_to_all | solution.py:167
  145.6 2.5 %collective-permute-start.5 = (f32[1,128]{1,0:T(1,128)S(1)}, f32[1,128]{1,0:T(1,128)S(1)}, u32[]{:S(2)}, u32[]{:S(2)}) collective-permute-start(f32[1,128]{1,0:T(1,128)S(1)} %get-tuple-element.90), channel_id=1, source_target_pairs={{0,8},{8,16},{16,24},{24,32},{32,40},{40,48},{48,56},{56,64},{64,7... | collective-permute-start | bytes 1544 | tf_op jit(solution)/shard_map/ppermute | solution.py:35
  148.2 5.4 %collective-permute-start.4 = (f32[1,128]{1,0:T(1,128)S(1)}, f32[1,128]{1,0:T(1,128)S(1)}, u32[]{:S(2)}, u32[]{:S(2)}) collective-permute-start(f32[1,128]{1,0:T(1,128)S(1)} %get-tuple-element.91), channel_id=1, source_target_pairs={{8,0},{16,8},{24,16},{32,24},{40,32},{48,40},{56,48},{64,56},{72,6... | collective-permute-start | bytes 1544 | tf_op jit(solution)/shard_map/ppermute | solution.py:37
  153.6 3.3 %slice_bitcast_fusion.2 = (f32[80,18,130]{0,2,1:T(8,128)S(1)}, f32[80,18,130]{0,2,1:T(8,128)}, f32[80,18,130]{0,2,1:T(8,128)S(1)}) fusion(f32[3,80,18,130]{1,3,2,0:T(8,128)} %copy-done.1), kind=kLoop, calls=%fused_computation.104 | loop fusion | bytes 4492800 | tf_op jit(solution)/shard_map/squeeze | solution.py:108
  157.3 1.3 collective-permute-start.7
  158.6 1.3 collective-permute-start.6
  159.9 2.6 %collective-permute-done.6 = f32[18,1]{1,0:T(8,128)S(1)} collective-permute-done((f32[18,1]{1,0:T(8,128)S(1)}, f32[18,1]{1,0:T(8,128)S(1)}, u32[]{:S(2)}, u32[]{:S(2)}) %collective-permute-start.6) | collective-permute-done | bytes 104 | tf_op jit(solution)/shard_map/ppermute | solution.py:37
  163.0 0.8 copy-done
  163.8 1.9 %fusion.72 = (f32[1,80,16,128]{1,3,2,0:T(8,128)S(1)}, f32[1,80,16,128]{1,3,2,0:T(8,128)S(1)}) fusion(f32[80,18,130]{0,2,1:T(8,128)S(1)} %get-tuple-element.25, f32[16,128]{1,0:T(8,128)S(1)} %get-tuple-element.88, f32[80]{0:T(128)S(1)} %exponential_multiply_fusion, f32[16,128]{1,0:T(8,128)S(1)} %mul.290, f32[80,18,130]{0,2,1:T(8,128)S(1)} %copy-done, ...), kind=kLoop, calls=%fused_computation.135 | loop fusion | flops 4587520 | bytes 8536384 | tf_op jit(solution)/shard_map/stack | solution.py:123
  166.1 2.1 %copy.141 = f32[3,80,16,128]{3,2,1,0:T(8,128)} copy(f32[3,80,16,128]{1,3,2,0:T(8,128)S(1)} %pad_maximum_fusion.1) | data formatting | bytes 3932160
  (132 shorter events, 7.9 us)
Async XLA Ops:
  0.6 12.6 %copy-start.4 = (s32[1,64,32]{1,2,0:T(8,128)S(1)}, s32[1,64,32]{1,2,0:T(8,128)}, u32[]{:S(2)}) copy-start(s32[1,64,32]{1,2,0:T(8,128)} %param.7) | copy-start | bytes 24580
  3.6 18.3 %collective-permute-start.1 = (f32[3,80,1,128]{1,3,2,0:T(8,128)}, f32[3,80,1,128]{1,3,2,0:T(8,128)S(1)}, u32[]{:S(2)}, u32[]{:S(2)}) collective-permute-start(f32[3,80,1,128]{1,3,2,0:T(8,128)} %get-tuple-element.31), channel_id=1, source_target_pairs={{8,0},{16,8},{24,16},{32,24},{40,32},{48,40},{56,48},{64,56},{72,6... | collective-permute-start | bytes 368648 | tf_op jit(solution)/shard_map/ppermute | solution.py:37
  11.3 10.6 %collective-permute-start = (f32[3,80,1,128]{1,3,2,0:T(8,128)}, f32[3,80,1,128]{1,3,2,0:T(8,128)S(1)}, u32[]{:S(2)}, u32[]{:S(2)}) collective-permute-start(f32[3,80,1,128]{1,3,2,0:T(8,128)} %get-tuple-element.30), channel_id=1, source_target_pairs={{0,8},{8,16},{16,24},{24,32},{32,40},{40,48},{48,56},{56,64},{64,7... | collective-permute-start | bytes 368648 | tf_op jit(solution)/shard_map/ppermute | solution.py:35
  16.2 0.6 copy-start.5
  16.2 0.6 copy-start.7
  21.3 5.0 %copy-start.9 = (s32[64,32]{0,1:T(8,128)S(1)}, s32[64,32]{0,1:T(8,128)}, u32[]{:S(2)}) copy-start(s32[64,32]{0,1:T(8,128)} %add_select_fusion) | copy-start | bytes 24580
  21.4 5.0 %copy-start.10 = (pred[64,32]{0,1:T(8,128)(4,1)S(1)}, pred[64,32]{0,1:T(8,128)(4,1)}, u32[]{:S(2)}) copy-start(pred[64,32]{0,1:T(8,128)(4,1)} %fusion.93) | copy-start | bytes 6148
  22.0 4.5 %collective-permute-start.3 = (f32[3,80,18,1]{1,3,2,0:T(1,128)S(1)}, f32[3,80,18,1]{1,3,2,0:T(1,128)S(1)}, u32[]{:S(2)}, u32[]{:S(2)}) collective-permute-start(f32[3,80,18,1]{1,3,2,0:T(1,128)S(1)} %get-tuple-element.29), channel_id=1, source_target_pairs={{1,0},{2,1},{3,2},{4,3},{5,4},{6,5},{7,6},{9,8},{10,9},{11,10},{12... | collective-permute-start | bytes 51848 | tf_op jit(solution)/shard_map/ppermute | solution.py:37
  23.3 3.9 %collective-permute-start.2 = (f32[3,80,18,1]{1,3,2,0:T(1,128)S(1)}, f32[3,80,18,1]{1,3,2,0:T(1,128)S(1)}, u32[]{:S(2)}, u32[]{:S(2)}) collective-permute-start(f32[3,80,18,1]{1,3,2,0:T(1,128)S(1)} %get-tuple-element.28), channel_id=1, source_target_pairs={{0,1},{1,2},{2,3},{3,4},{4,5},{5,6},{6,7},{8,9},{9,10},{10,11},{11... | collective-permute-start | bytes 51848 | tf_op jit(solution)/shard_map/ppermute | solution.py:35
  27.7 1.8 %copy-start.1 = (f32[3,80,18,130]{1,3,2,0:T(8,128)}, f32[3,80,18,130]{1,3,2,0:T(8,128)S(1)}, u32[]{:S(2)}) copy-start(f32[3,80,18,130]{1,3,2,0:T(8,128)S(1)} %pad_maximum_fusion) | copy-start | bytes 6739204
  31.0 26.0 %copy-start.11 = (pred[32]{0:T(512)(128)(4,1)S(1)}, pred[32]{0:T(512)(128)(4,1)}, u32[]{:S(2)}) copy-start(pred[32]{0:T(512)(128)(4,1)} %get-tuple-element.93) | copy-start | bytes 100
  31.0 26.0 %copy-start.12 = (s32[32]{0:T(128)S(1)}, s32[32]{0:T(128)}, u32[]{:S(2)}) copy-start(s32[32]{0:T(128)} %and_select_fusion) | copy-start | bytes 388
  35.2 26.6 %copy-start.3 = (f32[32,130,1]{2,1,0:T(8,128)S(1)}, f32[32,130,1]{2,1,0:T(8,128)}, u32[]{:S(2)}) copy-start(f32[32,130,1]{2,1,0:T(8,128)} %get-tuple-element.38) | copy-start | bytes 49924
  35.2 26.6 %copy-start.6 = (f32[32,1,128]{2,1,0:T(1,128)S(1)}, f32[32,1,128]{2,1,0:T(1,128)}, u32[]{:S(2)}) copy-start(f32[32,1,128]{2,1,0:T(1,128)} %copy-done.5) | copy-start | bytes 49156
  35.2 26.6 %copy-start.8 = (f32[32,1,128]{2,1,0:T(1,128)S(1)}, f32[32,1,128]{2,1,0:T(1,128)}, u32[]{:S(2)}) copy-start(f32[32,1,128]{2,1,0:T(1,128)} %copy-done.7) | copy-start | bytes 49156
  35.9 21.0 %all-to-all-start = ((f32[64,1,200]{2,1,0:T(1,128)}), f32[64,1,200]{2,1,0:T(1,128)S(1)}, u32[]{:S(2)}, u32[]{:S(2)}) async-start(f32[64,1,200]{2,1,0:T(1,128)} %copy.127), calls=%async_computation | async-start | bytes 131072 | tf_op jit(solution)/shard_map/all_to_all | solution.py:156
  102.7 1.3 copy-start.2
  125.4 4.5 %copy-start.13 = (f32[32]{0:T(128)S(1)}, f32[32]{0:T(128)}, u32[]{:S(2)}) copy-start(f32[32]{0:T(128)} %get-tuple-element.92) | copy-start | bytes 388
  130.9 14.1 %all-to-all-start.1 = ((f32[64,1,128]{2,1,0:T(1,128)}), f32[64,1,128]{2,1,0:T(1,128)S(1)}, u32[]{:S(2)}, u32[]{:S(2)}) async-start(f32[64,1,128]{2,1,0:T(1,128)} %bitcast.21), calls=%async_computation.1 | async-start | bytes 65536 | tf_op jit(solution)/shard_map/all_to_all | solution.py:167
  145.6 11.5 %collective-permute-start.5 = (f32[1,128]{1,0:T(1,128)S(1)}, f32[1,128]{1,0:T(1,128)S(1)}, u32[]{:S(2)}, u32[]{:S(2)}) collective-permute-start(f32[1,128]{1,0:T(1,128)S(1)} %get-tuple-element.90), channel_id=1, source_target_pairs={{0,8},{8,16},{16,24},{24,32},{32,40},{40,48},{48,56},{56,64},{64,7... | collective-permute-start | bytes 1544 | tf_op jit(solution)/shard_map/ppermute | solution.py:35
  148.2 9.0 %collective-permute-start.4 = (f32[1,128]{1,0:T(1,128)S(1)}, f32[1,128]{1,0:T(1,128)S(1)}, u32[]{:S(2)}, u32[]{:S(2)}) collective-permute-start(f32[1,128]{1,0:T(1,128)S(1)} %get-tuple-element.91), channel_id=1, source_target_pairs={{8,0},{16,8},{24,16},{32,24},{40,32},{48,40},{56,48},{64,56},{72,6... | collective-permute-start | bytes 1544 | tf_op jit(solution)/shard_map/ppermute | solution.py:37
  157.3 2.6 %collective-permute-start.7 = (f32[18,1]{1,0:T(8,128)S(1)}, f32[18,1]{1,0:T(8,128)S(1)}, u32[]{:S(2)}, u32[]{:S(2)}) collective-permute-start(f32[18,1]{1,0:T(8,128)S(1)} %get-tuple-element.87), channel_id=1, source_target_pairs={{0,1},{1,2},{2,3},{3,4},{4,5},{5,6},{6,7},{8,9},{9,10},{10,11},{11... | collective-permute-start | bytes 224 | tf_op jit(solution)/shard_map/ppermute | solution.py:35
  158.6 3.9 %collective-permute-start.6 = (f32[18,1]{1,0:T(8,128)S(1)}, f32[18,1]{1,0:T(8,128)S(1)}, u32[]{:S(2)}, u32[]{:S(2)}) collective-permute-start(f32[18,1]{1,0:T(8,128)S(1)} %get-tuple-element.86), channel_id=1, source_target_pairs={{1,0},{2,1},{3,2},{4,3},{5,4},{6,5},{7,6},{9,8},{10,9},{11,10},{12... | collective-permute-start | bytes 224 | tf_op jit(solution)/shard_map/ppermute | solution.py:37
  162.5 1.3 copy-start
where the time goes:
time: 172 us; the launch traced here: 168 us
  other arithmetic  43 us (25%)
  starting transfers between devices  40.2 us (23%)
  local copies, waits for them, and re-layouts  36.8 us (21%)
  matrix products  24 us (14%)
  waiting for transfers between devices  22.6 us (13%)
    dot_general x1, matrix products, fire_advance(): jnp.dot(jnp.dot(table, window[1], precision=highest), table.T, precision=...  17.8 us
    ppermute x4, starting transfers between devices, with_halo(): lax.ppermute(head, axis, [((i + 1) % count, i) for i in range(ends)])  15.7 us
    all_to_all x1, starting transfers between devices, on_device(): lax.all_to_all(outgoing, ('gx', 'gy'), split_axis=0, concat_axis=0, tiled...  11.2 us
    sub x2, other arithmetic, fire_advance(): phase = phase - fire_time * rate * jnp.sqrt(upwind)  11.1 us
    all_to_all x1, waiting for transfers between devices, on_device(): lax.all_to_all(outgoing, ('gx', 'gy'), split_axis=0, concat_axis=0, tiled...  9.83 us
    all_to_all x1, waiting for transfers between devices, on_device(): lax.all_to_all(returning, ('gx', 'gy'), split_axis=0, concat_axis=0, tile...  9.5 us
    mul x1, other arithmetic, fire_advance(): lookup(category, heat_yields) * burning  9.08 us
    unnamed x30, local copies, waits for them, and re-layouts  8.88 us
  transfers between devices with their start and end apart: 10, of which 4 were waited for; matrix products, arithmetic and copies ran while one was open for 7% of the time, Pallas kernels for 0%

commit v1 on v0

v1 whole, which is shorter than its diff:
```python
import jax
import jax.numpy as jnp
import numpy as np
from jax import lax
from jax.experimental import pallas as pl
from jax.experimental.pallas import tpu as pltpu
from jax.sharding import PartitionSpec as P

SUB = 4
LEV = 80
N_GRP, N_GX, N_GY = 4, 8, 8

spread_rates = np.array(
    [0.3, 0.5, 0.9, 1.2, 0.6, 0.4, 0.7, 0.35, 0.25, 0.45, 0.55, 0.8, 1.0], np.float32
)
heat_yields = np.array(
    [1.0, 2.5, 4.0, 3.0, 1.5, 2.0, 5.0, 1.2, 0.8, 3.5, 2.2, 4.5, 2.8], np.float32
)
smoke_yields = np.array(
    [0.5, 1.5, 2.5, 1.0, 3.0, 0.8, 2.0, 1.8, 0.6, 2.6, 1.1, 3.4, 1.4], np.float32
)
courant = 0.1
viscosity = 0.1
buoyancy = 0.5
source_step = 0.5
fire_time = 0.1
wind_gain = 0.3

F32 = jnp.float32
BF16 = jnp.bfloat16
VMEM = pl.BlockSpec(memory_space=pltpu.VMEM)
SMEM = pl.BlockSpec(memory_space=pltpu.SMEM)
ANY = pl.BlockSpec(memory_space=pl.ANY)


def room(mib):
    return pltpu.CompilerParams(vmem_limit_bytes=mib * 1024 * 1024)


def shape(*dims, dtype=F32):
    return jax.ShapeDtypeStruct(dims, dtype)


def cost(flops, moved):
    return pl.CostEstimate(flops=flops, bytes_accessed=moved, transcendentals=0)


def lanes_of(rows=8):
    return lax.broadcasted_iota(jnp.int32, (rows, 128), 1)


def sublanes_of(rows=8):
    return lax.broadcasted_iota(jnp.int32, (rows, 128), 0)


def halves(value):
    high = value.astype(BF16).astype(F32)
    return high, value - high


def spread_line(line, row, low, high, rims):
    lane, sub = lanes_of(), sublanes_of()
    line = jnp.broadcast_to(line, (8, 128))
    here = (lane >= 12 * row) & (lane < 12 * row + 10)
    fanned = pltpu.roll(line, 0, 1, stride=8, stride_axis=0)
    first = pltpu.roll(fanned, (12 * row + 73) % 128, 1)
    second = pltpu.roll(fanned, (12 * row + 9) % 128, 1)
    low = jnp.where(here & ((sub < 7) | (lane > 12 * row)), first, low)
    high = jnp.where(here & ((sub > 0) | (lane < 12 * row + 9)), second, high)
    edges = pltpu.roll(line, (12 * row + 11) % 128, 1)
    rims = jnp.where((lane == 12 * row + 10 + sub) & (sub < 2), edges, rims)
    return low, high, rims


def table_kernel(surf_ref, tile_ref):
    none = jnp.zeros((8, 128), F32)
    for comp in range(2):
        lanes = slice(128 * comp, 128 * comp + 128)
        field = surf_ref[comp] * wind_gain
        for half in range(2):
            low = high = rims = none
            for row in range(10):
                at = 8 * half + row - 1
                if 0 <= at < 16:
                    low, high, rims = spread_line(field[at : at + 1], row, low, high, rims)
            tile_ref[16 * half : 16 * half + 8, lanes] = low
            tile_ref[16 * half + 8 : 16 * half + 16, lanes] = high
            tile_ref[40 + 8 * half : 48 + 8 * half, lanes] = rims
        tile_ref[32:40, lanes] = none


def windows_kernel(
    pick_ref, table_ref, above_ref, below_ref, left_ref, out_ref, token_ref, tile_ref
):
    token_ref[...] = jnp.zeros((8, 128), F32) + left_ref[0:1, 0:128] * 0.0
    tile_ref[...] = table_ref[...]
    for comp in range(2):
        lanes = slice(128 * comp, 128 * comp + 128)
        line_at = slice(LEV * comp, LEV * comp + 1)
        for half, (ref, row) in enumerate(((above_ref, 0), (below_ref, 9))):
            places = (
                slice(16 * half, 16 * half + 8),
                slice(16 * half + 8, 16 * half + 16),
                slice(40 + 8 * half, 48 + 8 * half),
            )
            old = [tile_ref[rows, lanes] for rows in places]
            fresh = spread_line(ref[line_at, :] * wind_gain, row, *old)
            for rows, value in zip(places, fresh):
                tile_ref[rows, lanes] = value

    def one(at, carry):
        for spot in range(16):
            fire = 16 * at + spot
            picks = pick_ref[fire]
            own = tile_ref[pl.ds(picks & 63, 1), :]
            rim_right = tile_ref[pl.ds((picks >> 6) & 63, 1), :]
            rim_left = tile_ref[pl.ds(picks >> 12, 1), :]
            out_ref[fire] = own + (rim_right + rim_left)
        return carry

    lax.fori_loop(0, 4, one, 0)


def fire_kernel(
    slots_ref, phase_in, fuel_in, recv_ref, words_ref, wcol_ref, spread_ref,
    left_in, right_in, token_in, out_ref, msg_ref, left_out, right_out,
    phase_ref, fuel_ref, done_ref, column_ref, sums_ref, means_ref, bag_ref, *rest,
):
    buffers, sem, sem_in = rest[:-2], rest[-2], rest[-1]
    sides = [buffers[at::2] for at in range(2)]
    left_out[...] = left_in[...]
    right_out[...] = right_in[...]
    loads = []
    for at, (low, high) in enumerate(((0, 2), (2, 8), (8, 32))):
        some = pl.ds(low, high - low)
        loads.append(
            (
                pltpu.make_async_copy(phase_in.at[some], phase_ref.at[some], sem_in.at[at]),
                pltpu.make_async_copy(fuel_in.at[some], fuel_ref.at[some], sem_in.at[3 + at]),
            )
        )
        for load in loads[-1]:
            load.start()
    lane24 = lanes_of(24)
    knot = sublanes_of(24)
    knot = (knot & 7) + (knot >> 3)
    unfold = (lane24 >= 12 * knot) & (lane24 < 12 * knot + 12)
    place = lax.broadcasted_iota(jnp.int32, (1, 128), 1) % 12
    words = words_ref[...]
    row8, lane8 = sublanes_of(), lanes_of()

    def place_of(slot):
        tile = slots_ref[slot]
        return jnp.maximum(tile, 0) >> 5, jnp.maximum(tile, 0) & 15, tile >= 0

    def columns(at, carry):
        parts = []
        for spot in range(4):
            owner, col, live = place_of(4 * at + spot)
            gy = owner & (N_GY - 1)
            left = jnp.maximum(owner - 1, 0)
            right = jnp.minimum(owner + 1, N_GX * N_GY - 1)
            left_rim = (place == 10) & ((col == 0) & (gy > 0))
            right_rim = (place == 11) & ((col == 15) & (gy < N_GY - 1))
            for comp in range(2):
                lanes = slice(128 * comp, 128 * comp + 128)
                line = jnp.where(place < 10, recv_ref[owner, :, lanes], 0.0)
                line = jnp.where(left_rim, recv_ref[left, :, lanes], line)
                line = jnp.where(right_rim, recv_ref[right, :, lanes], line)
                line = jnp.where(live, line, 0.0)
                parts.append(jnp.where(unfold, jnp.broadcast_to(line, (24, 128)), 0.0))
        high, low = halves(jnp.concatenate(parts, axis=0))
        both = jnp.dot(high.astype(BF16), wcol_ref[...], preferred_element_type=F32) + jnp.dot(
            low.astype(BF16), wcol_ref[...], preferred_element_type=F32
        )
        for spot in range(4):
            column_ref[4 * at + spot] = both[48 * spot : 48 * spot + 48]
        return carry

    def result(slot):
        return pltpu.make_async_copy(done_ref.at[slot], out_ref.at[slot], sem.at[slot])

    def block(at):
        return slice(8 * at, 8 * at + 8)

    def store(target, at, values):
        field, behind, beyond = target
        turned = [pltpu.roll(value, 1, 1) for value in values]
        for k, value in enumerate(values):
            field[block(at + k), :] = value
        backs = [jnp.where(lane8 == 0, 0.0, x - y) for x, y in zip(values, turned)]
        aheads = [pltpu.roll(back, 127, 1) for back in backs]
        for k, (back, ahead) in enumerate(zip(backs, aheads)):
            behind[block(at + k), :] = back
            beyond[block(at + k), :] = ahead

    def begin(slot, side):
        gust, rate, word = side[:3]
        runs = [column_ref[slot, 8 * at : 8 * at + 8, :] for at in range(6)]
        steps = [runs[at + 1] - runs[at] for at in (0, 1, 3, 4)]
        for first in range(0, 16, 8):
            blocks = range(first, first + 8)
            places = [pl.ds(j, 8, stride=16) for j in blocks]
            fuels = [fuel_ref[slot, there, :] for there in places]
            packed = [
                jnp.take_along_axis(words, fuel, axis=1, mode="promise_in_bounds")
                for fuel in fuels
            ]
            store(side[3:6], first, [phase_ref[slot, there, :] for there in places])
            bases = [(x & 31).astype(F32) * np.float32(0.05 * fire_time) for x in packed]
            for j, x, base in zip(blocks, packed, bases):
                rate[block(j), :] = base
                word[block(j), :] = x
            low = first // 8
            for comp in range(2):
                run, step = runs[3 * comp + low], steps[2 * comp + low]
                parts = [np.float32((j + 0.5) / 16 + 0.5 - low) for j in blocks]
                winds = [run + part * step for part in parts]
                for j, wind, base in zip(blocks, winds, bases):
                    gust[block(16 * comp + j), :] = wind * base

    def advance(side, source, keep):
        gust, rate = side[:2]
        field, behind, beyond = source
        edge = field[block(0), :] - pltpu.roll(field[block(15), :], 1, 0)
        edge = jnp.where(row8 == 0, 0.0, edge)
        last = pltpu.roll(edge, 7, 0)
        for first in range(0, 16, 8):
            blocks = range(first, first + 8)
            fields = [field[block(j), :] for j in range(first, min(first + 9, 16))]
            aheads = [y - x for x, y in zip(fields, fields[1:])]
            if first == 8:
                aheads.append(last)
            backs = [edge] + aheads[:-1]
            edge = aheads[-1]
            side_backs = [behind[block(j), :] for j in blocks]
            side_aheads = [beyond[block(j), :] for j in blocks]
            a = [jnp.maximum(x, 0.0) for x in backs]
            b = [jnp.minimum(x, 0.0) for x in aheads]
            upwinds = [x * x + y * y for x, y in zip(a, b)]
            c = [jnp.maximum(x, 0.0) for x in side_backs]
            d = [jnp.minimum(x, 0.0) for x in side_aheads]
            upwinds = [u + (x * x + y * y) for u, x, y in zip(upwinds, c, d)]
            inverses = [lax.rsqrt(jnp.maximum(u, 1e-36)) for u in upwinds]
            row_slopes = [x + y for x, y in zip(backs, aheads)]
            col_slopes = [x + y for x, y in zip(side_backs, side_aheads)]
            squares = [x * x + y * y for x, y in zip(row_slopes, col_slopes)]
            factors = [lax.rsqrt(jnp.maximum(x, 4.0)) for x in squares]
            along = [
                gust[block(j), :] * x + gust[block(16 + j), :] * y
                for j, x, y in zip(blocks, row_slopes, col_slopes)
            ]
            roots = [u * x for u, x in zip(upwinds, inverses)]
            speeds = [
                rate[block(j), :] + jnp.maximum(x * f, 0.0)
                for j, x, f in zip(blocks, along, factors)
            ]
            keep(first, [x - v * r for x, v, r in zip(fields, speeds, roots)])

    def finish(slot, side):
        word = side[2]
        sums = [[], []]

        def keep(first, values):
            for k, value in enumerate(values):
                done_ref[slot, pl.ds(first + k, 8, stride=16), :] = value
            burning = [jnp.exp(value) for value in values]
            burning = [1.0 / (1.0 + value) for value in burning]
            packed = [word[block(first + k), :] for k in range(8)]
            heats = [((x >> 5) & 63).astype(F32) * y for x, y in zip(packed, burning)]
            smokes = [(x >> 11).astype(F32) * y for x, y in zip(packed, burning)]
            for total, terms in zip(sums, (heats, smokes)):
                while len(terms) > 1:
                    terms = [x + y for x, y in zip(terms[::2], terms[1::2])]
                total.append(terms[0])

        advance(side, side[6:9], keep)
        result(slot).start()
        sums_ref[slot, :, 0:128] = sums[0][0] + sums[0][1]
        sums_ref[slot, :, 128:256] = sums[1][0] + sums[1][1]

    def into(target):
        return lambda first, values: store(target, first, values)

    lax.fori_loop(0, 8, columns, 0)

    def pair(at, carry):
        slot = 2 * at
        for start, some in zip((0, 1, 4), loads):

            @pl.when(at == start)
            def _():
                for load in some:
                    load.wait()

        for spot, side in enumerate(sides):
            begin(slot + spot, side)
        for step in range(SUB - 1):
            for side in sides:
                pair_of = (side[3:6], side[6:9])
                advance(side, pair_of[step % 2], into(pair_of[1 - step % 2]))
        for spot, side in enumerate(sides):
            finish(slot + spot, side)
        return carry

    lax.fori_loop(0, 16, pair, 0)
    high, low = halves(sums_ref[...].reshape(256, 256))
    spread = spread_ref[...]
    means_ref[...] = (
        jnp.dot(high.astype(BF16), spread, preferred_element_type=F32)
        + jnp.dot(low.astype(BF16), spread, preferred_element_type=F32)
    ) * np.float32(0.1 / 256)
    dense = means_ref[pl.ds(0, 32, stride=8), :]
    for row in range(1, 8):
        dense = dense + pltpu.roll(means_ref[pl.ds(row, 32, stride=8), :], 16 * row, 1)
    means_ref[0:32, :] = dense
    bag_ref[...] = jnp.zeros(bag_ref.shape, F32)
    spot = lax.broadcasted_iota(jnp.int32, (1, 128), 1) % 16
    own, beside = slice(0, 128), slice(128, 256)

    def send(slot, carry):
        owner, col, live = place_of(slot)
        gy = owner & (N_GY - 1)
        line = means_ref[pl.ds(slot, 1), :]
        bag_ref[jnp.where(live, owner, 64), :, own] = line
        to_left = live & (col == 0) & (gy > 0)
        to_right = live & (col == 15) & (gy < N_GY - 1)
        target = jnp.where(to_left, owner - 1, jnp.where(to_right, owner + 1, 64))
        kept = jnp.where(to_left, 0, 7)
        bag_ref[target, :, beside] = jnp.where(spot == kept, line, bag_ref[target, :, beside])
        return carry

    lax.fori_loop(0, 32, send, 0, unroll=4)
    msg_ref[...] = bag_ref[0:64]

    def settle(slot, carry):
        result(slot).wait()
        return carry

    lax.fori_loop(0, 32, settle, 0)


def place_kernel(where_ref, flux_ref, heat_ref, side_ref, smoke_ref, first_ref, last_ref):
    lane, sub = lanes_of(), sublanes_of()
    key = lane // 8
    heat_from = sub * 16 + lane % 8
    zero = jnp.zeros((8, 128), F32)

    def tile(at, lanes):
        fire = where_ref[at]
        line = flux_ref[jnp.maximum(fire, 0), :, lanes]
        return jnp.where(fire >= 0, jnp.broadcast_to(line, (8, 128)), 0.0)

    def find(value, index):
        return jnp.take_along_axis(value, index, axis=1, mode="promise_in_bounds")

    own, beside = slice(0, 128), slice(128, 256)
    for half in range(2):
        rows = slice(8 * half, 8 * half + 8)
        heat = smoke = zero
        for col in range(16):
            value = tile(16 * half + col, own)
            heat = jnp.where(key == col, find(value, heat_from), heat)
            smoke = jnp.where(key == col, find(value, heat_from + 8), smoke)
        rim_left = find(tile(32 + half, beside), heat_from)
        rim_right = find(tile(34 + half, beside), heat_from)
        left = pltpu.roll(jnp.where(lane == 127, rim_left, heat), 1, 1)
        right = pltpu.roll(jnp.where(lane == 0, rim_right, heat), 127, 1)
        heat_ref[rows, :] = heat
        smoke_ref[rows, :] = smoke
        side_ref[rows, :] = 0.5 * (right - left)
        if half == 0:
            first_ref[...] = heat[0:1]
        else:
            last_ref[...] = heat[7:8]


def rows_kernel(air_ref, first_ref, last_ref, surf_ref, sem):
    copies = (
        pltpu.make_async_copy(air_ref.at[:, 0, :], first_ref, sem.at[0]),
        pltpu.make_async_copy(air_ref.at[:, 15, :], last_ref, sem.at[1]),
        pltpu.make_async_copy(air_ref.at[0], surf_ref.at[0], sem.at[2]),
        pltpu.make_async_copy(air_ref.at[LEV], surf_ref.at[1], sem.at[3]),
    )
    for copy in copies:
        copy.start()
    for copy in copies:
        copy.wait()


def sides_kernel(air_ref, left_ref, right_ref):
    lane, sub = lanes_of(), sublanes_of()
    pick = jnp.where((lane == 127 * sub) & (sub < 2), 1.0, 0.0)
    picked = lax.dot_general(
        pick, air_ref[...].reshape(3 * LEV * 16, 128), (((1,), (1,)), ((), ())),
        precision=lax.Precision.HIGHEST, preferred_element_type=F32,
    )
    left_ref[...] = picked[0:1]
    right_ref[...] = picked[1:2]


def air_kernel(air_ref, above_ref, below_ref, token_in, out_ref, token_ref):
    token_ref[...] = token_in[...]
    lane = lax.broadcasted_iota(jnp.int32, (8, 16, 128), 2)
    row = lax.broadcasted_iota(jnp.int32, (8, 16, 128), 1)

    def chunk(at, carry):
        fields = []
        for part in range(3):
            start = part * LEV + at * 8
            mid = air_ref[pl.ds(start, 8)]
            above = above_ref[pl.ds(start, 8), :][:, None, :]
            below = below_ref[pl.ds(start, 8), :][:, None, :]
            up = jnp.where(row == 0, above, pltpu.roll(mid, 1, 1))
            down = jnp.where(row == 15, below, pltpu.roll(mid, 15, 1))
            left = jnp.where(lane == 0, 0.0, pltpu.roll(mid, 1, 2))
            right = jnp.where(lane == 127, 0.0, pltpu.roll(mid, 127, 2))
            fields.append((mid, up, down, left, right))
        for part in range(2):
            mid, up, down, left, right = fields[part]
            around = (up + down) + (left + right)
            out_ref[pl.ds(part * LEV + at * 8, 8)] = mid + viscosity * (around - 4.0 * mid)
        u, v = fields[0][0], fields[1][0]
        mid, up, down, left, right = fields[2]
        upwind = (
            jnp.maximum(u, 0.0) * (mid - up)
            + jnp.minimum(u, 0.0) * (down - mid)
            + jnp.maximum(v, 0.0) * (mid - left)
            + jnp.minimum(v, 0.0) * (right - mid)
        )
        out_ref[pl.ds(2 * LEV + at * 8, 8)] = mid - courant * upwind
        return carry

    lax.fori_loop(0, LEV // 8, chunk, 0)


def rims_kernel(part_ref, left_ref, right_ref, own_left_ref, own_right_ref, out_ref):
    sub, lane = sublanes_of(), lanes_of()
    expand = jnp.where((sub < 2) & (lane == 0), 1.0, 0.0) + jnp.where(
        (sub >= 2) & (sub < 4) & (lane == 127), 1.0, 0.0
    )
    expand = expand.astype(BF16)

    def chunk(at, carry):
        for part in range(3):
            spot = pl.ds(pl.multiple_of(part * (LEV * 16) + at * 128, 128), 128)
            left, right = left_ref[:, spot], right_ref[:, spot]
            if part < 2:
                left, right = viscosity * left, viscosity * right
            else:
                wind = pl.ds(pl.multiple_of(LEV * 16 + at * 128, 128), 128)
                left = courant * jnp.maximum(own_left_ref[:, wind], 0.0) * left
                right = -courant * jnp.minimum(own_right_ref[:, wind], 0.0) * right
            left_high, left_low = halves(left)
            right_high, right_low = halves(right)
            rims = jnp.where(sub == 0, left_high, 0.0)
            rims = jnp.where(sub == 1, left_low, rims)
            rims = jnp.where(sub == 2, right_high, rims)
            rims = jnp.where(sub == 3, right_low, rims)
            rim = lax.dot_general(
                rims.astype(BF16), expand, (((0,), (0,)), ((), ())), preferred_element_type=F32
            ).reshape(8, 16, 128)
            levels = pl.ds(part * LEV + at * 8, 8)
            out_ref[levels] = part_ref[levels] + rim
        return carry

    lax.fori_loop(0, LEV // 8, chunk, 0, unroll=2)


def final_kernel(part_ref, heat_ref, side_ref, smoke_ref, above_ref, below_ref, prof_ref, out_ref):
    heat = heat_ref[...]
    row = sublanes_of(16)
    up = jnp.where(row == 0, above_ref[...], pltpu.roll(heat, 1, 0))
    down = jnp.where(row == 15, below_ref[...], pltpu.roll(heat, 15, 0))
    sources = (0.5 * (down - up), side_ref[...], smoke_ref[...])

    def one(at, carry):
        for spot in range(4):
            level = 4 * at + spot
            weight = prof_ref[pl.ds(level, 1), :]
            for part in range(3):
                before = part_ref[part * LEV + level]
                out_ref[part * LEV + level] = before + weight * sources[part]
        return carry

    lax.fori_loop(0, LEV // 4, one, 0)


def constants():
    spots = (np.arange(128) + 0.5) / 16 + 0.5
    weights = np.maximum(0.0, 1.0 - np.abs(spots[:, None] - np.arange(10)[None, :]))
    wcol = np.zeros((128, 128), np.float32)
    for row in range(10):
        wcol[12 * row : 12 * row + 10, :] = weights.T
        wcol[12 * row + 10, :] = weights[:, 0]
        wcol[12 * row + 11, :] = weights[:, 9]
    spread = np.zeros((256, 128), np.float32)
    for c in range(128):
        spread[c, c // 16] = 1.0
        spread[128 + c, 8 + c // 16] = 1.0
    words = np.zeros((8, 128), np.int32)
    tables = (spread_rates * 20, heat_yields * 10, smoke_yields * 10)
    rates, heats, smokes = (np.rint(table).astype(np.int32) for table in tables)
    words[:, :13] = rates + 32 * heats + 2048 * smokes
    levels = np.arange(LEV, dtype=np.float32)
    profile = np.exp(-levels * np.float32(8.0) / np.float32(LEV))
    profile = np.broadcast_to((np.float32(0.5) * profile)[:, None], (LEV, 128))
    return wcol, spread, words, np.ascontiguousarray(profile)


def neighbours(last, first, axes, count):
    ends = count - 1
    before = lax.ppermute(last, axes, [(i, i + 1) for i in range(ends)])
    after = lax.ppermute(first, axes, [(i + 1, i) for i in range(ends)])
    return before, after


def on_device(air, level_set, fuel, tile_list):
    wcol, spread, words, profile = constants()
    rows = ("grp", "gx")
    my_gx, my_gy = lax.axis_index("gx"), lax.axis_index("gy")
    myself = my_gx * N_GY + my_gy
    levels = air.reshape(3 * LEV, 16, 128)

    first, last, surface = pl.pallas_call(
        rows_kernel,
        out_shape=(shape(3 * LEV, 128), shape(3 * LEV, 128), shape(2, 16, 128)),
        in_specs=[ANY], out_specs=(VMEM,) * 3, scratch_shapes=[pltpu.SemaphoreType.DMA((4,))],
        compiler_params=room(60), name="rows", cost_estimate=cost(10**5, 10**6),
    )(levels)
    air_above, air_below = neighbours(last, first, rows, N_GRP * N_GX)

    listed = tile_list[0]
    slots = lax.dynamic_index_in_dim(listed, myself, 0, keepdims=False)
    right_at = jnp.where(my_gy < N_GY - 1, (myself + 1) * 32, -64)
    left_at = jnp.where(my_gy > 0, (myself - 1) * 32 + 15, -64)
    own_tile = jnp.where(listed // 32 == myself, ((listed % 32) ^ 7) - 32, 0)
    own_tile = jnp.where(listed >= 0, own_tile, 0)
    own_row = jnp.min(own_tile, axis=1) + 32
    rim_right = jnp.where(listed == right_at, 8, jnp.where(listed == right_at + 16, 16, 0))
    rim_left = jnp.where(listed == left_at, 9, jnp.where(listed == left_at + 16, 17, 0))
    picks = own_row + jnp.max(rim_right, axis=1) * 64 + jnp.max(rim_left, axis=1) * 4096
    picks = picks + 32 * 64 + 32 * 4096
    beside = jnp.array([15, 31], jnp.int32)
    wanted = jnp.concatenate(
        [
            myself * 32 + jnp.arange(32, dtype=jnp.int32),
            jnp.where(my_gy > 0, (myself - 1) * 32 + beside, -2),
            jnp.where(my_gy < N_GY - 1, (myself + 1) * 32 + beside - 15, -2),
        ]
    )
    found = listed[None, :, :] == wanted[:, None, None]
    order = lax.broadcasted_iota(jnp.int32, found.shape, 1)
    where = jnp.max(jnp.where(found, order, -1), axis=(1, 2))

    left, right = pl.pallas_call(
        sides_kernel, out_shape=(shape(1, 3 * LEV * 16), shape(1, 3 * LEV * 16)),
        in_specs=[VMEM], out_specs=(VMEM,) * 2, compiler_params=room(4),
        name="sides", cost_estimate=cost(10**8, 2 * 10**6),
    )(levels)
    table = pl.pallas_call(
        table_kernel, out_shape=shape(56, 256), in_specs=[VMEM], out_specs=VMEM,
        compiler_params=room(2), name="table", cost_estimate=cost(10**6, 10**6),
    )(surface)
    windows, token = pl.pallas_call(
        windows_kernel,
        out_shape=(shape(N_GX * N_GY, 1, 256), shape(8, 128)),
        in_specs=[SMEM] + [VMEM] * 4, out_specs=(VMEM,) * 2,
        scratch_shapes=[pltpu.VMEM((56, 256), F32)],
        compiler_params=room(2), name="windows", cost_estimate=cost(10**6, 10**6),
    )(picks, table, air_above, air_below, left)
    windows = lax.all_to_all(windows, ("gx", "gy"), split_axis=0, concat_axis=0, tiled=True)
    moved, token = pl.pallas_call(
        air_kernel, out_shape=(shape(3 * LEV, 16, 128), shape(8, 128)),
        in_specs=[VMEM] * 4, out_specs=(VMEM, VMEM),
        compiler_params=room(8), name="air", cost_estimate=cost(2 * 10**8, 4 * 10**6),
    )(levels, air_above, air_below, token)

    phases, message, edge_left, edge_right = pl.pallas_call(
        fire_kernel,
        out_shape=(
            shape(32, 128, 128), shape(N_GX * N_GY, 1, 256),
            shape(1, 3 * LEV * 16), shape(1, 3 * LEV * 16),
        ),
        in_specs=[SMEM, ANY, ANY] + [VMEM] * 7, out_specs=(ANY, VMEM, VMEM, VMEM),
        scratch_shapes=[
            pltpu.VMEM((32, 128, 128), F32),
            pltpu.VMEM((32, 128, 128), jnp.int32),
            pltpu.VMEM((32, 128, 128), F32),
            pltpu.VMEM((32, 48, 128), F32),
            pltpu.VMEM((32, 8, 256), F32),
            pltpu.VMEM((256, 128), F32),
            pltpu.VMEM((72, 1, 256), F32),
        ]
        + [pltpu.VMEM((256, 128), F32)] * 2
        + [pltpu.VMEM((128, 128), F32)] * 2
        + [pltpu.VMEM((128, 128), jnp.int32)] * 2
        + [pltpu.VMEM((128, 128), F32)] * 12
        + [pltpu.SemaphoreType.DMA((32,)), pltpu.SemaphoreType.DMA((6,))],
        compiler_params=room(60), name="fire", cost_estimate=cost(10**9, 8 * 10**6),
    )(
        slots, level_set, fuel, windows, jnp.asarray(words), jnp.asarray(wcol, BF16),
        jnp.asarray(spread, BF16), left, right, token,
    )
    fluxes = lax.all_to_all(message, ("gx", "gy"), split_axis=0, concat_axis=0, tiled=True)
    air_left, air_right = neighbours(edge_right, edge_left, "gy", N_GY)
    rimmed = pl.pallas_call(
        rims_kernel, out_shape=shape(3 * LEV, 16, 128), in_specs=[VMEM] * 5, out_specs=VMEM,
        compiler_params=room(8), name="rims", cost_estimate=cost(2 * 10**8, 4 * 10**6),
    )(moved, air_left, air_right, left, right)
    heat, side, smoke, heat_first, heat_last = pl.pallas_call(
        place_kernel,
        out_shape=(shape(16, 128), shape(16, 128), shape(16, 128), shape(1, 128), shape(1, 128)),
        in_specs=[SMEM, VMEM], out_specs=(VMEM,) * 5, compiler_params=room(4),
        name="place", cost_estimate=cost(10**6, 10**6),
    )(where, fluxes)
    heat_above, heat_below = neighbours(heat_last, heat_first, rows, N_GRP * N_GX)
    result = pl.pallas_call(
        final_kernel, out_shape=shape(3 * LEV, 16, 128), in_specs=[VMEM] * 7, out_specs=VMEM,
        compiler_params=room(8), name="final", cost_estimate=cost(10**6, 4 * 10**6),
    )(
        rimmed, heat, side, smoke, heat_above, heat_below, jnp.asarray(profile)
    )
    return (result.reshape(3, LEV, 16, 128), phases)


def solution(mesh):
    in_specs = (
        P(None, None, ("grp", "gx"), "gy"),
        P(("grp", "gx", "gy"), None, None),
        P(("grp", "gx", "gy"), None, None),
        P("grp", None, None),
    )
    out_specs = (P(None, None, ("grp", "gx"), "gy"), P(("grp", "gx", "gy"), None, None))
    return jax.shard_map(
        on_device, mesh=mesh, in_specs=in_specs, out_specs=out_specs, check_vma=False
    )
```

time: 172 us -> 82.8 us (0.48); the launches traced: 168 us -> 82.4 us
  other arithmetic: 43 us -> 0.96 us
  local copies, waits for them, and re-layouts: 36.8 us -> 4.54 us
  Pallas kernels: 0 us -> 28.7 us
  matrix products: 24 us -> 0 us
  waiting for transfers between devices: 22.6 us -> 12.2 us
  starting transfers between devices: 40.2 us -> 35 us
    pallas_call x0 -> x9, Pallas kernels: none -> 28.7 us  [the longest x1 17.8 us: on_device(): pl.pallas_call(fire_kernel, out_shape=(shape(32, 128, 128), shape(N_GX *...]
    dot_general x8 -> x0, matrix products: 24 us -> none  [the longest x1 17.8 us: fire_advance(): jnp.dot(jnp.dot(table, window[1], precision=highest), table.T, precision=...]
    mul x4 -> x0, other arithmetic: 14.9 us -> none  [the longest x1 9.08 us: fire_advance(): lookup(category, heat_yields) * burning]
    mul x3 -> x0, local copies, waits for them, and re-layouts: 11.2 us -> none  [the longest x1 6.37 us: fire_advance(): lookup(category, smoke_yields) * burning]
    sub x2 -> x0, other arithmetic: 11.1 us -> none  [fire_advance(): phase = phase - fire_time * rate * jnp.sqrt(upwind)]
    slice x50 -> x0, local copies, waits for them, and re-layouts: 9.09 us -> none  [the longest x8 5.97 us: fire_advance(): padded = jnp.pad(phase, 1, mode='edge')]
    reduce_sum x3 -> x0, other arithmetic: 9.04 us -> none  [the longest x1 4.45 us: fire_advance(): (lookup(category, smoke_yields) * burning).reshape(8, refine, 8, refine)]
    all_to_all x2, waiting for transfers between devices: 19.3 us -> 12.2 us  [the longest x1 6.3 us: on_device(): lax.all_to_all(windows, ('gx', 'gy'), split_axis=0, concat_axis=0, tiled=...]
  transfers between devices with their start and end apart: 10 -> 8, of which waited for: 4 -> 2; matrix products, arithmetic and copies ran while one was open for 7% -> 2% of each run, Pallas kernels for 0% -> 7%
where the time goes in v1:
time: 82.8 us; the launch traced here: 82.4 us
  starting transfers between devices  35 us (42%)
  Pallas kernels  28.7 us (35%)
  waiting for transfers between devices  12.2 us (15%)
  local copies, waits for them, and re-layouts  4.54 us (5%)
  other arithmetic  0.96 us (1%)
  between operations  0.92 us (1%)
    pallas_call x1, Pallas kernels, on_device(): pl.pallas_call(fire_kernel, out_shape=(shape(32, 128, 128), shape(N_GX *...  17.8 us
    ppermute x3, starting transfers between devices, neighbours(): after = lax.ppermute(first, axes, [(i + 1, i) for i in range(ends)])  12.4 us
    all_to_all x1, starting transfers between devices, on_device(): lax.all_to_all(windows, ('gx', 'gy'), split_axis=0, concat_axis=0, tiled=...  9.67 us
    ppermute x3, starting transfers between devices, neighbours(): before = lax.ppermute(last, axes, [(i, i + 1) for i in range(ends)])  8.35 us
    all_to_all x1, waiting for transfers between devices, on_device(): lax.all_to_all(windows, ('gx', 'gy'), split_axis=0, concat_axis=0, tiled=...  6.3 us
    all_to_all x1, waiting for transfers between devices, on_device(): lax.all_to_all(message, ('gx', 'gy'), split_axis=0, concat_axis=0, tiled=...  5.92 us
    all_to_all x1, starting transfers between devices, on_device(): lax.all_to_all(message, ('gx', 'gy'), split_axis=0, concat_axis=0, tiled=...  4.63 us
    unnamed x26, local copies, waits for them, and re-layouts  3.82 us
  transfers between devices with their start and end apart: 8, of which 2 were waited for; matrix products, arithmetic and copies ran while one was open for 2% of the time, Pallas kernels for 7%

profile of v1, /device:TPU:2, one launch (start us, length us, event | category | flops | bytes accessed | tf_op | source)
XLA Modules:
  0.0 82.4 jit_solution(14034420869497505169)
XLA Ops:
  0.6 0.0 copy-start
  0.6 0.0 copy-start.11
  0.6 0.0 copy-start.12
  0.7 1.8 %rows.1 = (f32[240,128]{1,0:T(8,128)}, f32[240,128]{1,0:T(8,128)}, f32[2,16,128]{2,1,0:T(8,128)}) custom-call(f32[240,16,128]{2,1,0:T(8,128)} %bitcast.6), custom_call_target="tpu_custom_call" | custom-call | flops 100000 | bytes 1000000 | tf_op jit(solution)/shard_map/rows/pallas_call | solution.py:525
  2.5 0.0 copy-start.8
  2.5 3.8 %collective-permute-start = (f32[240,128]{1,0:T(8,128)}, f32[240,128]{1,0:T(8,128)S(1)}, u32[]{:S(2)}, u32[]{:S(2)}) collective-permute-start(f32[240,128]{1,0:T(8,128)} %get-tuple-element.20), channel_id=1, source_target_pairs={{0,8},{8,16},{16,24},{24,32},{32,40},{40,48},{48,56},{56,64},{64,7... | collective-permute-start | bytes 368648 | tf_op jit(solution)/shard_map/ppermute | solution.py:513
  6.4 5.8 %collective-permute-start.1 = (f32[240,128]{1,0:T(8,128)}, f32[240,128]{1,0:T(8,128)S(1)}, u32[]{:S(2)}, u32[]{:S(2)}) collective-permute-start(f32[240,128]{1,0:T(8,128)} %get-tuple-element.21), channel_id=1, source_target_pairs={{8,0},{16,8},{24,16},{32,24},{40,32},{48,40},{56,48},{64,56},{72,6... | collective-permute-start | bytes 368648 | tf_op jit(solution)/shard_map/ppermute | solution.py:514
  12.2 0.0 copy-done
  12.2 1.7 %sides.1 = (f32[1,3840]{1,0:T(1,128)S(1)}, f32[1,3840]{1,0:T(1,128)S(1)}) custom-call(f32[240,16,128]{2,1,0:T(8,128)S(1)} %bitcast.7), custom_call_target="tpu_custom_call" | custom-call | flops 100000000 | bytes 2000000 | tf_op jit(solution)/shard_map/sides/pallas_call | solution.py:556
  13.9 0.0 copy-start.5
  13.9 0.6 copy-done.5
  14.5 0.0 copy-done.8
  14.5 0.3 table.1.table_ref
  14.8 0.0 copy-done.11
  14.8 0.7 dynamic-slice_reduce_fusion.slots_ref
  15.6 0.0 copy-done.12
  15.6 0.0 collective-permute-done.above_ref
  15.6 0.0 collective-permute-done.1.below_ref
  15.6 1.7 %windows.1 = (f32[64,1,256]{2,1,0:T(1,128)}, f32[8,128]{1,0:T(8,128)S(1)}) custom-call(s32[64]{0:T(128)S(1)} %add_add_fusion.pick_ref, f32[56,256]{1,0:T(8,128)S(1)} %table.1.table_ref, f32[240,128]{1,0:T(8,128)S(1)} %collective-permute-done.above_ref, f32[240,128]{1,0:T(8,128)S(1)} %collective-permute-done.1.below_ref, ...), custom_call_target="tpu_custom_call" | custom-call | flops 1000000 | bytes 1000000 | tf_op jit(solution)/shard_map/windows/pallas_call | solution.py:565
  17.3 9.7 %all-to-all-start = ((f32[64,1,256]{2,1,0:T(1,128)}), f32[64,1,256]{2,1,0:T(1,128)S(1)}, u32[]{:S(2)}, u32[]{:S(2)}) async-start(f32[64,1,256]{2,1,0:T(1,128)} %get-tuple-element.26), calls=%async_computation | async-start | bytes 131072 | tf_op jit(solution)/shard_map/all_to_all | solution.py:572
  27.0 1.8 %air.1 = (f32[240,16,128]{2,1,0:T(8,128)S(1)}, f32[8,128]{1,0:T(8,128)S(1)}) custom-call(f32[240,16,128]{2,1,0:T(8,128)S(1)} %bitcast.8, f32[240,128]{1,0:T(8,128)S(1)} %collective-permute-done.above_ref, f32[240,128]{1,0:T(8,128)S(1)} %collective-permute-done.1.below_ref, f32[8,128]{1,0:T(8,128)S(1)} %get-tuple-element.24.token_in), custom_call_target="tpu_custom_call" | custom-call | flops 200000000 | bytes 4000000 | tf_op jit(solution)/shard_map/air/pallas_call | solution.py:573
  28.8 0.0 copy-start.1
  28.9 1.3 %copy-done.1 = f32[240,16,128]{2,1,0:T(8,128)} copy-done((f32[240,16,128]{2,1,0:T(8,128)}, f32[240,16,128]{2,1,0:T(8,128)S(1)}, u32[]{:S(2)}) %copy-start.1) | copy-done | bytes 1966104
  30.1 0.6 copy-done.9
  30.7 6.3 %all-to-all-done.recv_ref = f32[64,1,256]{2,1,0:T(1,128)S(1)} async-done(((f32[64,1,256]{2,1,0:T(1,128)}), f32[64,1,256]{2,1,0:T(1,128)S(1)}, u32[]{:S(2)}, u32[]{:S(2)}) %all-to-all-start) | async-done | bytes 65568 | tf_op jit(solution)/shard_map/all_to_all | solution.py:572
  37.0 0.0 copy-done.3
  37.0 0.6 copy-done.10
  37.6 17.8 %fire.1 = (f32[32,128,128]{2,1,0:T(8,128)}, f32[64,1,256]{2,1,0:T(1,128)}, f32[1,3840]{1,0:T(1,128)}, f32[1,3840]{1,0:T(1,128)}) custom-call(s32[32]{0:T(128)} %dynamic-slice_reduce_fusion.slots_ref, f32[32,128,128]{2,1,0:T(8,128)} %phase_in.1, s32[32,128,128]{2,1,0:T(8,128)} %fuel_in.1, f32[64,1,256]{2,1,0:T(1,128)} %copy-done.10, ...), custom_call_target="tpu_custom_call" | custom-call | flops 1000000000 | bytes 8000000 | tf_op jit(solution)/shard_map/fire/pallas_call | solution.py:579
  55.4 4.6 %all-to-all-start.1 = ((f32[64,1,256]{2,1,0:T(1,128)}), f32[64,1,256]{2,1,0:T(1,128)S(1)}, u32[]{:S(2)}, u32[]{:S(2)}) async-start(f32[64,1,256]{2,1,0:T(1,128)} %get-tuple-element.31), calls=%async_computation.1 | async-start | bytes 131072 | tf_op jit(solution)/shard_map/all_to_all | solution.py:605
  60.1 0.1 pad_add_fusion
  60.1 1.8 %collective-permute-start.2 = (f32[1,3840]{1,0:T(1,128)}, f32[1,3840]{1,0:T(1,128)S(1)}, u32[]{:S(2)}, u32[]{:S(2)}) collective-permute-start(f32[1,3840]{1,0:T(1,128)} %get-tuple-element.29), channel_id=1, source_target_pairs={{0,1},{1,2},{2,3},{3,4},{4,5},{5,6},{6,7},{8,9},{9,10},{10,11},{11... | collective-permute-start | bytes 46088 | tf_op jit(solution)/shard_map/ppermute | solution.py:513
  62.0 1.3 %collective-permute-start.3 = (f32[1,3840]{1,0:T(1,128)}, f32[1,3840]{1,0:T(1,128)S(1)}, u32[]{:S(2)}, u32[]{:S(2)}) collective-permute-start(f32[1,3840]{1,0:T(1,128)} %get-tuple-element.30), channel_id=1, source_target_pairs={{1,0},{2,1},{3,2},{4,3},{5,4},{6,5},{7,6},{9,8},{10,9},{11,10},{12... | collective-permute-start | bytes 46088 | tf_op jit(solution)/shard_map/ppermute | solution.py:514
  63.3 0.8 select_reduce_fusion.where_ref
  64.1 5.9 %all-to-all-done.1.flux_ref = f32[64,1,256]{2,1,0:T(1,128)S(1)} async-done(((f32[64,1,256]{2,1,0:T(1,128)}), f32[64,1,256]{2,1,0:T(1,128)S(1)}, u32[]{:S(2)}, u32[]{:S(2)}) %all-to-all-start.1) | async-done | bytes 65568 | tf_op jit(solution)/shard_map/all_to_all | solution.py:605
  70.0 0.7 place.1
  70.8 2.7 %collective-permute-start.4 = (f32[1,128]{1,0:T(1,128)S(1)}, f32[1,128]{1,0:T(1,128)S(1)}, u32[]{:S(2)}, u32[]{:S(2)}) collective-permute-start(f32[1,128]{1,0:T(1,128)S(1)} %get-tuple-element.35), channel_id=1, source_target_pairs={{0,8},{8,16},{16,24},{24,32},{32,40},{40,48},{48,56},{56,64},{64,7... | collective-permute-start | bytes 1544 | tf_op jit(solution)/shard_map/ppermute | solution.py:513
  73.5 5.3 %collective-permute-start.5 = (f32[1,128]{1,0:T(1,128)S(1)}, f32[1,128]{1,0:T(1,128)S(1)}, u32[]{:S(2)}, u32[]{:S(2)}) collective-permute-start(f32[1,128]{1,0:T(1,128)S(1)} %get-tuple-element.36), channel_id=1, source_target_pairs={{8,0},{16,8},{24,16},{32,24},{40,32},{48,40},{56,48},{64,56},{72,6... | collective-permute-start | bytes 1544 | tf_op jit(solution)/shard_map/ppermute | solution.py:514
  78.8 0.0 collective-permute-done.2.left_ref
  78.8 0.0 collective-permute-done.3.right_ref
  78.8 0.0 copy-done.2
  78.8 0.0 copy-done.6
  78.8 0.0 copy-start.4
  78.8 0.7 copy-done.4
  79.5 1.3 %rims.1.part_ref = f32[240,16,128]{2,1,0:T(8,128)S(1)} custom-call(f32[240,16,128]{2,1,0:T(8,128)S(1)} %copy-done.2, f32[1,3840]{1,0:T(1,128)S(1)} %collective-permute-done.2.left_ref, f32[1,3840]{1,0:T(1,128)S(1)} %collective-permute-done.3.right_ref, f32[1,3840]{1,0:T(1,128)S(1)} %copy-done.4, f32[1,3840]{1,0:T(1,128)S(1)} %copy-done.6), custom_call_target="tpu_custom_call" | custom-call | flops 200000000 | bytes 4000000 | tf_op jit(solution)/shard_map/rims/pallas_call | solution.py:607
  80.8 0.0 collective-permute-done.4.above_ref
  80.8 0.0 collective-permute-done.5.below_ref
  80.8 0.0 copy-done.7
  80.8 1.5 %final.1 = f32[240,16,128]{2,1,0:T(8,128)} custom-call(f32[240,16,128]{2,1,0:T(8,128)S(1)} %rims.1.part_ref, f32[16,128]{1,0:T(8,128)S(1)} %get-tuple-element.32.heat_ref, f32[16,128]{1,0:T(8,128)S(1)} %get-tuple-element.33.side_ref, f32[16,128]{1,0:T(8,128)S(1)} %get-tuple-element.34.smoke_ref, f32[1,128]{1,0:T(1,128)S(1)} %collective-permute-done.4.above_ref, ...), custom_call_target="tpu_custom_call" | custom-call | flops 1000000 | bytes 4000000 | tf_op jit(solution)/shard_map/final/pallas_call | solution.py:618
  (10 shorter events, 0.1 us)
Async XLA Ops:
  0.6 11.6 %copy-start = (f32[3,80,16,128]{3,2,1,0:T(8,128)S(1)}, f32[3,80,16,128]{3,2,1,0:T(8,128)}, u32[]{:S(2)}) copy-start(f32[3,80,16,128]{3,2,1,0:T(8,128)} %param.9) | copy-start | bytes 5898244
  0.6 14.2 %copy-start.11 = (s32[1,64,32]{1,2,0:T(8,128)S(1)}, s32[1,64,32]{1,2,0:T(8,128)}, u32[]{:S(2)}) copy-start(s32[1,64,32]{1,2,0:T(8,128)} %param.12) | copy-start | bytes 24580
  0.6 14.9 %copy-start.12 = (s32[2]{0:T(128)S(1)}, s32[2]{0:T(128)}, u32[]{:S(2)}) copy-start(s32[2]{0:T(128)} %constant.91.clone) | copy-start | bytes 28
  2.5 12.0 %copy-start.8 = (f32[2,16,128]{2,1,0:T(8,128)S(1)}, f32[2,16,128]{2,1,0:T(8,128)}, u32[]{:S(2)}) copy-start(f32[2,16,128]{2,1,0:T(8,128)} %get-tuple-element.22.surf_ref) | copy-start | bytes 49156
  2.5 13.1 %collective-permute-start = (f32[240,128]{1,0:T(8,128)}, f32[240,128]{1,0:T(8,128)S(1)}, u32[]{:S(2)}, u32[]{:S(2)}) collective-permute-start(f32[240,128]{1,0:T(8,128)} %get-tuple-element.20), channel_id=1, source_target_pairs={{0,8},{8,16},{16,24},{24,32},{32,40},{40,48},{48,56},{56,64},{64,7... | collective-permute-start | bytes 368648 | tf_op jit(solution)/shard_map/ppermute | solution.py:513
  6.4 9.3 %collective-permute-start.1 = (f32[240,128]{1,0:T(8,128)}, f32[240,128]{1,0:T(8,128)S(1)}, u32[]{:S(2)}, u32[]{:S(2)}) collective-permute-start(f32[240,128]{1,0:T(8,128)} %get-tuple-element.21), channel_id=1, source_target_pairs={{8,0},{16,8},{24,16},{32,24},{40,32},{48,40},{56,48},{64,56},{72,6... | collective-permute-start | bytes 368648 | tf_op jit(solution)/shard_map/ppermute | solution.py:514
  13.9 0.6 copy-start.5
  13.9 23.1 %copy-start.3 = (f32[1,3840]{1,0:T(1,128)}, f32[1,3840]{1,0:T(1,128)S(1)}, u32[]{:S(2)}) copy-start(f32[1,3840]{1,0:T(1,128)S(1)} %get-tuple-element.23.left_ref.left_in.own_left_ref) | copy-start | bytes 46084
  17.3 19.7 %all-to-all-start = ((f32[64,1,256]{2,1,0:T(1,128)}), f32[64,1,256]{2,1,0:T(1,128)S(1)}, u32[]{:S(2)}, u32[]{:S(2)}) async-start(f32[64,1,256]{2,1,0:T(1,128)} %get-tuple-element.26), calls=%async_computation | async-start | bytes 131072 | tf_op jit(solution)/shard_map/all_to_all | solution.py:572
  28.8 1.3 %copy-start.1 = (f32[240,16,128]{2,1,0:T(8,128)}, f32[240,16,128]{2,1,0:T(8,128)S(1)}, u32[]{:S(2)}) copy-start(f32[240,16,128]{2,1,0:T(8,128)S(1)} %get-tuple-element.25.part_ref) | copy-start | bytes 5898244
  30.1 0.6 copy-start.9
  37.0 0.6 copy-start.10
  37.6 41.1 %copy-start.2 = (f32[240,16,128]{2,1,0:T(8,128)S(1)}, f32[240,16,128]{2,1,0:T(8,128)}, u32[]{:S(2)}) copy-start(f32[240,16,128]{2,1,0:T(8,128)} %copy-done.1) | copy-start | bytes 5898244
  37.6 41.1 %copy-start.6 = (f32[1,3840]{1,0:T(1,128)S(1)}, f32[1,3840]{1,0:T(1,128)}, u32[]{:S(2)}) copy-start(f32[1,3840]{1,0:T(1,128)} %copy-done.5) | copy-start | bytes 46084
  55.4 14.6 %all-to-all-start.1 = ((f32[64,1,256]{2,1,0:T(1,128)}), f32[64,1,256]{2,1,0:T(1,128)S(1)}, u32[]{:S(2)}, u32[]{:S(2)}) async-start(f32[64,1,256]{2,1,0:T(1,128)} %get-tuple-element.31), calls=%async_computation.1 | async-start | bytes 131072 | tf_op jit(solution)/shard_map/all_to_all | solution.py:605
  60.1 18.6 %collective-permute-start.2 = (f32[1,3840]{1,0:T(1,128)}, f32[1,3840]{1,0:T(1,128)S(1)}, u32[]{:S(2)}, u32[]{:S(2)}) collective-permute-start(f32[1,3840]{1,0:T(1,128)} %get-tuple-element.29), channel_id=1, source_target_pairs={{0,1},{1,2},{2,3},{3,4},{4,5},{5,6},{6,7},{8,9},{9,10},{10,11},{11... | collective-permute-start | bytes 46088 | tf_op jit(solution)/shard_map/ppermute | solution.py:513
  62.0 16.8 %collective-permute-start.3 = (f32[1,3840]{1,0:T(1,128)}, f32[1,3840]{1,0:T(1,128)S(1)}, u32[]{:S(2)}, u32[]{:S(2)}) collective-permute-start(f32[1,3840]{1,0:T(1,128)} %get-tuple-element.30), channel_id=1, source_target_pairs={{1,0},{2,1},{3,2},{4,3},{5,4},{6,5},{7,6},{9,8},{10,9},{11,10},{12... | collective-permute-start | bytes 46088 | tf_op jit(solution)/shard_map/ppermute | solution.py:514
  70.8 10.0 %collective-permute-start.4 = (f32[1,128]{1,0:T(1,128)S(1)}, f32[1,128]{1,0:T(1,128)S(1)}, u32[]{:S(2)}, u32[]{:S(2)}) collective-permute-start(f32[1,128]{1,0:T(1,128)S(1)} %get-tuple-element.35), channel_id=1, source_target_pairs={{0,8},{8,16},{16,24},{24,32},{32,40},{40,48},{48,56},{56,64},{64,7... | collective-permute-start | bytes 1544 | tf_op jit(solution)/shard_map/ppermute | solution.py:513
  73.5 7.4 %collective-permute-start.5 = (f32[1,128]{1,0:T(1,128)S(1)}, f32[1,128]{1,0:T(1,128)S(1)}, u32[]{:S(2)}, u32[]{:S(2)}) collective-permute-start(f32[1,128]{1,0:T(1,128)S(1)} %get-tuple-element.36), channel_id=1, source_target_pairs={{8,0},{16,8},{24,16},{32,24},{40,32},{48,40},{56,48},{64,56},{72,6... | collective-permute-start | bytes 1544 | tf_op jit(solution)/shard_map/ppermute | solution.py:514
  78.8 0.7 copy-start.4
  79.5 1.3 %copy-start.7 = (f32[80,128]{1,0:T(8,128)S(1)}, f32[80,128]{1,0:T(8,128)}, u32[]{:S(2)}) copy-start(f32[80,128]{1,0:T(8,128)} %constant.95.clone.prof_ref) | copy-start | bytes 122884

commit v2 on v1

--- a/solution.py
+++ b/solution.py
@@ -9,6 +9,7 @@
 SUB = 4
 LEV = 80
 N_GRP, N_GX, N_GY = 4, 8, 8
+WIDE = 2
 
 spread_rates = np.array(
     [0.3, 0.5, 0.9, 1.2, 0.6, 0.4, 0.7, 0.35, 0.25, 0.45, 0.55, 0.8, 1.0], np.float32
@@ -30,7 +31,7 @@
 BF16 = jnp.bfloat16
 VMEM = pl.BlockSpec(memory_space=pltpu.VMEM)
 SMEM = pl.BlockSpec(memory_space=pltpu.SMEM)
-ANY = pl.BlockSpec(memory_space=pl.ANY)
+HBM = pl.BlockSpec(memory_space=pltpu.HBM)
 
 
 def room(mib):
@@ -72,25 +73,42 @@
     return low, high, rims
 
 
-def table_kernel(surf_ref, tile_ref):
+def table_kernel(list_ref, surf_ref, tile_ref, choice_ref):
+    gx, gy = lax.axis_index("gx"), lax.axis_index("gy")
+    me = gx * N_GY + gy
+    left, right = gy > 0, gy < N_GY - 1
+    k = lax.broadcasted_iota(jnp.int32, (1, 128), 1)
+    codes = jnp.where(k < 32, me * 32 + (k ^ 7), -5)
+    singles = (
+        (40, right, me + 1, 0), (41, left, me - 1, 15), (48, right, me + 1, 16),
+        (49, left, me - 1, 31),
+    )
+    for at, there, device, tile in singles:
+        codes = jnp.where((k == at) & there, device * 32 + tile, codes)
+    listed = list_ref[0]
+    choice = jnp.zeros((64, 128), F32)
+    for slot in range(32):
+        entry = jnp.broadcast_to(listed[:, slot : slot + 1], (64, 128))
+        choice = jnp.where(entry == codes, 1.0, choice)
+    choice_ref[...] = choice.astype(BF16)
+    tile_ref[...] = jnp.zeros(tile_ref.shape, F32)
     none = jnp.zeros((8, 128), F32)
     for comp in range(2):
         lanes = slice(128 * comp, 128 * comp + 128)
         field = surf_ref[comp] * wind_gain
         for half in range(2):
-            low = high = rims = none
+            found = [none, none, none]
             for row in range(10):
                 at = 8 * half + row - 1
                 if 0 <= at < 16:
-                    low, high, rims = spread_line(field[at : at + 1], row, low, high, rims)
-            tile_ref[16 * half : 16 * half + 8, lanes] = low
-            tile_ref[16 * half + 8 : 16 * half + 16, lanes] = high
-            tile_ref[40 + 8 * half : 48 + 8 * half, lanes] = rims
-        tile_ref[32:40, lanes] = none
+                    found = spread_line(field[at : at + 1], row, *found)
+            tile_ref[16 * half : 16 * half + 8, lanes] = found[0]
+            tile_ref[16 * half + 8 : 16 * half + 16, lanes] = found[1]
+            tile_ref[40 + 8 * half : 48 + 8 * half, lanes] = found[2]
 
 
 def windows_kernel(
-    pick_ref, table_ref, above_ref, below_ref, left_ref, out_ref, token_ref, tile_ref
+    table_ref, choice_ref, above_ref, below_ref, left_ref, out_ref, token_ref, tile_ref, made_ref
 ):
     token_ref[...] = jnp.zeros((8, 128), F32) + left_ref[0:1, 0:128] * 0.0
     tile_ref[...] = table_ref[...]
@@ -107,27 +125,22 @@
             fresh = spread_line(ref[line_at, :] * wind_gain, row, *old)
             for rows, value in zip(places, fresh):
                 tile_ref[rows, lanes] = value
-
-    def one(at, carry):
-        for spot in range(16):
-            fire = 16 * at + spot
-            picks = pick_ref[fire]
-            own = tile_ref[pl.ds(picks & 63, 1), :]
-            rim_right = tile_ref[pl.ds((picks >> 6) & 63, 1), :]
-            rim_left = tile_ref[pl.ds(picks >> 12, 1), :]
-            out_ref[fire] = own + (rim_right + rim_left)
-        return carry
-
-    lax.fori_loop(0, 4, one, 0)
+    choice = choice_ref[...]
+    high, low = halves(tile_ref[...])
+    made_ref[...] = jnp.dot(choice, high.astype(BF16), preferred_element_type=F32) + jnp.dot(
+        choice, low.astype(BF16), preferred_element_type=F32
+    )
+    for fire in range(N_GX * N_GY):
+        out_ref[fire] = made_ref[fire : fire + 1, :]
 
 
 def fire_kernel(
-    slots_ref, phase_in, fuel_in, recv_ref, words_ref, wcol_ref, spread_ref,
+    list_ref, phase_in, fuel_in, recv_ref, words_ref, wcol_ref, spread_ref,
     left_in, right_in, token_in, out_ref, msg_ref, left_out, right_out,
-    phase_ref, fuel_ref, done_ref, column_ref, sums_ref, means_ref, bag_ref, *rest,
+    phase_ref, fuel_ref, done_ref, column_ref, sums_ref, means_ref, flat_ref, line_ref, *rest,
 ):
     buffers, sem, sem_in = rest[:-2], rest[-2], rest[-1]
-    sides = [buffers[at::2] for at in range(2)]
+    sides = [buffers[at::WIDE] for at in range(WIDE)]
     left_out[...] = left_in[...]
     right_out[...] = right_in[...]
     loads = []
@@ -145,36 +158,54 @@
     knot = sublanes_of(24)
     knot = (knot & 7) + (knot >> 3)
     unfold = (lane24 >= 12 * knot) & (lane24 < 12 * knot + 12)
-    place = lax.broadcasted_iota(jnp.int32, (1, 128), 1) % 12
+    place = lax.broadcasted_iota(jnp.int32, (64, 256), 1)
+    place = (place & 127) % 12
+    me = lax.axis_index("gx") * N_GY + lax.axis_index("gy")
+    entries = jnp.broadcast_to(list_ref[0, pl.ds(me, 1), :].astype(F32), (32, 32))
+    across = lax.broadcasted_iota(jnp.int32, (32, 32), 1)
+    along_slots = lax.broadcasted_iota(jnp.int32, (32, 32), 0)
+    tiles = jnp.sum(jnp.where(across == along_slots, entries, 0.0), axis=1, keepdims=True)
     words = words_ref[...]
     row8, lane8 = sublanes_of(), lanes_of()
 
-    def place_of(slot):
-        tile = slots_ref[slot]
-        return jnp.maximum(tile, 0) >> 5, jnp.maximum(tile, 0) & 15, tile >= 0
+    tiles = jnp.broadcast_to(tiles, (32, 256)).astype(jnp.int32)
+    target = lax.broadcasted_iota(jnp.int32, (32, 256), 1)
+    owner, col = tiles >> 5, tiles & 15
+    from_left = (owner - 1 == target - 64) & (col == 0) & ((owner & 7) > 0)
+    from_right = (owner + 1 == target - 128) & (col == 15) & ((owner & 7) < 7)
+    from_left = from_left & (target >= 64) & (target < 128)
+    from_right = from_right & (target >= 128) & (target < 192)
+    taken = ((owner == target) & (target < 64)) | from_left | from_right
+    taken = jnp.where(taken & (tiles >= 0), 1.0, 0.0).astype(BF16)
+    for device in range(N_GX * N_GY):
+        flat_ref[device : device + 1, :] = recv_ref[device]
+    sent = flat_ref[...]
+    sent = jnp.concatenate(
+        [
+            jnp.where(place < 10, sent, 0.0), jnp.where(place == 10, sent, 0.0),
+            jnp.where(place == 11, sent, 0.0), jnp.zeros((64, 256), F32),
+        ],
+        axis=0,
+    )
+    high, low = halves(sent)
+    lines = jnp.dot(taken, high.astype(BF16), preferred_element_type=F32) + jnp.dot(
+        taken, low.astype(BF16), preferred_element_type=F32
+    )
+    line_ref[0:32, :] = lines[:, 0:128]
+    line_ref[32:64, :] = lines[:, 128:256]
 
     def columns(at, carry):
         parts = []
-        for spot in range(4):
-            owner, col, live = place_of(4 * at + spot)
-            gy = owner & (N_GY - 1)
-            left = jnp.maximum(owner - 1, 0)
-            right = jnp.minimum(owner + 1, N_GX * N_GY - 1)
-            left_rim = (place == 10) & ((col == 0) & (gy > 0))
-            right_rim = (place == 11) & ((col == 15) & (gy < N_GY - 1))
+        for spot in range(8):
             for comp in range(2):
-                lanes = slice(128 * comp, 128 * comp + 128)
-                line = jnp.where(place < 10, recv_ref[owner, :, lanes], 0.0)
-                line = jnp.where(left_rim, recv_ref[left, :, lanes], line)
-                line = jnp.where(right_rim, recv_ref[right, :, lanes], line)
-                line = jnp.where(live, line, 0.0)
+                line = line_ref[pl.ds(32 * comp + 8 * at + spot, 1), :]
                 parts.append(jnp.where(unfold, jnp.broadcast_to(line, (24, 128)), 0.0))
         high, low = halves(jnp.concatenate(parts, axis=0))
         both = jnp.dot(high.astype(BF16), wcol_ref[...], preferred_element_type=F32) + jnp.dot(
             low.astype(BF16), wcol_ref[...], preferred_element_type=F32
         )
-        for spot in range(4):
-            column_ref[4 * at + spot] = both[48 * spot : 48 * spot + 48]
+        for spot in range(8):
+            column_ref[8 * at + spot] = both[48 * spot : 48 * spot + 48]
         return carry
 
     def result(slot):
@@ -282,11 +313,11 @@
     def into(target):
         return lambda first, values: store(target, first, values)
 
-    lax.fori_loop(0, 8, columns, 0)
-
-    def pair(at, carry):
-        slot = 2 * at
-        for start, some in zip((0, 1, 4), loads):
+    lax.fori_loop(0, 4, columns, 0)
+
+    def several(at, carry):
+        slot = WIDE * at
+        for start, some in zip((0, 2 // WIDE, 8 // WIDE), loads):
 
             @pl.when(at == start)
             def _():
@@ -303,7 +334,7 @@
             finish(slot + spot, side)
         return carry
 
-    lax.fori_loop(0, 16, pair, 0)
+    lax.fori_loop(0, 32 // WIDE, several, 0)
     high, low = halves(sums_ref[...].reshape(256, 256))
     spread = spread_ref[...]
     means_ref[...] = (
@@ -313,25 +344,28 @@
     dense = means_ref[pl.ds(0, 32, stride=8), :]
     for row in range(1, 8):
         dense = dense + pltpu.roll(means_ref[pl.ds(row, 32, stride=8), :], 16 * row, 1)
-    means_ref[0:32, :] = dense
-    bag_ref[...] = jnp.zeros(bag_ref.shape, F32)
-    spot = lax.broadcasted_iota(jnp.int32, (1, 128), 1) % 16
-    own, beside = slice(0, 128), slice(128, 256)
-
-    def send(slot, carry):
-        owner, col, live = place_of(slot)
-        gy = owner & (N_GY - 1)
-        line = means_ref[pl.ds(slot, 1), :]
-        bag_ref[jnp.where(live, owner, 64), :, own] = line
-        to_left = live & (col == 0) & (gy > 0)
-        to_right = live & (col == 15) & (gy < N_GY - 1)
-        target = jnp.where(to_left, owner - 1, jnp.where(to_right, owner + 1, 64))
-        kept = jnp.where(to_left, 0, 7)
-        bag_ref[target, :, beside] = jnp.where(spot == kept, line, bag_ref[target, :, beside])
-        return carry
-
-    lax.fori_loop(0, 32, send, 0, unroll=4)
-    msg_ref[...] = bag_ref[0:64]
+    tile_row = list_ref[0, pl.ds(me, 1), :]
+    owners = jnp.broadcast_to(tile_row >> 5, (64, 32))
+    col = jnp.broadcast_to(tile_row & 15, (64, 32))
+    live = jnp.broadcast_to(tile_row, (64, 32)) >= 0
+    device = lax.broadcasted_iota(jnp.int32, (64, 32), 0)
+    to_left = live & (owners - 1 == device) & (col == 0) & ((owners & 7) > 0)
+    to_right = live & (owners + 1 == device) & (col == 15) & ((owners & 7) < 7)
+    spot = lax.broadcasted_iota(jnp.int32, (32, 128), 1) & 15
+    picked = []
+    for chosen, kept in (
+        (live & (owners == device), None), (to_left, spot == 0), (to_right, spot == 7),
+    ):
+        chosen = jnp.where(chosen, 1.0, 0.0).astype(BF16)
+        high, low = halves(dense if kept is None else jnp.where(kept, dense, 0.0))
+        picked.append(
+            jnp.dot(chosen, high.astype(BF16), preferred_element_type=F32)
+            + jnp.dot(chosen, low.astype(BF16), preferred_element_type=F32)
+        )
+    flat_ref[:, 0:128] = picked[0]
+    flat_ref[:, 128:256] = picked[1] + picked[2]
+    for device in range(N_GX * N_GY):
+        msg_ref[device] = flat_ref[device : device + 1, :]
 
     def settle(slot, carry):
         result(slot).wait()
@@ -405,12 +439,12 @@
     row = lax.broadcasted_iota(jnp.int32, (8, 16, 128), 1)
 
     def chunk(at, carry):
+        levels = pl.ds(8 * at, 8)
         fields = []
         for part in range(3):
-            start = part * LEV + at * 8
-            mid = air_ref[pl.ds(start, 8)]
-            above = above_ref[pl.ds(start, 8), :][:, None, :]
-            below = below_ref[pl.ds(start, 8), :][:, None, :]
+            mid = air_ref[part, levels]
+            above = above_ref[part, levels, :][:, None, :]
+            below = below_ref[part, levels, :][:, None, :]
             up = jnp.where(row == 0, above, pltpu.roll(mid, 1, 1))
             down = jnp.where(row == 15, below, pltpu.roll(mid, 15, 1))
             left = jnp.where(lane == 0, 0.0, pltpu.roll(mid, 1, 2))
@@ -419,7 +453,7 @@
         for part in range(2):
             mid, up, down, left, right = fields[part]
             around = (up + down) + (left + right)
-            out_ref[pl.ds(part * LEV + at * 8, 8)] = mid + viscosity * (around - 4.0 * mid)
+            out_ref[part, levels] = mid + viscosity * (around - 4.0 * mid)
         u, v = fields[0][0], fields[1][0]
         mid, up, down, left, right = fields[2]
         upwind = (
@@ -428,10 +462,10 @@
             + jnp.maximum(v, 0.0) * (mid - left)
             + jnp.minimum(v, 0.0) * (right - mid)
         )
-        out_ref[pl.ds(2 * LEV + at * 8, 8)] = mid - courant * upwind
+        out_ref[2, levels] = mid - courant * upwind
         return carry
 
-    lax.fori_loop(0, LEV // 8, chunk, 0)
+    lax.fori_loop(0, 2, chunk, 0)
 
 
 def rims_kernel(part_ref, left_ref, right_ref, own_left_ref, own_right_ref, out_ref):
@@ -467,23 +501,38 @@
     lax.fori_loop(0, LEV // 8, chunk, 0, unroll=2)
 
 
-def final_kernel(part_ref, heat_ref, side_ref, smoke_ref, above_ref, below_ref, prof_ref, out_ref):
+def final_kernel(
+    part_ref, heat_ref, side_ref, smoke_ref, above_ref, below_ref, prof_ref,
+    out_ref, made_ref, sem,
+):
     heat = heat_ref[...]
     row = sublanes_of(16)
     up = jnp.where(row == 0, above_ref[...], pltpu.roll(heat, 1, 0))
     down = jnp.where(row == 15, below_ref[...], pltpu.roll(heat, 15, 0))
     sources = (0.5 * (down - up), side_ref[...], smoke_ref[...])
-
-    def one(at, carry):
-        for spot in range(4):
-            level = 4 * at + spot
-            weight = prof_ref[pl.ds(level, 1), :]
-            for part in range(3):
-                before = part_ref[part * LEV + level]
-                out_ref[part * LEV + level] = before + weight * sources[part]
-        return carry
-
-    lax.fori_loop(0, LEV // 4, one, 0)
+    copies = []
+    for part in range(3):
+        for half in range(2):
+            first = part * LEV + half * (LEV // 2)
+
+            def one(at, carry):
+                for spot in range(8):
+                    level = half * (LEV // 2) + 8 * at + spot
+                    weight = prof_ref[pl.ds(level, 1), :]
+                    before = part_ref[part * LEV + level]
+                    made_ref[part * LEV + level] = before + weight * sources[part]
+                return carry
+
+            lax.fori_loop(0, LEV // 16, one, 0)
+            some = pl.ds(first, LEV // 2)
+            copies.append(
+                pltpu.make_async_copy(
+                    made_ref.at[some], out_ref.at[some], sem.at[2 * part + half]
+                )
+            )
+            copies[-1].start()
+    for copy in copies:
+        copy.wait()
 
 
 def constants():
@@ -525,22 +574,12 @@
     first, last, surface = pl.pallas_call(
         rows_kernel,
         out_shape=(shape(3 * LEV, 128), shape(3 * LEV, 128), shape(2, 16, 128)),
-        in_specs=[ANY], out_specs=(VMEM,) * 3, scratch_shapes=[pltpu.SemaphoreType.DMA((4,))],
+        in_specs=[HBM], out_specs=(VMEM,) * 3, scratch_shapes=[pltpu.SemaphoreType.DMA((4,))],
         compiler_params=room(60), name="rows", cost_estimate=cost(10**5, 10**6),
     )(levels)
     air_above, air_below = neighbours(last, first, rows, N_GRP * N_GX)
 
     listed = tile_list[0]
-    slots = lax.dynamic_index_in_dim(listed, myself, 0, keepdims=False)
-    right_at = jnp.where(my_gy < N_GY - 1, (myself + 1) * 32, -64)
-    left_at = jnp.where(my_gy > 0, (myself - 1) * 32 + 15, -64)
-    own_tile = jnp.where(listed // 32 == myself, ((listed % 32) ^ 7) - 32, 0)
-    own_tile = jnp.where(listed >= 0, own_tile, 0)
-    own_row = jnp.min(own_tile, axis=1) + 32
-    rim_right = jnp.where(listed == right_at, 8, jnp.where(listed == right_at + 16, 16, 0))
-    rim_left = jnp.where(listed == left_at, 9, jnp.where(listed == left_at + 16, 17, 0))
-    picks = own_row + jnp.max(rim_right, axis=1) * 64 + jnp.max(rim_left, axis=1) * 4096
-    picks = picks + 32 * 64 + 32 * 4096
     beside = jnp.array([15, 31], jnp.int32)
     wanted = jnp.concatenate(
         [
@@ -558,23 +597,28 @@
         in_specs=[VMEM], out_specs=(VMEM,) * 2, compiler_params=room(4),
         name="sides", cost_estimate=cost(10**8, 2 * 10**6),
     )(levels)
-    table = pl.pallas_call(
-        table_kernel, out_shape=shape(56, 256), in_specs=[VMEM], out_specs=VMEM,
+    table, choice = pl.pallas_call(
+        table_kernel, out_shape=(shape(128, 256), shape(64, 128, dtype=BF16)),
+        in_specs=[VMEM, VMEM], out_specs=(VMEM, VMEM),
         compiler_params=room(2), name="table", cost_estimate=cost(10**6, 10**6),
-    )(surface)
+    )(tile_list, surface)
     windows, token = pl.pallas_call(
         windows_kernel,
         out_shape=(shape(N_GX * N_GY, 1, 256), shape(8, 128)),
-        in_specs=[SMEM] + [VMEM] * 4, out_specs=(VMEM,) * 2,
-        scratch_shapes=[pltpu.VMEM((56, 256), F32)],
+        in_specs=[VMEM] * 5, out_specs=(VMEM,) * 2,
+        scratch_shapes=[pltpu.VMEM((128, 256), F32), pltpu.VMEM((64, 256), F32)],
         compiler_params=room(2), name="windows", cost_estimate=cost(10**6, 10**6),
-    )(picks, table, air_above, air_below, left)
+    )(table, choice, air_above, air_below, left)
     windows = lax.all_to_all(windows, ("gx", "gy"), split_axis=0, concat_axis=0, tiled=True)
+    per_block = pl.BlockSpec((3, 16, 16, 128), lambda i: (0, i, 0, 0))
+    per_rows = pl.BlockSpec((3, 16, 128), lambda i: (0, i, 0))
+    fixed = pl.BlockSpec((8, 128), lambda i: (0, 0))
     moved, token = pl.pallas_call(
-        air_kernel, out_shape=(shape(3 * LEV, 16, 128), shape(8, 128)),
-        in_specs=[VMEM] * 4, out_specs=(VMEM, VMEM),
-        compiler_params=room(8), name="air", cost_estimate=cost(2 * 10**8, 4 * 10**6),
-    )(levels, air_above, air_below, token)
+        air_kernel, out_shape=(shape(3, LEV, 16, 128), shape(8, 128)), grid=(LEV // 16,),
+        in_specs=[per_block, per_rows, per_rows, fixed], out_specs=(per_block, fixed),
+        compiler_params=room(60), name="air", cost_estimate=cost(2 * 10**8, 4 * 10**6),
+    )(air, air_above.reshape(3, LEV, 128), air_below.reshape(3, LEV, 128), token)
+    moved = moved.reshape(3 * LEV, 16, 128)
 
     phases, message, edge_left, edge_right = pl.pallas_call(
         fire_kernel,
@@ -582,7 +626,7 @@
             shape(32, 128, 128), shape(N_GX * N_GY, 1, 256),
             shape(1, 3 * LEV * 16), shape(1, 3 * LEV * 16),
         ),
-        in_specs=[SMEM, ANY, ANY] + [VMEM] * 7, out_specs=(ANY, VMEM, VMEM, VMEM),
+        in_specs=[VMEM, HBM, HBM] + [VMEM] * 7, out_specs=(HBM, VMEM, VMEM, VMEM),
         scratch_shapes=[
             pltpu.VMEM((32, 128, 128), F32),
             pltpu.VMEM((32, 128, 128), jnp.int32),
@@ -590,16 +634,17 @@
             pltpu.VMEM((32, 48, 128), F32),
             pltpu.VMEM((32, 8, 256), F32),
             pltpu.VMEM((256, 128), F32),
-            pltpu.VMEM((72, 1, 256), F32),
+            pltpu.VMEM((64, 256), F32),
+            pltpu.VMEM((64, 128), F32),
         ]
-        + [pltpu.VMEM((256, 128), F32)] * 2
-        + [pltpu.VMEM((128, 128), F32)] * 2
-        + [pltpu.VMEM((128, 128), jnp.int32)] * 2
-        + [pltpu.VMEM((128, 128), F32)] * 12
+        + [pltpu.VMEM((256, 128), F32)] * WIDE
+        + [pltpu.VMEM((128, 128), F32)] * WIDE
+        + [pltpu.VMEM((128, 128), jnp.int32)] * WIDE
+        + [pltpu.VMEM((128, 128), F32)] * (6 * WIDE)
         + [pltpu.SemaphoreType.DMA((32,)), pltpu.SemaphoreType.DMA((6,))],
         compiler_params=room(60), name="fire", cost_estimate=cost(10**9, 8 * 10**6),
     )(
-        slots, level_set, fuel, windows, jnp.asarray(words), jnp.asarray(wcol, BF16),
+        tile_list, level_set, fuel, windows, jnp.asarray(words), jnp.asarray(wcol, BF16),
         jnp.asarray(spread, BF16), left, right, token,
     )
     fluxes = lax.all_to_all(message, ("gx", "gy"), split_axis=0, concat_axis=0, tiled=True)
@@ -616,7 +661,8 @@
     )(where, fluxes)
     heat_above, heat_below = neighbours(heat_last, heat_first, rows, N_GRP * N_GX)
     result = pl.pallas_call(
-        final_kernel, out_shape=shape(3 * LEV, 16, 128), in_specs=[VMEM] * 7, out_specs=VMEM,
+        final_kernel, out_shape=shape(3 * LEV, 16, 128), in_specs=[VMEM] * 7, out_specs=HBM,
+        scratch_shapes=[pltpu.VMEM((3 * LEV, 16, 128), F32), pltpu.SemaphoreType.DMA((6,))],
         compiler_params=room(8), name="final", cost_estimate=cost(10**6, 4 * 10**6),
     )(
         rimmed, heat, side, smoke, heat_above, heat_below, jnp.asarray(profile)

time: 82.8 us -> 83.7 us (1.011)
  Pallas kernels: 28.7 us -> 32 us
  local copies, waits for them, and re-layouts: 4.54 us -> 2.66 us
  waiting for transfers between devices: 12.2 us -> 10.7 us
  starting transfers between devices: 35 us -> 35.9 us
    pallas_call x2, Pallas kernels: 2.13 us -> 6.86 us  [the longest x1 5.23 us: on_device(): pl.pallas_call(air_kernel, out_shape=(shape(3, LEV, 16, 128), shape(8, 12...]
    all_to_all x1, waiting for transfers between devices: 6.3 us -> 4.76 us  [on_device(): lax.all_to_all(windows, ('gx', 'gy'), split_axis=0, concat_axis=0, tiled=...]
    unnamed x26 -> x31, local copies, waits for them, and re-layouts: 3.82 us -> 2.66 us
    all_to_all x1, starting transfers between devices: 4.63 us -> 5.55 us  [on_device(): lax.all_to_all(message, ('gx', 'gy'), split_axis=0, concat_axis=0, tiled=...]
  transfers between devices with their start and end apart: 8 -> 8, of which waited for: 2 -> 2; matrix products, arithmetic and copies ran while one was open for 2% -> 1% of each run, Pallas kernels for 7% -> 13%
where the time goes in v2:
time: 83.7 us; the launch traced here: 83.1 us
  starting transfers between devices  35.9 us (43%)
  Pallas kernels  32 us (38%)
  waiting for transfers between devices  10.7 us (13%)
  local copies, waits for them, and re-layouts  2.66 us (3%)
  between operations  0.92 us (1%)
  other arithmetic  0.9 us (1%)
    pallas_call x1, Pallas kernels, on_device(): pl.pallas_call(fire_kernel, out_shape=(shape(32, 128, 128), shape(N_GX *...  17.3 us
    ppermute x3, starting transfers between devices, neighbours(): after = lax.ppermute(first, axes, [(i + 1, i) for i in range(ends)])  12.5 us
    all_to_all x1, starting transfers between devices, on_device(): lax.all_to_all(windows, ('gx', 'gy'), split_axis=0, concat_axis=0, tiled=...  9.5 us
    ppermute x3, starting transfers between devices, neighbours(): before = lax.ppermute(last, axes, [(i, i + 1) for i in range(ends)])  8.38 us
    all_to_all x1, waiting for transfers between devices, on_device(): lax.all_to_all(message, ('gx', 'gy'), split_axis=0, concat_axis=0, tiled=...  5.88 us
    all_to_all x1, starting transfers between devices, on_device(): lax.all_to_all(message, ('gx', 'gy'), split_axis=0, concat_axis=0, tiled=...  5.55 us
    pallas_call x1, Pallas kernels, on_device(): pl.pallas_call(air_kernel, out_shape=(shape(3, LEV, 16, 128), shape(8, 12...  5.23 us
    all_to_all x1, waiting for transfers between devices, on_device(): lax.all_to_all(windows, ('gx', 'gy'), split_axis=0, concat_axis=0, tiled=...  4.76 us
  transfers between devices with their start and end apart: 8, of which 2 were waited for; matrix products, arithmetic and copies ran while one was open for 1% of the time, Pallas kernels for 13%

profile of v2, /device:TPU:2, one launch (start us, length us, event | category | flops | bytes accessed | tf_op | source)
XLA Modules:
  0.0 83.1 jit_solution(9479503803618274484)
XLA Ops:
  0.6 0.0 copy-start
  0.6 0.0 copy-start.13
  0.7 0.0 copy-start.14
  0.7 1.8 %rows.1 = (f32[240,128]{1,0:T(8,128)}, f32[240,128]{1,0:T(8,128)}, f32[2,16,128]{2,1,0:T(8,128)}) custom-call(f32[240,16,128]{2,1,0:T(8,128)} %bitcast.6), custom_call_target="tpu_custom_call" | custom-call | flops 100000 | bytes 1000000 | tf_op jit(solution)/shard_map/rows/pallas_call | solution.py:574
  2.5 0.0 copy-start.10
  2.5 3.8 %collective-permute-start = (f32[240,128]{1,0:T(8,128)}, f32[240,128]{1,0:T(8,128)S(1)}, u32[]{:S(2)}, u32[]{:S(2)}) collective-permute-start(f32[240,128]{1,0:T(8,128)} %get-tuple-element.22), channel_id=1, source_target_pairs={{0,8},{8,16},{16,24},{24,32},{32,40},{40,48},{48,56},{56,64},{64,7... | collective-permute-start | bytes 368648 | tf_op jit(solution)/shard_map/ppermute | solution.py:562
  6.4 5.8 %collective-permute-start.1 = (f32[240,128]{1,0:T(8,128)}, f32[240,128]{1,0:T(8,128)S(1)}, u32[]{:S(2)}, u32[]{:S(2)}) collective-permute-start(f32[240,128]{1,0:T(8,128)} %get-tuple-element.23), channel_id=1, source_target_pairs={{8,0},{16,8},{24,16},{32,24},{40,32},{48,40},{56,48},{64,56},{72,6... | collective-permute-start | bytes 368648 | tf_op jit(solution)/shard_map/ppermute | solution.py:563
  12.2 0.0 copy-done
  12.2 1.7 %sides.1 = (f32[1,3840]{1,0:T(1,128)S(1)}, f32[1,3840]{1,0:T(1,128)S(1)}) custom-call(f32[240,16,128]{2,1,0:T(8,128)S(1)} %bitcast.7), custom_call_target="tpu_custom_call" | custom-call | flops 100000000 | bytes 2000000 | tf_op jit(solution)/shard_map/sides/pallas_call | solution.py:595
  13.9 0.6 copy-done.7
  14.5 0.0 copy-done.13
  14.5 0.1 copy.14.list_ref
  14.6 0.0 copy-done.10
  14.6 1.6 %table.1 = (f32[128,256]{1,0:T(8,128)S(1)}, bf16[64,128]{1,0:T(8,128)(2,1)S(1)}) custom-call(s32[1,64,32]{2,1,0:T(8,128)S(1)} %copy.14.list_ref, f32[2,16,128]{2,1,0:T(8,128)S(1)} %copy-done.10), custom_call_target="tpu_custom_call" | custom-call | flops 1000000 | bytes 1000000 | tf_op jit(solution)/shard_map/table/pallas_call | solution.py:600
  16.2 0.0 copy-done.14
  16.2 0.0 collective-permute-done.above_ref
  16.3 0.0 copy-start.2
  16.3 0.0 collective-permute-done.1.below_ref
  16.3 0.0 copy-start.3
  16.3 1.0 %windows.1 = (f32[64,1,256]{2,1,0:T(1,128)}, f32[8,128]{1,0:T(8,128)S(1)}) custom-call(f32[128,256]{1,0:T(8,128)S(1)} %get-tuple-element.25.table_ref, bf16[64,128]{1,0:T(8,128)(2,1)S(1)} %get-tuple-element.26.choice_ref, f32[240,128]{1,0:T(8,128)S(1)} %collective-permute-done.above_ref, f32[240,128]{1,0:T(8,128)S(1)} %collective-permute-done.1.below_ref, ...), custom_call_target="tpu_custom_call" | custom-call | flops 1000000 | bytes 1000000 | tf_op jit(solution)/shard_map/windows/pallas_call | solution.py:605
  17.2 0.6 copy-done.11
  17.8 9.5 %all-to-all-start = ((f32[64,1,256]{2,1,0:T(1,128)}), f32[64,1,256]{2,1,0:T(1,128)S(1)}, u32[]{:S(2)}, u32[]{:S(2)}) async-start(f32[64,1,256]{2,1,0:T(1,128)} %get-tuple-element.30), calls=%async_computation | async-start | bytes 131072 | tf_op jit(solution)/shard_map/all_to_all | solution.py:612
  27.4 0.0 copy-done.2
  27.4 0.0 copy-done.3
  27.4 5.2 %air.1 = (f32[3,80,16,128]{3,2,1,0:T(8,128)}, f32[8,128]{1,0:T(8,128)}) custom-call(f32[3,80,16,128]{3,2,1,0:T(8,128)} %air_ref.1, f32[3,80,128]{2,1,0:T(8,128)} %bitcast.9, f32[3,80,128]{2,1,0:T(8,128)} %bitcast.10, f32[8,128]{1,0:T(8,128)} %copy-done.11), custom_call_target="tpu_custom_call" | custom-call | flops 200000000 | bytes 4000000 | tf_op jit(solution)/shard_map/air/pallas_call | solution.py:616
  32.6 4.8 %all-to-all-done.recv_ref = f32[64,1,256]{2,1,0:T(1,128)S(1)} async-done(((f32[64,1,256]{2,1,0:T(1,128)}), f32[64,1,256]{2,1,0:T(1,128)S(1)}, u32[]{:S(2)}, u32[]{:S(2)}) %all-to-all-start) | async-done | bytes 65568 | tf_op jit(solution)/shard_map/all_to_all | solution.py:612
  37.4 0.0 copy-done.5
  37.4 0.0 copy-done.4
  37.4 0.6 copy-done.12
  38.0 17.3 %fire.1 = (f32[32,128,128]{2,1,0:T(8,128)}, f32[64,1,256]{2,1,0:T(1,128)}, f32[1,3840]{1,0:T(1,128)}, f32[1,3840]{1,0:T(1,128)}) custom-call(s32[1,64,32]{2,1,0:T(8,128)} %copy-done.4, f32[32,128,128]{2,1,0:T(8,128)} %phase_in.1, s32[32,128,128]{2,1,0:T(8,128)} %fuel_in.1, f32[64,1,256]{2,1,0:T(1,128)} %copy-done.12, s32[8,128]{1,0:T(8,128)} %constant.38.clone.words_ref, ...), custom_call_target="tpu_custom_call" | custom-call | flops 1000000000 | bytes 8000000 | tf_op jit(solution)/shard_map/fire/pallas_call | solution.py:623
  55.3 5.6 %all-to-all-start.1 = ((f32[64,1,256]{2,1,0:T(1,128)}), f32[64,1,256]{2,1,0:T(1,128)S(1)}, u32[]{:S(2)}, u32[]{:S(2)}) async-start(f32[64,1,256]{2,1,0:T(1,128)} %get-tuple-element.35), calls=%async_computation.1 | async-start | bytes 131072 | tf_op jit(solution)/shard_map/all_to_all | solution.py:650
  60.9 0.1 pad_add_fusion
  60.9 1.9 %collective-permute-start.2 = (f32[1,3840]{1,0:T(1,128)}, f32[1,3840]{1,0:T(1,128)S(1)}, u32[]{:S(2)}, u32[]{:S(2)}) collective-permute-start(f32[1,3840]{1,0:T(1,128)} %get-tuple-element.33), channel_id=1, source_target_pairs={{0,1},{1,2},{2,3},{3,4},{4,5},{5,6},{6,7},{8,9},{9,10},{10,11},{11... | collective-permute-start | bytes 46088 | tf_op jit(solution)/shard_map/ppermute | solution.py:562
  62.9 1.3 %collective-permute-start.3 = (f32[1,3840]{1,0:T(1,128)}, f32[1,3840]{1,0:T(1,128)S(1)}, u32[]{:S(2)}, u32[]{:S(2)}) collective-permute-start(f32[1,3840]{1,0:T(1,128)} %get-tuple-element.34), channel_id=1, source_target_pairs={{1,0},{2,1},{3,2},{4,3},{5,4},{6,5},{7,6},{9,8},{10,9},{11,10},{12... | collective-permute-start | bytes 46088 | tf_op jit(solution)/shard_map/ppermute | solution.py:563
  64.2 0.8 select_reduce_fusion.where_ref
  65.0 5.9 %all-to-all-done.1.flux_ref = f32[64,1,256]{2,1,0:T(1,128)S(1)} async-done(((f32[64,1,256]{2,1,0:T(1,128)}), f32[64,1,256]{2,1,0:T(1,128)S(1)}, u32[]{:S(2)}, u32[]{:S(2)}) %all-to-all-start.1) | async-done | bytes 65568 | tf_op jit(solution)/shard_map/all_to_all | solution.py:650
  70.9 0.7 place.1
  71.6 2.6 %collective-permute-start.4 = (f32[1,128]{1,0:T(1,128)S(1)}, f32[1,128]{1,0:T(1,128)S(1)}, u32[]{:S(2)}, u32[]{:S(2)}) collective-permute-start(f32[1,128]{1,0:T(1,128)S(1)} %get-tuple-element.39), channel_id=1, source_target_pairs={{0,8},{8,16},{16,24},{24,32},{32,40},{40,48},{48,56},{56,64},{64,7... | collective-permute-start | bytes 1544 | tf_op jit(solution)/shard_map/ppermute | solution.py:562
  74.3 5.4 %collective-permute-start.5 = (f32[1,128]{1,0:T(1,128)S(1)}, f32[1,128]{1,0:T(1,128)S(1)}, u32[]{:S(2)}, u32[]{:S(2)}) collective-permute-start(f32[1,128]{1,0:T(1,128)S(1)} %get-tuple-element.40), channel_id=1, source_target_pairs={{8,0},{16,8},{24,16},{32,24},{40,32},{48,40},{56,48},{64,56},{72,6... | collective-permute-start | bytes 1544 | tf_op jit(solution)/shard_map/ppermute | solution.py:563
  79.6 0.0 collective-permute-done.2.left_ref
  79.6 0.0 collective-permute-done.3.right_ref
  79.6 0.0 copy-done.1
  79.7 0.7 copy-done.6
  80.4 1.3 %rims.1.part_ref = f32[240,16,128]{2,1,0:T(8,128)S(1)} custom-call(f32[240,16,128]{2,1,0:T(8,128)S(1)} %bitcast.8, f32[1,3840]{1,0:T(1,128)S(1)} %collective-permute-done.2.left_ref, f32[1,3840]{1,0:T(1,128)S(1)} %collective-permute-done.3.right_ref, f32[1,3840]{1,0:T(1,128)S(1)} %copy-done.6, f32[1,3840]{1,0:T(1,128)S(1)} %copy-done.8), custom_call_target="tpu_custom_call" | custom-call | flops 200000000 | bytes 4000000 | tf_op jit(solution)/shard_map/rims/pallas_call | solution.py:652
  81.7 0.0 collective-permute-done.4.above_ref
  81.7 0.0 collective-permute-done.5.below_ref
  81.7 0.0 copy-done.9
  81.7 1.4 %final.1 = f32[240,16,128]{2,1,0:T(8,128)} custom-call(f32[240,16,128]{2,1,0:T(8,128)S(1)} %rims.1.part_ref, f32[16,128]{1,0:T(8,128)S(1)} %get-tuple-element.36.heat_ref, f32[16,128]{1,0:T(8,128)S(1)} %get-tuple-element.37.side_ref, f32[16,128]{1,0:T(8,128)S(1)} %get-tuple-element.38.smoke_ref, f32[1,128]{1,0:T(1,128)S(1)} %collective-permute-done.4.above_ref, ...), custom_call_target="tpu_custom_call" | custom-call | flops 1000000 | bytes 4000000 | tf_op jit(solution)/shard_map/final/pallas_call | solution.py:663
  (12 shorter events, 0.0 us)
Async XLA Ops:
  0.6 11.6 %copy-start = (f32[3,80,16,128]{3,2,1,0:T(8,128)S(1)}, f32[3,80,16,128]{3,2,1,0:T(8,128)}, u32[]{:S(2)}) copy-start(f32[3,80,16,128]{3,2,1,0:T(8,128)} %air_ref.1) | copy-start | bytes 5898244
  0.6 13.9 %copy-start.13 = (s32[1,64,32]{1,2,0:T(8,128)S(1)}, s32[1,64,32]{1,2,0:T(8,128)}, u32[]{:S(2)}) copy-start(s32[1,64,32]{1,2,0:T(8,128)} %param.12) | copy-start | bytes 24580
  0.7 15.6 %copy-start.14 = (s32[2]{0:T(128)S(1)}, s32[2]{0:T(128)}, u32[]{:S(2)}) copy-start(s32[2]{0:T(128)} %constant.37.clone) | copy-start | bytes 28
  2.5 12.1 %copy-start.10 = (f32[2,16,128]{2,1,0:T(8,128)S(1)}, f32[2,16,128]{2,1,0:T(8,128)}, u32[]{:S(2)}) copy-start(f32[2,16,128]{2,1,0:T(8,128)} %get-tuple-element.24.surf_ref) | copy-start | bytes 49156
  2.5 13.7 %collective-permute-start = (f32[240,128]{1,0:T(8,128)}, f32[240,128]{1,0:T(8,128)S(1)}, u32[]{:S(2)}, u32[]{:S(2)}) collective-permute-start(f32[240,128]{1,0:T(8,128)} %get-tuple-element.22), channel_id=1, source_target_pairs={{0,8},{8,16},{16,24},{24,32},{32,40},{40,48},{48,56},{56,64},{64,7... | collective-permute-start | bytes 368648 | tf_op jit(solution)/shard_map/ppermute | solution.py:562
  6.4 9.9 %collective-permute-start.1 = (f32[240,128]{1,0:T(8,128)}, f32[240,128]{1,0:T(8,128)S(1)}, u32[]{:S(2)}, u32[]{:S(2)}) collective-permute-start(f32[240,128]{1,0:T(8,128)} %get-tuple-element.23), channel_id=1, source_target_pairs={{8,0},{16,8},{24,16},{32,24},{40,32},{48,40},{56,48},{64,56},{72,6... | collective-permute-start | bytes 368648 | tf_op jit(solution)/shard_map/ppermute | solution.py:563
  13.9 0.6 copy-start.7
  14.5 22.9 %copy-start.5 = (f32[1,3840]{1,0:T(1,128)}, f32[1,3840]{1,0:T(1,128)S(1)}, u32[]{:S(2)}) copy-start(f32[1,3840]{1,0:T(1,128)S(1)} %get-tuple-element.27.left_ref.left_in.own_left_ref) | copy-start | bytes 46084
  14.6 22.8 %copy-start.4 = (s32[1,64,32]{2,1,0:T(8,128)}, s32[1,64,32]{2,1,0:T(8,128)S(1)}, u32[]{:S(2)}) copy-start(s32[1,64,32]{2,1,0:T(8,128)S(1)} %copy.14.list_ref) | copy-start | bytes 24580
  16.3 11.1 %copy-start.2 = (f32[240,128]{1,0:T(8,128)}, f32[240,128]{1,0:T(8,128)S(1)}, u32[]{:S(2)}) copy-start(f32[240,128]{1,0:T(8,128)S(1)} %collective-permute-done.above_ref) | copy-start | bytes 368644
  16.3 11.1 %copy-start.3 = (f32[240,128]{1,0:T(8,128)}, f32[240,128]{1,0:T(8,128)S(1)}, u32[]{:S(2)}) copy-start(f32[240,128]{1,0:T(8,128)S(1)} %collective-permute-done.1.below_ref) | copy-start | bytes 368644
  17.2 0.6 copy-start.11
  17.8 19.5 %all-to-all-start = ((f32[64,1,256]{2,1,0:T(1,128)}), f32[64,1,256]{2,1,0:T(1,128)S(1)}, u32[]{:S(2)}, u32[]{:S(2)}) async-start(f32[64,1,256]{2,1,0:T(1,128)} %get-tuple-element.30), calls=%async_computation | async-start | bytes 131072 | tf_op jit(solution)/shard_map/all_to_all | solution.py:612
  37.4 0.6 copy-start.12
  38.0 41.7 %copy-start.1 = (f32[3,80,16,128]{3,2,1,0:T(8,128)S(1)}, f32[3,80,16,128]{3,2,1,0:T(8,128)}, u32[]{:S(2)}) copy-start(f32[3,80,16,128]{3,2,1,0:T(8,128)} %get-tuple-element.29) | copy-start | bytes 5898244
  38.0 41.7 %copy-start.8 = (f32[1,3840]{1,0:T(1,128)S(1)}, f32[1,3840]{1,0:T(1,128)}, u32[]{:S(2)}) copy-start(f32[1,3840]{1,0:T(1,128)} %copy-done.7) | copy-start | bytes 46084
  55.3 15.6 %all-to-all-start.1 = ((f32[64,1,256]{2,1,0:T(1,128)}), f32[64,1,256]{2,1,0:T(1,128)S(1)}, u32[]{:S(2)}, u32[]{:S(2)}) async-start(f32[64,1,256]{2,1,0:T(1,128)} %get-tuple-element.35), calls=%async_computation.1 | async-start | bytes 131072 | tf_op jit(solution)/shard_map/all_to_all | solution.py:650
  60.9 18.7 %collective-permute-start.2 = (f32[1,3840]{1,0:T(1,128)}, f32[1,3840]{1,0:T(1,128)S(1)}, u32[]{:S(2)}, u32[]{:S(2)}) collective-permute-start(f32[1,3840]{1,0:T(1,128)} %get-tuple-element.33), channel_id=1, source_target_pairs={{0,1},{1,2},{2,3},{3,4},{4,5},{5,6},{6,7},{8,9},{9,10},{10,11},{11... | collective-permute-start | bytes 46088 | tf_op jit(solution)/shard_map/ppermute | solution.py:562
  62.9 16.7 %collective-permute-start.3 = (f32[1,3840]{1,0:T(1,128)}, f32[1,3840]{1,0:T(1,128)S(1)}, u32[]{:S(2)}, u32[]{:S(2)}) collective-permute-start(f32[1,3840]{1,0:T(1,128)} %get-tuple-element.34), channel_id=1, source_target_pairs={{1,0},{2,1},{3,2},{4,3},{5,4},{6,5},{7,6},{9,8},{10,9},{11,10},{12... | collective-permute-start | bytes 46088 | tf_op jit(solution)/shard_map/ppermute | solution.py:563
  71.6 10.0 %collective-permute-start.4 = (f32[1,128]{1,0:T(1,128)S(1)}, f32[1,128]{1,0:T(1,128)S(1)}, u32[]{:S(2)}, u32[]{:S(2)}) collective-permute-start(f32[1,128]{1,0:T(1,128)S(1)} %get-tuple-element.39), channel_id=1, source_target_pairs={{0,8},{8,16},{16,24},{24,32},{32,40},{40,48},{48,56},{56,64},{64,7... | collective-permute-start | bytes 1544 | tf_op jit(solution)/shard_map/ppermute | solution.py:562
  74.3 7.4 %collective-permute-start.5 = (f32[1,128]{1,0:T(1,128)S(1)}, f32[1,128]{1,0:T(1,128)S(1)}, u32[]{:S(2)}, u32[]{:S(2)}) collective-permute-start(f32[1,128]{1,0:T(1,128)S(1)} %get-tuple-element.40), channel_id=1, source_target_pairs={{8,0},{16,8},{24,16},{32,24},{40,32},{48,40},{56,48},{64,56},{72,6... | collective-permute-start | bytes 1544 | tf_op jit(solution)/shard_map/ppermute | solution.py:563
  79.7 0.7 copy-start.6
  80.4 1.3 %copy-start.9 = (f32[80,128]{1,0:T(8,128)S(1)}, f32[80,128]{1,0:T(8,128)}, u32[]{:S(2)}) copy-start(f32[80,128]{1,0:T(8,128)} %constant.41.clone.prof_ref) | copy-start | bytes 122884

commit v3 on v2

--- a/solution.py
+++ b/solution.py
@@ -73,7 +73,13 @@
     return low, high, rims
 
 
-def table_kernel(list_ref, surf_ref, tile_ref, choice_ref):
+def table_kernel(list_ref, air_ref, tile_ref, choice_ref, where_ref, surf_ref, sem):
+    copies = [
+        pltpu.make_async_copy(air_ref.at[LEV * comp], surf_ref.at[comp], sem.at[comp])
+        for comp in range(2)
+    ]
+    for copy in copies:
+        copy.start()
     gx, gy = lax.axis_index("gx"), lax.axis_index("gy")
     me = gx * N_GY + gy
     left, right = gy > 0, gy < N_GY - 1
@@ -91,7 +97,12 @@
         entry = jnp.broadcast_to(listed[:, slot : slot + 1], (64, 128))
         choice = jnp.where(entry == codes, 1.0, choice)
     choice_ref[...] = choice.astype(BF16)
+    device = sublanes_of(64).astype(F32) + 1.0
+    holder = jnp.sum(choice * device, axis=0, keepdims=True) - 1.0
+    where_ref[...] = holder.astype(jnp.int32)
     tile_ref[...] = jnp.zeros(tile_ref.shape, F32)
+    for copy in copies:
+        copy.wait()
     none = jnp.zeros((8, 128), F32)
     for comp in range(2):
         lanes = slice(128 * comp, 128 * comp + 128)
@@ -256,11 +267,11 @@
         edge = field[block(0), :] - pltpu.roll(field[block(15), :], 1, 0)
         edge = jnp.where(row8 == 0, 0.0, edge)
         last = pltpu.roll(edge, 7, 0)
-        for first in range(0, 16, 8):
-            blocks = range(first, first + 8)
-            fields = [field[block(j), :] for j in range(first, min(first + 9, 16))]
+        for first in range(0, 16, 4):
+            blocks = range(first, first + 4)
+            fields = [field[block(j), :] for j in range(first, min(first + 4 + 1, 16))]
             aheads = [y - x for x, y in zip(fields, fields[1:])]
-            if first == 8:
+            if first == 16 - 4:
                 aheads.append(last)
             backs = [edge] + aheads[:-1]
             edge = aheads[-1]
@@ -297,7 +308,7 @@
                 done_ref[slot, pl.ds(first + k, 8, stride=16), :] = value
             burning = [jnp.exp(value) for value in values]
             burning = [1.0 / (1.0 + value) for value in burning]
-            packed = [word[block(first + k), :] for k in range(8)]
+            packed = [word[block(first + k), :] for k in range(len(values))]
             heats = [((x >> 5) & 63).astype(F32) * y for x, y in zip(packed, burning)]
             smokes = [(x >> 11).astype(F32) * y for x, y in zip(packed, burning)]
             for total, terms in zip(sums, (heats, smokes)):
@@ -307,8 +318,8 @@
 
         advance(side, side[6:9], keep)
         result(slot).start()
-        sums_ref[slot, :, 0:128] = sums[0][0] + sums[0][1]
-        sums_ref[slot, :, 128:256] = sums[1][0] + sums[1][1]
+        sums_ref[slot, :, 0:128] = sum(sums[0])
+        sums_ref[slot, :, 128:256] = sum(sums[1])
 
     def into(target):
         return lambda first, values: store(target, first, values)
@@ -381,7 +392,7 @@
     zero = jnp.zeros((8, 128), F32)
 
     def tile(at, lanes):
-        fire = where_ref[at]
+        fire = where_ref[0, at]
         line = flux_ref[jnp.maximum(fire, 0), :, lanes]
         return jnp.where(fire >= 0, jnp.broadcast_to(line, (8, 128)), 0.0)
 
@@ -393,11 +404,11 @@
         rows = slice(8 * half, 8 * half + 8)
         heat = smoke = zero
         for col in range(16):
-            value = tile(16 * half + col, own)
+            value = tile(16 * half + (col ^ 7), own)
             heat = jnp.where(key == col, find(value, heat_from), heat)
             smoke = jnp.where(key == col, find(value, heat_from + 8), smoke)
-        rim_left = find(tile(32 + half, beside), heat_from)
-        rim_right = find(tile(34 + half, beside), heat_from)
+        rim_left = find(tile(41 + 8 * half, beside), heat_from)
+        rim_right = find(tile(40 + 8 * half, beside), heat_from)
         left = pltpu.roll(jnp.where(lane == 127, rim_left, heat), 1, 1)
         right = pltpu.roll(jnp.where(lane == 0, rim_right, heat), 127, 1)
         heat_ref[rows, :] = heat
@@ -409,12 +420,10 @@
             last_ref[...] = heat[7:8]
 
 
-def rows_kernel(air_ref, first_ref, last_ref, surf_ref, sem):
+def rows_kernel(air_ref, first_ref, last_ref, sem):
     copies = (
         pltpu.make_async_copy(air_ref.at[:, 0, :], first_ref, sem.at[0]),
         pltpu.make_async_copy(air_ref.at[:, 15, :], last_ref, sem.at[1]),
-        pltpu.make_async_copy(air_ref.at[0], surf_ref.at[0], sem.at[2]),
-        pltpu.make_async_copy(air_ref.at[LEV], surf_ref.at[1], sem.at[3]),
     )
     for copy in copies:
         copy.start()
@@ -425,26 +434,35 @@
 def sides_kernel(air_ref, left_ref, right_ref):
     lane, sub = lanes_of(), sublanes_of()
     pick = jnp.where((lane == 127 * sub) & (sub < 2), 1.0, 0.0)
-    picked = lax.dot_general(
-        pick, air_ref[...].reshape(3 * LEV * 16, 128), (((1,), (1,)), ((), ())),
-        precision=lax.Precision.HIGHEST, preferred_element_type=F32,
-    )
+    columns = air_ref[...].reshape(3 * LEV * 16, 128)
+    picked = 0.0
+    for part in halves(columns):
+        picked += lax.dot_general(
+            pick.astype(BF16), part.astype(BF16), (((1,), (1,)), ((), ())),
+            preferred_element_type=F32,
+        )
     left_ref[...] = picked[0:1]
     right_ref[...] = picked[1:2]
 
 
-def air_kernel(air_ref, above_ref, below_ref, token_in, out_ref, token_ref):
+def air_kernel(
+    air_ref, above_ref, below_ref, left_ref, right_ref, token_in, out_ref, token_ref
+):
     token_ref[...] = token_in[...]
+    for side, ref in enumerate((left_ref, right_ref)):
+        for at in range(30):
+            level, line = 3 * LEV + 2 * side + at // 16, at % 16
+            out_ref[level, line : line + 1, :] = ref[:, 128 * at : 128 * at + 128]
     lane = lax.broadcasted_iota(jnp.int32, (8, 16, 128), 2)
     row = lax.broadcasted_iota(jnp.int32, (8, 16, 128), 1)
 
     def chunk(at, carry):
-        levels = pl.ds(8 * at, 8)
         fields = []
         for part in range(3):
-            mid = air_ref[part, levels]
-            above = above_ref[part, levels, :][:, None, :]
-            below = below_ref[part, levels, :][:, None, :]
+            start = part * LEV + at * 8
+            mid = air_ref[pl.ds(start, 8)]
+            above = above_ref[pl.ds(start, 8), :][:, None, :]
+            below = below_ref[pl.ds(start, 8), :][:, None, :]
             up = jnp.where(row == 0, above, pltpu.roll(mid, 1, 1))
             down = jnp.where(row == 15, below, pltpu.roll(mid, 15, 1))
             left = jnp.where(lane == 0, 0.0, pltpu.roll(mid, 1, 2))
@@ -453,7 +471,7 @@
         for part in range(2):
             mid, up, down, left, right = fields[part]
             around = (up + down) + (left + right)
-            out_ref[part, levels] = mid + viscosity * (around - 4.0 * mid)
+            out_ref[pl.ds(part * LEV + at * 8, 8)] = mid + viscosity * (around - 4.0 * mid)
         u, v = fields[0][0], fields[1][0]
         mid, up, down, left, right = fields[2]
         upwind = (
@@ -462,13 +480,13 @@
             + jnp.maximum(v, 0.0) * (mid - left)
             + jnp.minimum(v, 0.0) * (right - mid)
         )
-        out_ref[2, levels] = mid - courant * upwind
+        out_ref[pl.ds(2 * LEV + at * 8, 8)] = mid - courant * upwind
         return carry
 
-    lax.fori_loop(0, 2, chunk, 0)
-
-
-def rims_kernel(part_ref, left_ref, right_ref, own_left_ref, own_right_ref, out_ref):
+    lax.fori_loop(0, LEV // 8, chunk, 0)
+
+
+def rims_kernel(part_ref, left_ref, right_ref, out_ref):
     sub, lane = sublanes_of(), lanes_of()
     expand = jnp.where((sub < 2) & (lane == 0), 1.0, 0.0) + jnp.where(
         (sub >= 2) & (sub < 4) & (lane == 127), 1.0, 0.0
@@ -482,9 +500,10 @@
             if part < 2:
                 left, right = viscosity * left, viscosity * right
             else:
-                wind = pl.ds(pl.multiple_of(LEV * 16 + at * 128, 128), 128)
-                left = courant * jnp.maximum(own_left_ref[:, wind], 0.0) * left
-                right = -courant * jnp.minimum(own_right_ref[:, wind], 0.0) * right
+                line = LEV // 8 + at
+                level, line = 3 * LEV + (line >> 4), pl.ds(line & 15, 1)
+                left = courant * jnp.maximum(part_ref[level, line, :], 0.0) * left
+                right = -courant * jnp.minimum(part_ref[level + 2, line, :], 0.0) * right
             left_high, left_low = halves(left)
             right_high, right_low = halves(right)
             rims = jnp.where(sub == 0, left_high, 0.0)
@@ -567,41 +586,29 @@
 def on_device(air, level_set, fuel, tile_list):
     wcol, spread, words, profile = constants()
     rows = ("grp", "gx")
-    my_gx, my_gy = lax.axis_index("gx"), lax.axis_index("gy")
-    myself = my_gx * N_GY + my_gy
     levels = air.reshape(3 * LEV, 16, 128)
 
-    first, last, surface = pl.pallas_call(
+    first, last = pl.pallas_call(
         rows_kernel,
-        out_shape=(shape(3 * LEV, 128), shape(3 * LEV, 128), shape(2, 16, 128)),
-        in_specs=[HBM], out_specs=(VMEM,) * 3, scratch_shapes=[pltpu.SemaphoreType.DMA((4,))],
+        out_shape=(shape(3 * LEV, 128), shape(3 * LEV, 128)),
+        in_specs=[HBM], out_specs=(VMEM,) * 2, scratch_shapes=[pltpu.SemaphoreType.DMA((2,))],
         compiler_params=room(60), name="rows", cost_estimate=cost(10**5, 10**6),
     )(levels)
     air_above, air_below = neighbours(last, first, rows, N_GRP * N_GX)
-
-    listed = tile_list[0]
-    beside = jnp.array([15, 31], jnp.int32)
-    wanted = jnp.concatenate(
-        [
-            myself * 32 + jnp.arange(32, dtype=jnp.int32),
-            jnp.where(my_gy > 0, (myself - 1) * 32 + beside, -2),
-            jnp.where(my_gy < N_GY - 1, (myself + 1) * 32 + beside - 15, -2),
-        ]
-    )
-    found = listed[None, :, :] == wanted[:, None, None]
-    order = lax.broadcasted_iota(jnp.int32, found.shape, 1)
-    where = jnp.max(jnp.where(found, order, -1), axis=(1, 2))
 
     left, right = pl.pallas_call(
         sides_kernel, out_shape=(shape(1, 3 * LEV * 16), shape(1, 3 * LEV * 16)),
         in_specs=[VMEM], out_specs=(VMEM,) * 2, compiler_params=room(4),
         name="sides", cost_estimate=cost(10**8, 2 * 10**6),
     )(levels)
-    table, choice = pl.pallas_call(
-        table_kernel, out_shape=(shape(128, 256), shape(64, 128, dtype=BF16)),
-        in_specs=[VMEM, VMEM], out_specs=(VMEM, VMEM),
+    table, choice, where = pl.pallas_call(
+        table_kernel, out_shape=(
+            shape(128, 256), shape(64, 128, dtype=BF16), shape(1, 128, dtype=jnp.int32)
+        ),
+        in_specs=[VMEM, HBM], out_specs=(VMEM,) * 3,
+        scratch_shapes=[pltpu.VMEM((2, 16, 128), F32), pltpu.SemaphoreType.DMA((2,))],
         compiler_params=room(2), name="table", cost_estimate=cost(10**6, 10**6),
-    )(tile_list, surface)
+    )(tile_list, levels)
     windows, token = pl.pallas_call(
         windows_kernel,
         out_shape=(shape(N_GX * N_GY, 1, 256), shape(8, 128)),
@@ -610,15 +617,11 @@
         compiler_params=room(2), name="windows", cost_estimate=cost(10**6, 10**6),
     )(table, choice, air_above, air_below, left)
     windows = lax.all_to_all(windows, ("gx", "gy"), split_axis=0, concat_axis=0, tiled=True)
-    per_block = pl.BlockSpec((3, 16, 16, 128), lambda i: (0, i, 0, 0))
-    per_rows = pl.BlockSpec((3, 16, 128), lambda i: (0, i, 0))
-    fixed = pl.BlockSpec((8, 128), lambda i: (0, 0))
     moved, token = pl.pallas_call(
-        air_kernel, out_shape=(shape(3, LEV, 16, 128), shape(8, 128)), grid=(LEV // 16,),
-        in_specs=[per_block, per_rows, per_rows, fixed], out_specs=(per_block, fixed),
-        compiler_params=room(60), name="air", cost_estimate=cost(2 * 10**8, 4 * 10**6),
-    )(air, air_above.reshape(3, LEV, 128), air_below.reshape(3, LEV, 128), token)
-    moved = moved.reshape(3 * LEV, 16, 128)
+        air_kernel, out_shape=(shape(3 * LEV + 4, 16, 128), shape(8, 128)),
+        in_specs=[VMEM] * 6, out_specs=(VMEM, VMEM),
+        compiler_params=room(8), name="air", cost_estimate=cost(2 * 10**8, 4 * 10**6),
+    )(levels, air_above, air_below, left, right, token)
 
     phases, message, edge_left, edge_right = pl.pallas_call(
         fire_kernel,
@@ -650,9 +653,9 @@
     fluxes = lax.all_to_all(message, ("gx", "gy"), split_axis=0, concat_axis=0, tiled=True)
     air_left, air_right = neighbours(edge_right, edge_left, "gy", N_GY)
     rimmed = pl.pallas_call(
-        rims_kernel, out_shape=shape(3 * LEV, 16, 128), in_specs=[VMEM] * 5, out_specs=VMEM,
+        rims_kernel, out_shape=shape(3 * LEV, 16, 128), in_specs=[VMEM] * 3, out_specs=VMEM,
         compiler_params=room(8), name="rims", cost_estimate=cost(2 * 10**8, 4 * 10**6),
-    )(moved, air_left, air_right, left, right)
+    )(moved, air_left, air_right)
     heat, side, smoke, heat_first, heat_last = pl.pallas_call(
         place_kernel,
         out_shape=(shape(16, 128), shape(16, 128), shape(16, 128), shape(1, 128), shape(1, 128)),

time: 83.7 us -> 80.8 us (0.965)
  Pallas kernels: 32 us -> 26.9 us
  waiting for transfers between devices: 10.7 us -> 13.7 us
  other arithmetic: 0.9 us -> 0 us
    pallas_call x1, Pallas kernels: 5.23 us -> 1.87 us  [on_device(): pl.pallas_call(air_kernel, out_shape=(shape(3 * LEV + 4, 16, 128), shape(...]
    all_to_all x1, waiting for transfers between devices: 4.76 us -> 6.26 us  [on_device(): lax.all_to_all(windows, ('gx', 'gy'), split_axis=0, concat_axis=0, tiled=...]
    pallas_call x1, Pallas kernels: 1.67 us -> 0.61 us  [on_device(): pl.pallas_call(sides_kernel, out_shape=(shape(1, 3 * LEV * 16), shape(1,...]
    all_to_all x1, starting transfers between devices: 5.55 us -> 4.62 us  [on_device(): lax.all_to_all(message, ('gx', 'gy'), split_axis=0, concat_axis=0, tiled=...]
    all_to_all x1, waiting for transfers between devices: 5.88 us -> 6.8 us  [on_device(): lax.all_to_all(message, ('gx', 'gy'), split_axis=0, concat_axis=0, tiled=...]
    pallas_call x1, Pallas kernels: 1.62 us -> 0.75 us  [on_device(): pl.pallas_call(table_kernel, out_shape=(shape(128, 256), shape(64, 128, d...]
    unnamed x31 -> x19, local copies, waits for them, and re-layouts: 2.66 us -> 3.33 us
  transfers between devices with their start and end apart: 8 -> 8, of which waited for: 2 -> 3; matrix products, arithmetic and copies ran while one was open for 1% -> 1% of each run, Pallas kernels for 13% -> 7%
where the time goes in v3:
time: 80.8 us; the launch traced here: 80.4 us
  starting transfers between devices  35.6 us (44%)
  Pallas kernels  26.9 us (33%)
  waiting for transfers between devices  13.7 us (17%)
  local copies, waits for them, and re-layouts  3.33 us (4%)
  between operations  0.85 us (1%)
    pallas_call x1, Pallas kernels, on_device(): pl.pallas_call(fire_kernel, out_shape=(shape(32, 128, 128), shape(N_GX *...  17.5 us
    ppermute x3, starting transfers between devices, neighbours(): after = lax.ppermute(first, axes, [(i + 1, i) for i in range(ends)])  12.4 us
    all_to_all x1, starting transfers between devices, on_device(): lax.all_to_all(windows, ('gx', 'gy'), split_axis=0, concat_axis=0, tiled=...  10.2 us
    ppermute x3, starting transfers between devices, neighbours(): before = lax.ppermute(last, axes, [(i, i + 1) for i in range(ends)])  8.36 us
    all_to_all x1, waiting for transfers between devices, on_device(): lax.all_to_all(message, ('gx', 'gy'), split_axis=0, concat_axis=0, tiled=...  6.8 us
    all_to_all x1, waiting for transfers between devices, on_device(): lax.all_to_all(windows, ('gx', 'gy'), split_axis=0, concat_axis=0, tiled=...  6.26 us
    all_to_all x1, starting transfers between devices, on_device(): lax.all_to_all(message, ('gx', 'gy'), split_axis=0, concat_axis=0, tiled=...  4.62 us
    unnamed x19, local copies, waits for them, and re-layouts  3.33 us
  transfers between devices with their start and end apart: 8, of which 3 were waited for; matrix products, arithmetic and copies ran while one was open for 1% of the time, Pallas kernels for 7%

profile of v3, /device:TPU:2, one launch (start us, length us, event | category | flops | bytes accessed | tf_op | source)
XLA Modules:
  0.0 80.4 jit_solution(14218460222323472010)
XLA Ops:
  0.6 0.0 copy-start
  0.6 1.8 %rows.1 = (f32[240,128]{1,0:T(8,128)}, f32[240,128]{1,0:T(8,128)}) custom-call(f32[240,16,128]{2,1,0:T(8,128)} %bitcast.2), custom_call_target="tpu_custom_call" | custom-call | flops 100000 | bytes 1000000 | tf_op jit(solution)/shard_map/rows/pallas_call | solution.py:591
  2.5 3.8 %collective-permute-start = (f32[240,128]{1,0:T(8,128)}, f32[240,128]{1,0:T(8,128)S(1)}, u32[]{:S(2)}, u32[]{:S(2)}) collective-permute-start(f32[240,128]{1,0:T(8,128)} %get-tuple-element.22), channel_id=1, source_target_pairs={{0,8},{8,16},{16,24},{24,32},{32,40},{40,48},{48,56},{56,64},{64,7... | collective-permute-start | bytes 368648 | tf_op jit(solution)/shard_map/ppermute | solution.py:581
  6.3 5.8 %collective-permute-start.1 = (f32[240,128]{1,0:T(8,128)}, f32[240,128]{1,0:T(8,128)S(1)}, u32[]{:S(2)}, u32[]{:S(2)}) collective-permute-start(f32[240,128]{1,0:T(8,128)} %get-tuple-element.23), channel_id=1, source_target_pairs={{8,0},{16,8},{24,16},{32,24},{40,32},{48,40},{56,48},{64,56},{72,6... | collective-permute-start | bytes 368648 | tf_op jit(solution)/shard_map/ppermute | solution.py:582
  12.1 0.8 copy.10.list_ref
  12.9 0.0 copy-done
  12.9 0.0 copy-start.3
  13.0 0.8 table.1
  13.7 0.6 sides.1
  14.3 0.0 copy-start.4
  14.3 0.0 copy-start.5
  14.4 0.0 collective-permute-done.above_ref
  14.4 0.6 collective-permute-done.1.below_ref
  15.0 1.0 %windows.1 = (f32[64,1,256]{2,1,0:T(1,128)}, f32[8,128]{1,0:T(8,128)S(1)}) custom-call(f32[128,256]{1,0:T(8,128)S(1)} %get-tuple-element.26.table_ref, bf16[64,128]{1,0:T(8,128)(2,1)S(1)} %get-tuple-element.27.choice_ref, f32[240,128]{1,0:T(8,128)S(1)} %collective-permute-done.above_ref, f32[240,128]{1,0:T(8,128)S(1)} %collective-permute-done.1.below_ref, ...), custom_call_target="tpu_custom_call" | custom-call | flops 1000000 | bytes 1000000 | tf_op jit(solution)/shard_map/windows/pallas_call | solution.py:612
  16.0 0.0 copy-done.3
  16.0 10.2 %all-to-all-start = ((f32[64,1,256]{2,1,0:T(1,128)}), f32[64,1,256]{2,1,0:T(1,128)S(1)}, u32[]{:S(2)}, u32[]{:S(2)}) async-start(f32[64,1,256]{2,1,0:T(1,128)} %get-tuple-element.30), calls=%async_computation | async-start | bytes 131072 | tf_op jit(solution)/shard_map/all_to_all | solution.py:619
  26.2 1.9 %air.1 = (f32[244,16,128]{2,1,0:T(8,128)S(1)}, f32[8,128]{1,0:T(8,128)S(1)}) custom-call(f32[240,16,128]{2,1,0:T(8,128)S(1)} %bitcast.5, f32[240,128]{1,0:T(8,128)S(1)} %collective-permute-done.above_ref, f32[240,128]{1,0:T(8,128)S(1)} %collective-permute-done.1.below_ref, f32[1,3840]{1,0:T(1,128)S(1)} %get-tuple-element.24.left_ref.left_in, ...), custom_call_target="tpu_custom_call" | custom-call | flops 200000000 | bytes 4000000 | tf_op jit(solution)/shard_map/air/pallas_call | solution.py:620
  28.1 0.0 copy-start.1
  28.1 1.3 %copy-done.1 = f32[244,16,128]{2,1,0:T(8,128)} copy-done((f32[244,16,128]{2,1,0:T(8,128)}, f32[244,16,128]{2,1,0:T(8,128)S(1)}, u32[]{:S(2)}) %copy-start.1) | copy-done | bytes 1998872
  29.4 0.0 copy-start.7
  29.4 0.6 copy-done.7
  30.0 6.3 %all-to-all-done.recv_ref = f32[64,1,256]{2,1,0:T(1,128)S(1)} async-done(((f32[64,1,256]{2,1,0:T(1,128)}), f32[64,1,256]{2,1,0:T(1,128)S(1)}, u32[]{:S(2)}, u32[]{:S(2)}) %all-to-all-start) | async-done | bytes 65568 | tf_op jit(solution)/shard_map/all_to_all | solution.py:619
  36.2 0.0 copy-start.8
  36.2 0.0 copy-done.4
  36.2 0.0 copy-done.5
  36.3 0.6 copy-done.8
  36.9 0.0 copy-start.2
  36.9 17.5 %fire.1 = (f32[32,128,128]{2,1,0:T(8,128)}, f32[64,1,256]{2,1,0:T(1,128)}, f32[1,3840]{1,0:T(1,128)}, f32[1,3840]{1,0:T(1,128)}) custom-call(s32[1,64,32]{2,1,0:T(8,128)} %copy-done.3, f32[32,128,128]{2,1,0:T(8,128)} %phase_in.1, s32[32,128,128]{2,1,0:T(8,128)} %fuel_in.1, f32[64,1,256]{2,1,0:T(1,128)} %copy-done.8, s32[8,128]{1,0:T(8,128)} %constant.8.clone.words_ref, ...), custom_call_target="tpu_custom_call" | custom-call | flops 1000000000 | bytes 8000000 | tf_op jit(solution)/shard_map/fire/pallas_call | solution.py:626
  54.3 4.6 %all-to-all-start.1 = ((f32[64,1,256]{2,1,0:T(1,128)}), f32[64,1,256]{2,1,0:T(1,128)S(1)}, u32[]{:S(2)}, u32[]{:S(2)}) async-start(f32[64,1,256]{2,1,0:T(1,128)} %get-tuple-element.35), calls=%async_computation.1 | async-start | bytes 131072 | tf_op jit(solution)/shard_map/all_to_all | solution.py:653
  59.0 1.8 %collective-permute-start.2 = (f32[1,3840]{1,0:T(1,128)}, f32[1,3840]{1,0:T(1,128)S(1)}, u32[]{:S(2)}, u32[]{:S(2)}) collective-permute-start(f32[1,3840]{1,0:T(1,128)} %get-tuple-element.32), channel_id=1, source_target_pairs={{0,1},{1,2},{2,3},{3,4},{4,5},{5,6},{6,7},{8,9},{9,10},{10,11},{11... | collective-permute-start | bytes 46088 | tf_op jit(solution)/shard_map/ppermute | solution.py:581
  60.8 1.3 %collective-permute-start.3 = (f32[1,3840]{1,0:T(1,128)}, f32[1,3840]{1,0:T(1,128)S(1)}, u32[]{:S(2)}, u32[]{:S(2)}) collective-permute-start(f32[1,3840]{1,0:T(1,128)} %get-tuple-element.33), channel_id=1, source_target_pairs={{1,0},{2,1},{3,2},{4,3},{5,4},{6,5},{7,6},{9,8},{10,9},{11,10},{12... | collective-permute-start | bytes 46088 | tf_op jit(solution)/shard_map/ppermute | solution.py:582
  62.1 6.8 %all-to-all-done.1.flux_ref = f32[64,1,256]{2,1,0:T(1,128)S(1)} async-done(((f32[64,1,256]{2,1,0:T(1,128)}), f32[64,1,256]{2,1,0:T(1,128)S(1)}, u32[]{:S(2)}, u32[]{:S(2)}) %all-to-all-start.1) | async-done | bytes 65568 | tf_op jit(solution)/shard_map/all_to_all | solution.py:653
  68.9 0.7 place.1
  69.7 2.7 %collective-permute-start.4 = (f32[1,128]{1,0:T(1,128)S(1)}, f32[1,128]{1,0:T(1,128)S(1)}, u32[]{:S(2)}, u32[]{:S(2)}) collective-permute-start(f32[1,128]{1,0:T(1,128)S(1)} %get-tuple-element.39), channel_id=1, source_target_pairs={{0,8},{8,16},{16,24},{24,32},{32,40},{40,48},{48,56},{56,64},{64,7... | collective-permute-start | bytes 1544 | tf_op jit(solution)/shard_map/ppermute | solution.py:581
  72.4 5.3 %collective-permute-start.5 = (f32[1,128]{1,0:T(1,128)S(1)}, f32[1,128]{1,0:T(1,128)S(1)}, u32[]{:S(2)}, u32[]{:S(2)}) collective-permute-start(f32[1,128]{1,0:T(1,128)S(1)} %get-tuple-element.40), channel_id=1, source_target_pairs={{8,0},{16,8},{24,16},{32,24},{40,32},{48,40},{56,48},{64,56},{72,6... | collective-permute-start | bytes 1544 | tf_op jit(solution)/shard_map/ppermute | solution.py:582
  77.6 0.0 collective-permute-done.2.left_ref
  77.7 0.0 collective-permute-done.3.right_ref
  77.7 0.0 copy-done.2
  77.7 0.0 copy-start.6
  77.7 1.3 %rims.1.part_ref = f32[240,16,128]{2,1,0:T(8,128)S(1)} custom-call(f32[244,16,128]{2,1,0:T(8,128)S(1)} %copy-done.2, f32[1,3840]{1,0:T(1,128)S(1)} %collective-permute-done.2.left_ref, f32[1,3840]{1,0:T(1,128)S(1)} %collective-permute-done.3.right_ref), custom_call_target="tpu_custom_call" | custom-call | flops 200000000 | bytes 4000000 | tf_op jit(solution)/shard_map/rims/pallas_call | solution.py:655
  79.0 0.0 collective-permute-done.4.above_ref
  79.0 0.0 collective-permute-done.5.below_ref
  79.0 0.0 copy-done.6
  79.0 1.4 %final.1 = f32[240,16,128]{2,1,0:T(8,128)} custom-call(f32[240,16,128]{2,1,0:T(8,128)S(1)} %rims.1.part_ref, f32[16,128]{1,0:T(8,128)S(1)} %get-tuple-element.36.heat_ref, f32[16,128]{1,0:T(8,128)S(1)} %get-tuple-element.37.side_ref, f32[16,128]{1,0:T(8,128)S(1)} %get-tuple-element.38.smoke_ref, f32[1,128]{1,0:T(1,128)S(1)} %collective-permute-done.4.above_ref, ...), custom_call_target="tpu_custom_call" | custom-call | flops 1000000 | bytes 4000000 | tf_op jit(solution)/shard_map/final/pallas_call | solution.py:666
Async XLA Ops:
  0.6 12.3 %copy-start = (f32[3,80,16,128]{3,2,1,0:T(8,128)S(1)}, f32[3,80,16,128]{3,2,1,0:T(8,128)}, u32[]{:S(2)}) copy-start(f32[3,80,16,128]{3,2,1,0:T(8,128)} %param.8) | copy-start | bytes 5898244
  2.5 11.9 %collective-permute-start = (f32[240,128]{1,0:T(8,128)}, f32[240,128]{1,0:T(8,128)S(1)}, u32[]{:S(2)}, u32[]{:S(2)}) collective-permute-start(f32[240,128]{1,0:T(8,128)} %get-tuple-element.22), channel_id=1, source_target_pairs={{0,8},{8,16},{16,24},{24,32},{32,40},{40,48},{48,56},{56,64},{64,7... | collective-permute-start | bytes 368648 | tf_op jit(solution)/shard_map/ppermute | solution.py:581
  6.3 8.7 %collective-permute-start.1 = (f32[240,128]{1,0:T(8,128)}, f32[240,128]{1,0:T(8,128)S(1)}, u32[]{:S(2)}, u32[]{:S(2)}) collective-permute-start(f32[240,128]{1,0:T(8,128)} %get-tuple-element.23), channel_id=1, source_target_pairs={{8,0},{16,8},{24,16},{32,24},{40,32},{48,40},{56,48},{64,56},{72,6... | collective-permute-start | bytes 368648 | tf_op jit(solution)/shard_map/ppermute | solution.py:582
  12.9 3.0 %copy-start.3 = (s32[1,64,32]{2,1,0:T(8,128)}, s32[1,64,32]{2,1,0:T(8,128)S(1)}, u32[]{:S(2)}) copy-start(s32[1,64,32]{2,1,0:T(8,128)S(1)} %copy.10.list_ref) | copy-start | bytes 24580
  14.3 21.9 %copy-start.4 = (f32[1,3840]{1,0:T(1,128)}, f32[1,3840]{1,0:T(1,128)S(1)}, u32[]{:S(2)}) copy-start(f32[1,3840]{1,0:T(1,128)S(1)} %get-tuple-element.24.left_ref.left_in) | copy-start | bytes 46084
  14.3 21.9 %copy-start.5 = (f32[1,3840]{1,0:T(1,128)}, f32[1,3840]{1,0:T(1,128)S(1)}, u32[]{:S(2)}) copy-start(f32[1,3840]{1,0:T(1,128)S(1)} %get-tuple-element.25.right_ref.right_in) | copy-start | bytes 46084
  16.0 20.3 %all-to-all-start = ((f32[64,1,256]{2,1,0:T(1,128)}), f32[64,1,256]{2,1,0:T(1,128)S(1)}, u32[]{:S(2)}, u32[]{:S(2)}) async-start(f32[64,1,256]{2,1,0:T(1,128)} %get-tuple-element.30), calls=%async_computation | async-start | bytes 131072 | tf_op jit(solution)/shard_map/all_to_all | solution.py:619
  28.1 1.3 %copy-start.1 = (f32[244,16,128]{2,1,0:T(8,128)}, f32[244,16,128]{2,1,0:T(8,128)S(1)}, u32[]{:S(2)}) copy-start(f32[244,16,128]{2,1,0:T(8,128)S(1)} %get-tuple-element.29.part_ref) | copy-start | bytes 5996548
  29.4 0.6 copy-start.7
  36.2 0.6 copy-start.8
  36.9 40.8 %copy-start.2 = (f32[244,16,128]{2,1,0:T(8,128)S(1)}, f32[244,16,128]{2,1,0:T(8,128)}, u32[]{:S(2)}) copy-start(f32[244,16,128]{2,1,0:T(8,128)} %copy-done.1) | copy-start | bytes 5996548
  54.3 14.6 %all-to-all-start.1 = ((f32[64,1,256]{2,1,0:T(1,128)}), f32[64,1,256]{2,1,0:T(1,128)S(1)}, u32[]{:S(2)}, u32[]{:S(2)}) async-start(f32[64,1,256]{2,1,0:T(1,128)} %get-tuple-element.35), calls=%async_computation.1 | async-start | bytes 131072 | tf_op jit(solution)/shard_map/all_to_all | solution.py:653
  59.0 18.7 %collective-permute-start.2 = (f32[1,3840]{1,0:T(1,128)}, f32[1,3840]{1,0:T(1,128)S(1)}, u32[]{:S(2)}, u32[]{:S(2)}) collective-permute-start(f32[1,3840]{1,0:T(1,128)} %get-tuple-element.32), channel_id=1, source_target_pairs={{0,1},{1,2},{2,3},{3,4},{4,5},{5,6},{6,7},{8,9},{9,10},{10,11},{11... | collective-permute-start | bytes 46088 | tf_op jit(solution)/shard_map/ppermute | solution.py:581
  60.8 16.8 %collective-permute-start.3 = (f32[1,3840]{1,0:T(1,128)}, f32[1,3840]{1,0:T(1,128)S(1)}, u32[]{:S(2)}, u32[]{:S(2)}) collective-permute-start(f32[1,3840]{1,0:T(1,128)} %get-tuple-element.33), channel_id=1, source_target_pairs={{1,0},{2,1},{3,2},{4,3},{5,4},{6,5},{7,6},{9,8},{10,9},{11,10},{12... | collective-permute-start | bytes 46088 | tf_op jit(solution)/shard_map/ppermute | solution.py:582
  69.7 9.3 %collective-permute-start.4 = (f32[1,128]{1,0:T(1,128)S(1)}, f32[1,128]{1,0:T(1,128)S(1)}, u32[]{:S(2)}, u32[]{:S(2)}) collective-permute-start(f32[1,128]{1,0:T(1,128)S(1)} %get-tuple-element.39), channel_id=1, source_target_pairs={{0,8},{8,16},{16,24},{24,32},{32,40},{40,48},{48,56},{56,64},{64,7... | collective-permute-start | bytes 1544 | tf_op jit(solution)/shard_map/ppermute | solution.py:581
  72.4 6.6 %collective-permute-start.5 = (f32[1,128]{1,0:T(1,128)S(1)}, f32[1,128]{1,0:T(1,128)S(1)}, u32[]{:S(2)}, u32[]{:S(2)}) collective-permute-start(f32[1,128]{1,0:T(1,128)S(1)} %get-tuple-element.40), channel_id=1, source_target_pairs={{8,0},{16,8},{24,16},{32,24},{40,32},{48,40},{56,48},{64,56},{72,6... | collective-permute-start | bytes 1544 | tf_op jit(solution)/shard_map/ppermute | solution.py:582
  77.7 1.3 %copy-start.6 = (f32[80,128]{1,0:T(8,128)S(1)}, f32[80,128]{1,0:T(8,128)}, u32[]{:S(2)}) copy-start(f32[80,128]{1,0:T(8,128)} %constant.11.clone.prof_ref) | copy-start | bytes 122884

commit v4 on v3

--- a/solution.py
+++ b/solution.py
@@ -146,14 +146,17 @@
 
 
 def fire_kernel(
-    list_ref, phase_in, fuel_in, recv_ref, words_ref, wcol_ref, spread_ref,
+    list_ref, phase_in, fuel_in, recv_in, words_ref, wcol_ref, spread_ref,
     left_in, right_in, token_in, out_ref, msg_ref, left_out, right_out,
-    phase_ref, fuel_ref, done_ref, column_ref, sums_ref, means_ref, flat_ref, line_ref, *rest,
+    recv_ref, phase_ref, fuel_ref, done_ref, column_ref, sums_ref, means_ref, flat_ref, line_ref,
+    *rest,
 ):
     buffers, sem, sem_in = rest[:-2], rest[-2], rest[-1]
     sides = [buffers[at::WIDE] for at in range(WIDE)]
     left_out[...] = left_in[...]
     right_out[...] = right_in[...]
+    arrival = pltpu.make_async_copy(recv_in, recv_ref, sem_in.at[6])
+    arrival.start()
     loads = []
     for at, (low, high) in enumerate(((0, 2), (2, 8), (8, 32))):
         some = pl.ds(low, high - low)
@@ -188,6 +191,7 @@
     from_right = from_right & (target >= 128) & (target < 192)
     taken = ((owner == target) & (target < 64)) | from_left | from_right
     taken = jnp.where(taken & (tiles >= 0), 1.0, 0.0).astype(BF16)
+    arrival.wait()
     for device in range(N_GX * N_GY):
         flat_ref[device : device + 1, :] = recv_ref[device]
     sent = flat_ref[...]
@@ -307,7 +311,9 @@
             for k, value in enumerate(values):
                 done_ref[slot, pl.ds(first + k, 8, stride=16), :] = value
             burning = [jnp.exp(value) for value in values]
-            burning = [1.0 / (1.0 + value) for value in burning]
+            burning = [1.0 + value for value in burning]
+            guesses = [pl.reciprocal(value, approx=True) for value in burning]
+            burning = [y * (2.0 - x * y) for x, y in zip(burning, guesses)]
             packed = [word[block(first + k), :] for k in range(len(values))]
             heats = [((x >> 5) & 63).astype(F32) * y for x, y in zip(packed, burning)]
             smokes = [(x >> 11).astype(F32) * y for x, y in zip(packed, burning)]
@@ -629,8 +635,9 @@
             shape(32, 128, 128), shape(N_GX * N_GY, 1, 256),
             shape(1, 3 * LEV * 16), shape(1, 3 * LEV * 16),
         ),
-        in_specs=[VMEM, HBM, HBM] + [VMEM] * 7, out_specs=(HBM, VMEM, VMEM, VMEM),
+        in_specs=[VMEM, HBM, HBM, HBM] + [VMEM] * 6, out_specs=(HBM, VMEM, VMEM, VMEM),
         scratch_shapes=[
+            pltpu.VMEM((N_GX * N_GY, 1, 256), F32),
             pltpu.VMEM((32, 128, 128), F32),
             pltpu.VMEM((32, 128, 128), jnp.int32),
             pltpu.VMEM((32, 128, 128), F32),
@@ -644,7 +651,7 @@
         + [pltpu.VMEM((128, 128), F32)] * WIDE
         + [pltpu.VMEM((128, 128), jnp.int32)] * WIDE
         + [pltpu.VMEM((128, 128), F32)] * (6 * WIDE)
-        + [pltpu.SemaphoreType.DMA((32,)), pltpu.SemaphoreType.DMA((6,))],
+        + [pltpu.SemaphoreType.DMA((32,)), pltpu.SemaphoreType.DMA((7,))],
         compiler_params=room(60), name="fire", cost_estimate=cost(10**9, 8 * 10**6),
     )(
         tile_list, level_set, fuel, windows, jnp.asarray(words), jnp.asarray(wcol, BF16),

time: 80.8 us -> 81.8 us (1.012)
  Pallas kernels: 26.9 us -> 27.9 us
    pallas_call x1, Pallas kernels: 17.5 us -> 18.5 us  [on_device(): pl.pallas_call(fire_kernel, out_shape=(shape(32, 128, 128), shape(N_GX *...]
  transfers between devices with their start and end apart: 8 -> 8, of which waited for: 3 -> 3; matrix products, arithmetic and copies ran while one was open for 1% -> 1% of each run, Pallas kernels for 7% -> 6%
where the time goes in v4:
time: 81.8 us; the launch traced here: 81.4 us
  starting transfers between devices  35.6 us (44%)
  Pallas kernels  27.9 us (34%)
  waiting for transfers between devices  13.7 us (17%)
  local copies, waits for them, and re-layouts  3.33 us (4%)
  between operations  0.85 us (1%)
    pallas_call x1, Pallas kernels, on_device(): pl.pallas_call(fire_kernel, out_shape=(shape(32, 128, 128), shape(N_GX *...  18.5 us
    ppermute x3, starting transfers between devices, neighbours(): after = lax.ppermute(first, axes, [(i + 1, i) for i in range(ends)])  12.4 us
    all_to_all x1, starting transfers between devices, on_device(): lax.all_to_all(windows, ('gx', 'gy'), split_axis=0, concat_axis=0, tiled=...  10.2 us
    ppermute x3, starting transfers between devices, neighbours(): before = lax.ppermute(last, axes, [(i, i + 1) for i in range(ends)])  8.36 us
    all_to_all x1, waiting for transfers between devices, on_device(): lax.all_to_all(message, ('gx', 'gy'), split_axis=0, concat_axis=0, tiled=...  6.8 us
    all_to_all x1, waiting for transfers between devices, on_device(): lax.all_to_all(windows, ('gx', 'gy'), split_axis=0, concat_axis=0, tiled=...  6.26 us
    all_to_all x1, starting transfers between devices, on_device(): lax.all_to_all(message, ('gx', 'gy'), split_axis=0, concat_axis=0, tiled=...  4.62 us
    unnamed x19, local copies, waits for them, and re-layouts  3.33 us
  transfers between devices with their start and end apart: 8, of which 3 were waited for; matrix products, arithmetic and copies ran while one was open for 1% of the time, Pallas kernels for 6%

profile of v4, /device:TPU:2, one launch (start us, length us, event | category | flops | bytes accessed | tf_op | source)
XLA Modules:
  0.0 81.4 jit_solution(4482113027965087)
XLA Ops:
  0.6 0.0 copy-start
  0.6 1.8 %rows.1 = (f32[240,128]{1,0:T(8,128)}, f32[240,128]{1,0:T(8,128)}) custom-call(f32[240,16,128]{2,1,0:T(8,128)} %bitcast.2), custom_call_target="tpu_custom_call" | custom-call | flops 100000 | bytes 1000000 | tf_op jit(solution)/shard_map/rows/pallas_call | solution.py:597
  2.5 3.8 %collective-permute-start = (f32[240,128]{1,0:T(8,128)}, f32[240,128]{1,0:T(8,128)S(1)}, u32[]{:S(2)}, u32[]{:S(2)}) collective-permute-start(f32[240,128]{1,0:T(8,128)} %get-tuple-element.22), channel_id=1, source_target_pairs={{0,8},{8,16},{16,24},{24,32},{32,40},{40,48},{48,56},{56,64},{64,7... | collective-permute-start | bytes 368648 | tf_op jit(solution)/shard_map/ppermute | solution.py:587
  6.3 5.8 %collective-permute-start.1 = (f32[240,128]{1,0:T(8,128)}, f32[240,128]{1,0:T(8,128)S(1)}, u32[]{:S(2)}, u32[]{:S(2)}) collective-permute-start(f32[240,128]{1,0:T(8,128)} %get-tuple-element.23), channel_id=1, source_target_pairs={{8,0},{16,8},{24,16},{32,24},{40,32},{48,40},{56,48},{64,56},{72,6... | collective-permute-start | bytes 368648 | tf_op jit(solution)/shard_map/ppermute | solution.py:588
  12.1 0.8 copy.10.list_ref
  12.9 0.0 copy-done
  12.9 0.0 copy-start.3
  13.0 0.8 table.1
  13.7 0.6 sides.1
  14.3 0.0 copy-start.4
  14.3 0.0 copy-start.5
  14.4 0.0 collective-permute-done.above_ref
  14.4 0.6 collective-permute-done.1.below_ref
  15.0 1.0 %windows.1 = (f32[64,1,256]{2,1,0:T(1,128)}, f32[8,128]{1,0:T(8,128)S(1)}) custom-call(f32[128,256]{1,0:T(8,128)S(1)} %get-tuple-element.26.table_ref, bf16[64,128]{1,0:T(8,128)(2,1)S(1)} %get-tuple-element.27.choice_ref, f32[240,128]{1,0:T(8,128)S(1)} %collective-permute-done.above_ref, f32[240,128]{1,0:T(8,128)S(1)} %collective-permute-done.1.below_ref, ...), custom_call_target="tpu_custom_call" | custom-call | flops 1000000 | bytes 1000000 | tf_op jit(solution)/shard_map/windows/pallas_call | solution.py:618
  16.0 0.0 copy-done.3
  16.0 10.2 %all-to-all-start = ((f32[64,1,256]{2,1,0:T(1,128)}), f32[64,1,256]{2,1,0:T(1,128)S(1)}, u32[]{:S(2)}, u32[]{:S(2)}) async-start(f32[64,1,256]{2,1,0:T(1,128)} %get-tuple-element.30), calls=%async_computation | async-start | bytes 131072 | tf_op jit(solution)/shard_map/all_to_all | solution.py:625
  26.2 1.9 %air.1 = (f32[244,16,128]{2,1,0:T(8,128)S(1)}, f32[8,128]{1,0:T(8,128)S(1)}) custom-call(f32[240,16,128]{2,1,0:T(8,128)S(1)} %bitcast.5, f32[240,128]{1,0:T(8,128)S(1)} %collective-permute-done.above_ref, f32[240,128]{1,0:T(8,128)S(1)} %collective-permute-done.1.below_ref, f32[1,3840]{1,0:T(1,128)S(1)} %get-tuple-element.24.left_ref.left_in, ...), custom_call_target="tpu_custom_call" | custom-call | flops 200000000 | bytes 4000000 | tf_op jit(solution)/shard_map/air/pallas_call | solution.py:626
  28.1 0.0 copy-start.1
  28.1 1.3 %copy-done.1 = f32[244,16,128]{2,1,0:T(8,128)} copy-done((f32[244,16,128]{2,1,0:T(8,128)}, f32[244,16,128]{2,1,0:T(8,128)S(1)}, u32[]{:S(2)}) %copy-start.1) | copy-done | bytes 1998872
  29.4 0.0 copy-start.7
  29.4 0.6 copy-done.7
  30.0 6.3 %all-to-all-done.recv_in = f32[64,1,256]{2,1,0:T(1,128)S(1)} async-done(((f32[64,1,256]{2,1,0:T(1,128)}), f32[64,1,256]{2,1,0:T(1,128)S(1)}, u32[]{:S(2)}, u32[]{:S(2)}) %all-to-all-start) | async-done | bytes 65568 | tf_op jit(solution)/shard_map/all_to_all | solution.py:625
  36.2 0.0 copy-start.8
  36.2 0.0 copy-done.4
  36.2 0.0 copy-done.5
  36.3 0.6 copy-done.8
  36.9 0.0 copy-start.2
  36.9 18.5 %fire.1 = (f32[32,128,128]{2,1,0:T(8,128)}, f32[64,1,256]{2,1,0:T(1,128)}, f32[1,3840]{1,0:T(1,128)}, f32[1,3840]{1,0:T(1,128)}) custom-call(s32[1,64,32]{2,1,0:T(8,128)} %copy-done.3, f32[32,128,128]{2,1,0:T(8,128)} %phase_in.1, s32[32,128,128]{2,1,0:T(8,128)} %fuel_in.1, f32[64,1,256]{2,1,0:T(1,128)} %copy-done.8, s32[8,128]{1,0:T(8,128)} %constant.8.clone.words_ref, ...), custom_call_target="tpu_custom_call" | custom-call | flops 1000000000 | bytes 8000000 | tf_op jit(solution)/shard_map/fire/pallas_call | solution.py:632
  55.3 4.6 %all-to-all-start.1 = ((f32[64,1,256]{2,1,0:T(1,128)}), f32[64,1,256]{2,1,0:T(1,128)S(1)}, u32[]{:S(2)}, u32[]{:S(2)}) async-start(f32[64,1,256]{2,1,0:T(1,128)} %get-tuple-element.35), calls=%async_computation.1 | async-start | bytes 131072 | tf_op jit(solution)/shard_map/all_to_all | solution.py:660
  60.0 1.8 %collective-permute-start.2 = (f32[1,3840]{1,0:T(1,128)}, f32[1,3840]{1,0:T(1,128)S(1)}, u32[]{:S(2)}, u32[]{:S(2)}) collective-permute-start(f32[1,3840]{1,0:T(1,128)} %get-tuple-element.32), channel_id=1, source_target_pairs={{0,1},{1,2},{2,3},{3,4},{4,5},{5,6},{6,7},{8,9},{9,10},{10,11},{11... | collective-permute-start | bytes 46088 | tf_op jit(solution)/shard_map/ppermute | solution.py:587
  61.8 1.3 %collective-permute-start.3 = (f32[1,3840]{1,0:T(1,128)}, f32[1,3840]{1,0:T(1,128)S(1)}, u32[]{:S(2)}, u32[]{:S(2)}) collective-permute-start(f32[1,3840]{1,0:T(1,128)} %get-tuple-element.33), channel_id=1, source_target_pairs={{1,0},{2,1},{3,2},{4,3},{5,4},{6,5},{7,6},{9,8},{10,9},{11,10},{12... | collective-permute-start | bytes 46088 | tf_op jit(solution)/shard_map/ppermute | solution.py:588
  63.1 6.8 %all-to-all-done.1.flux_ref = f32[64,1,256]{2,1,0:T(1,128)S(1)} async-done(((f32[64,1,256]{2,1,0:T(1,128)}), f32[64,1,256]{2,1,0:T(1,128)S(1)}, u32[]{:S(2)}, u32[]{:S(2)}) %all-to-all-start.1) | async-done | bytes 65568 | tf_op jit(solution)/shard_map/all_to_all | solution.py:660
  69.9 0.7 place.1
  70.7 2.7 %collective-permute-start.4 = (f32[1,128]{1,0:T(1,128)S(1)}, f32[1,128]{1,0:T(1,128)S(1)}, u32[]{:S(2)}, u32[]{:S(2)}) collective-permute-start(f32[1,128]{1,0:T(1,128)S(1)} %get-tuple-element.39), channel_id=1, source_target_pairs={{0,8},{8,16},{16,24},{24,32},{32,40},{40,48},{48,56},{56,64},{64,7... | collective-permute-start | bytes 1544 | tf_op jit(solution)/shard_map/ppermute | solution.py:587
  73.4 5.3 %collective-permute-start.5 = (f32[1,128]{1,0:T(1,128)S(1)}, f32[1,128]{1,0:T(1,128)S(1)}, u32[]{:S(2)}, u32[]{:S(2)}) collective-permute-start(f32[1,128]{1,0:T(1,128)S(1)} %get-tuple-element.40), channel_id=1, source_target_pairs={{8,0},{16,8},{24,16},{32,24},{40,32},{48,40},{56,48},{64,56},{72,6... | collective-permute-start | bytes 1544 | tf_op jit(solution)/shard_map/ppermute | solution.py:588
  78.7 0.0 collective-permute-done.2.left_ref
  78.7 0.0 collective-permute-done.3.right_ref
  78.7 0.0 copy-done.2
  78.7 0.0 copy-start.6
  78.7 1.3 %rims.1.part_ref = f32[240,16,128]{2,1,0:T(8,128)S(1)} custom-call(f32[244,16,128]{2,1,0:T(8,128)S(1)} %copy-done.2, f32[1,3840]{1,0:T(1,128)S(1)} %collective-permute-done.2.left_ref, f32[1,3840]{1,0:T(1,128)S(1)} %collective-permute-done.3.right_ref), custom_call_target="tpu_custom_call" | custom-call | flops 200000000 | bytes 4000000 | tf_op jit(solution)/shard_map/rims/pallas_call | solution.py:662
  80.0 0.0 collective-permute-done.4.above_ref
  80.0 0.0 collective-permute-done.5.below_ref
  80.0 0.0 copy-done.6
  80.0 1.4 %final.1 = f32[240,16,128]{2,1,0:T(8,128)} custom-call(f32[240,16,128]{2,1,0:T(8,128)S(1)} %rims.1.part_ref, f32[16,128]{1,0:T(8,128)S(1)} %get-tuple-element.36.heat_ref, f32[16,128]{1,0:T(8,128)S(1)} %get-tuple-element.37.side_ref, f32[16,128]{1,0:T(8,128)S(1)} %get-tuple-element.38.smoke_ref, f32[1,128]{1,0:T(1,128)S(1)} %collective-permute-done.4.above_ref, ...), custom_call_target="tpu_custom_call" | custom-call | flops 1000000 | bytes 4000000 | tf_op jit(solution)/shard_map/final/pallas_call | solution.py:673
Async XLA Ops:
  0.6 12.3 %copy-start = (f32[3,80,16,128]{3,2,1,0:T(8,128)S(1)}, f32[3,80,16,128]{3,2,1,0:T(8,128)}, u32[]{:S(2)}) copy-start(f32[3,80,16,128]{3,2,1,0:T(8,128)} %param.8) | copy-start | bytes 5898244
  2.5 11.9 %collective-permute-start = (f32[240,128]{1,0:T(8,128)}, f32[240,128]{1,0:T(8,128)S(1)}, u32[]{:S(2)}, u32[]{:S(2)}) collective-permute-start(f32[240,128]{1,0:T(8,128)} %get-tuple-element.22), channel_id=1, source_target_pairs={{0,8},{8,16},{16,24},{24,32},{32,40},{40,48},{48,56},{56,64},{64,7... | collective-permute-start | bytes 368648 | tf_op jit(solution)/shard_map/ppermute | solution.py:587
  6.3 8.7 %collective-permute-start.1 = (f32[240,128]{1,0:T(8,128)}, f32[240,128]{1,0:T(8,128)S(1)}, u32[]{:S(2)}, u32[]{:S(2)}) collective-permute-start(f32[240,128]{1,0:T(8,128)} %get-tuple-element.23), channel_id=1, source_target_pairs={{8,0},{16,8},{24,16},{32,24},{40,32},{48,40},{56,48},{64,56},{72,6... | collective-permute-start | bytes 368648 | tf_op jit(solution)/shard_map/ppermute | solution.py:588
  12.9 3.0 %copy-start.3 = (s32[1,64,32]{2,1,0:T(8,128)}, s32[1,64,32]{2,1,0:T(8,128)S(1)}, u32[]{:S(2)}) copy-start(s32[1,64,32]{2,1,0:T(8,128)S(1)} %copy.10.list_ref) | copy-start | bytes 24580
  14.3 21.9 %copy-start.4 = (f32[1,3840]{1,0:T(1,128)}, f32[1,3840]{1,0:T(1,128)S(1)}, u32[]{:S(2)}) copy-start(f32[1,3840]{1,0:T(1,128)S(1)} %get-tuple-element.24.left_ref.left_in) | copy-start | bytes 46084
  14.3 21.9 %copy-start.5 = (f32[1,3840]{1,0:T(1,128)}, f32[1,3840]{1,0:T(1,128)S(1)}, u32[]{:S(2)}) copy-start(f32[1,3840]{1,0:T(1,128)S(1)} %get-tuple-element.25.right_ref.right_in) | copy-start | bytes 46084
  16.0 20.3 %all-to-all-start = ((f32[64,1,256]{2,1,0:T(1,128)}), f32[64,1,256]{2,1,0:T(1,128)S(1)}, u32[]{:S(2)}, u32[]{:S(2)}) async-start(f32[64,1,256]{2,1,0:T(1,128)} %get-tuple-element.30), calls=%async_computation | async-start | bytes 131072 | tf_op jit(solution)/shard_map/all_to_all | solution.py:625
  28.1 1.3 %copy-start.1 = (f32[244,16,128]{2,1,0:T(8,128)}, f32[244,16,128]{2,1,0:T(8,128)S(1)}, u32[]{:S(2)}) copy-start(f32[244,16,128]{2,1,0:T(8,128)S(1)} %get-tuple-element.29.part_ref) | copy-start | bytes 5996548
  29.4 0.6 copy-start.7
  36.2 0.6 copy-start.8
  36.9 41.8 %copy-start.2 = (f32[244,16,128]{2,1,0:T(8,128)S(1)}, f32[244,16,128]{2,1,0:T(8,128)}, u32[]{:S(2)}) copy-start(f32[244,16,128]{2,1,0:T(8,128)} %copy-done.1) | copy-start | bytes 5996548
  55.3 14.6 %all-to-all-start.1 = ((f32[64,1,256]{2,1,0:T(1,128)}), f32[64,1,256]{2,1,0:T(1,128)S(1)}, u32[]{:S(2)}, u32[]{:S(2)}) async-start(f32[64,1,256]{2,1,0:T(1,128)} %get-tuple-element.35), calls=%async_computation.1 | async-start | bytes 131072 | tf_op jit(solution)/shard_map/all_to_all | solution.py:660
  60.0 18.7 %collective-permute-start.2 = (f32[1,3840]{1,0:T(1,128)}, f32[1,3840]{1,0:T(1,128)S(1)}, u32[]{:S(2)}, u32[]{:S(2)}) collective-permute-start(f32[1,3840]{1,0:T(1,128)} %get-tuple-element.32), channel_id=1, source_target_pairs={{0,1},{1,2},{2,3},{3,4},{4,5},{5,6},{6,7},{8,9},{9,10},{10,11},{11... | collective-permute-start | bytes 46088 | tf_op jit(solution)/shard_map/ppermute | solution.py:587
  61.8 16.8 %collective-permute-start.3 = (f32[1,3840]{1,0:T(1,128)}, f32[1,3840]{1,0:T(1,128)S(1)}, u32[]{:S(2)}, u32[]{:S(2)}) collective-permute-start(f32[1,3840]{1,0:T(1,128)} %get-tuple-element.33), channel_id=1, source_target_pairs={{1,0},{2,1},{3,2},{4,3},{5,4},{6,5},{7,6},{9,8},{10,9},{11,10},{12... | collective-permute-start | bytes 46088 | tf_op jit(solution)/shard_map/ppermute | solution.py:588
  70.7 9.3 %collective-permute-start.4 = (f32[1,128]{1,0:T(1,128)S(1)}, f32[1,128]{1,0:T(1,128)S(1)}, u32[]{:S(2)}, u32[]{:S(2)}) collective-permute-start(f32[1,128]{1,0:T(1,128)S(1)} %get-tuple-element.39), channel_id=1, source_target_pairs={{0,8},{8,16},{16,24},{24,32},{32,40},{40,48},{48,56},{56,64},{64,7... | collective-permute-start | bytes 1544 | tf_op jit(solution)/shard_map/ppermute | solution.py:587
  73.4 6.6 %collective-permute-start.5 = (f32[1,128]{1,0:T(1,128)S(1)}, f32[1,128]{1,0:T(1,128)S(1)}, u32[]{:S(2)}, u32[]{:S(2)}) collective-permute-start(f32[1,128]{1,0:T(1,128)S(1)} %get-tuple-element.40), channel_id=1, source_target_pairs={{8,0},{16,8},{24,16},{32,24},{40,32},{48,40},{56,48},{64,56},{72,6... | collective-permute-start | bytes 1544 | tf_op jit(solution)/shard_map/ppermute | solution.py:588
  78.7 1.3 %copy-start.6 = (f32[80,128]{1,0:T(8,128)S(1)}, f32[80,128]{1,0:T(8,128)}, u32[]{:S(2)}) copy-start(f32[80,128]{1,0:T(8,128)} %constant.11.clone.prof_ref) | copy-start | bytes 122884

commit v5 on v3

--- a/solution.py
+++ b/solution.py
@@ -207,16 +207,16 @@
 
     def columns(at, carry):
         parts = []
-        for spot in range(8):
+        for spot in range(16):
             for comp in range(2):
-                line = line_ref[pl.ds(32 * comp + 8 * at + spot, 1), :]
+                line = line_ref[pl.ds(32 * comp + 16 * at + spot, 1), :]
                 parts.append(jnp.where(unfold, jnp.broadcast_to(line, (24, 128)), 0.0))
         high, low = halves(jnp.concatenate(parts, axis=0))
         both = jnp.dot(high.astype(BF16), wcol_ref[...], preferred_element_type=F32) + jnp.dot(
             low.astype(BF16), wcol_ref[...], preferred_element_type=F32
         )
-        for spot in range(8):
-            column_ref[8 * at + spot] = both[48 * spot : 48 * spot + 48]
+        for spot in range(16):
+            column_ref[16 * at + spot] = both[48 * spot : 48 * spot + 48]
         return carry
 
     def result(slot):
@@ -307,7 +307,9 @@
             for k, value in enumerate(values):
                 done_ref[slot, pl.ds(first + k, 8, stride=16), :] = value
             burning = [jnp.exp(value) for value in values]
-            burning = [1.0 / (1.0 + value) for value in burning]
+            burning = [1.0 + value for value in burning]
+            guesses = [pl.reciprocal(value, approx=True) for value in burning]
+            burning = [y * (2.0 - x * y) for x, y in zip(burning, guesses)]
             packed = [word[block(first + k), :] for k in range(len(values))]
             heats = [((x >> 5) & 63).astype(F32) * y for x, y in zip(packed, burning)]
             smokes = [(x >> 11).astype(F32) * y for x, y in zip(packed, burning)]
@@ -324,7 +326,7 @@
     def into(target):
         return lambda first, values: store(target, first, values)
 
-    lax.fori_loop(0, 4, columns, 0)
+    lax.fori_loop(0, 2, columns, 0)
 
     def several(at, carry):
         slot = WIDE * at

time: 80.8 us -> 81.1 us (level)
  no operation moved by 1% of the time
where the time goes in v5:
time: 81.1 us; the launch traced here: 80.7 us
  starting transfers between devices  35.6 us (44%)
  Pallas kernels  27.1 us (33%)
  waiting for transfers between devices  13.7 us (17%)
  local copies, waits for them, and re-layouts  3.33 us (4%)
  between operations  0.85 us (1%)
    pallas_call x1, Pallas kernels, on_device(): pl.pallas_call(fire_kernel, out_shape=(shape(32, 128, 128), shape(N_GX *...  17.7 us
    ppermute x3, starting transfers between devices, neighbours(): after = lax.ppermute(first, axes, [(i + 1, i) for i in range(ends)])  12.4 us
    all_to_all x1, starting transfers between devices, on_device(): lax.all_to_all(windows, ('gx', 'gy'), split_axis=0, concat_axis=0, tiled=...  10.2 us
    ppermute x3, starting transfers between devices, neighbours(): before = lax.ppermute(last, axes, [(i, i + 1) for i in range(ends)])  8.36 us
    all_to_all x1, waiting for transfers between devices, on_device(): lax.all_to_all(message, ('gx', 'gy'), split_axis=0, concat_axis=0, tiled=...  6.8 us
    all_to_all x1, waiting for transfers between devices, on_device(): lax.all_to_all(windows, ('gx', 'gy'), split_axis=0, concat_axis=0, tiled=...  6.26 us
    all_to_all x1, starting transfers between devices, on_device(): lax.all_to_all(message, ('gx', 'gy'), split_axis=0, concat_axis=0, tiled=...  4.62 us
    unnamed x19, local copies, waits for them, and re-layouts  3.33 us
  transfers between devices with their start and end apart: 8, of which 3 were waited for; matrix products, arithmetic and copies ran while one was open for 1% of the time, Pallas kernels for 7%

profile of v5, /device:TPU:2, one launch (start us, length us, event | category | flops | bytes accessed | tf_op | source)
XLA Modules:
  0.0 80.7 jit_solution(13567044784752614130)
XLA Ops:
  0.6 0.0 copy-start
  0.6 1.8 %rows.1 = (f32[240,128]{1,0:T(8,128)}, f32[240,128]{1,0:T(8,128)}) custom-call(f32[240,16,128]{2,1,0:T(8,128)} %bitcast.2), custom_call_target="tpu_custom_call" | custom-call | flops 100000 | bytes 1000000 | tf_op jit(solution)/shard_map/rows/pallas_call | solution.py:593
  2.5 3.8 %collective-permute-start = (f32[240,128]{1,0:T(8,128)}, f32[240,128]{1,0:T(8,128)S(1)}, u32[]{:S(2)}, u32[]{:S(2)}) collective-permute-start(f32[240,128]{1,0:T(8,128)} %get-tuple-element.22), channel_id=1, source_target_pairs={{0,8},{8,16},{16,24},{24,32},{32,40},{40,48},{48,56},{56,64},{64,7... | collective-permute-start | bytes 368648 | tf_op jit(solution)/shard_map/ppermute | solution.py:583
  6.3 5.8 %collective-permute-start.1 = (f32[240,128]{1,0:T(8,128)}, f32[240,128]{1,0:T(8,128)S(1)}, u32[]{:S(2)}, u32[]{:S(2)}) collective-permute-start(f32[240,128]{1,0:T(8,128)} %get-tuple-element.23), channel_id=1, source_target_pairs={{8,0},{16,8},{24,16},{32,24},{40,32},{48,40},{56,48},{64,56},{72,6... | collective-permute-start | bytes 368648 | tf_op jit(solution)/shard_map/ppermute | solution.py:584
  12.1 0.8 copy.10.list_ref
  12.9 0.0 copy-done
  12.9 0.0 copy-start.3
  13.0 0.8 table.1
  13.7 0.6 sides.1
  14.3 0.0 copy-start.4
  14.3 0.0 copy-start.5
  14.4 0.0 collective-permute-done.above_ref
  14.4 0.6 collective-permute-done.1.below_ref
  15.0 1.0 %windows.1 = (f32[64,1,256]{2,1,0:T(1,128)}, f32[8,128]{1,0:T(8,128)S(1)}) custom-call(f32[128,256]{1,0:T(8,128)S(1)} %get-tuple-element.26.table_ref, bf16[64,128]{1,0:T(8,128)(2,1)S(1)} %get-tuple-element.27.choice_ref, f32[240,128]{1,0:T(8,128)S(1)} %collective-permute-done.above_ref, f32[240,128]{1,0:T(8,128)S(1)} %collective-permute-done.1.below_ref, ...), custom_call_target="tpu_custom_call" | custom-call | flops 1000000 | bytes 1000000 | tf_op jit(solution)/shard_map/windows/pallas_call | solution.py:614
  16.0 0.0 copy-done.3
  16.0 10.2 %all-to-all-start = ((f32[64,1,256]{2,1,0:T(1,128)}), f32[64,1,256]{2,1,0:T(1,128)S(1)}, u32[]{:S(2)}, u32[]{:S(2)}) async-start(f32[64,1,256]{2,1,0:T(1,128)} %get-tuple-element.30), calls=%async_computation | async-start | bytes 131072 | tf_op jit(solution)/shard_map/all_to_all | solution.py:621
  26.2 1.9 %air.1 = (f32[244,16,128]{2,1,0:T(8,128)S(1)}, f32[8,128]{1,0:T(8,128)S(1)}) custom-call(f32[240,16,128]{2,1,0:T(8,128)S(1)} %bitcast.5, f32[240,128]{1,0:T(8,128)S(1)} %collective-permute-done.above_ref, f32[240,128]{1,0:T(8,128)S(1)} %collective-permute-done.1.below_ref, f32[1,3840]{1,0:T(1,128)S(1)} %get-tuple-element.24.left_ref.left_in, ...), custom_call_target="tpu_custom_call" | custom-call | flops 200000000 | bytes 4000000 | tf_op jit(solution)/shard_map/air/pallas_call | solution.py:622
  28.1 0.0 copy-start.1
  28.1 1.3 %copy-done.1 = f32[244,16,128]{2,1,0:T(8,128)} copy-done((f32[244,16,128]{2,1,0:T(8,128)}, f32[244,16,128]{2,1,0:T(8,128)S(1)}, u32[]{:S(2)}) %copy-start.1) | copy-done | bytes 1998872
  29.4 0.0 copy-start.7
  29.4 0.6 copy-done.7
  30.0 6.3 %all-to-all-done.recv_ref = f32[64,1,256]{2,1,0:T(1,128)S(1)} async-done(((f32[64,1,256]{2,1,0:T(1,128)}), f32[64,1,256]{2,1,0:T(1,128)S(1)}, u32[]{:S(2)}, u32[]{:S(2)}) %all-to-all-start) | async-done | bytes 65568 | tf_op jit(solution)/shard_map/all_to_all | solution.py:621
  36.2 0.0 copy-start.8
  36.2 0.0 copy-done.4
  36.2 0.0 copy-done.5
  36.3 0.6 copy-done.8
  36.9 0.0 copy-start.2
  36.9 17.7 %fire.1 = (f32[32,128,128]{2,1,0:T(8,128)}, f32[64,1,256]{2,1,0:T(1,128)}, f32[1,3840]{1,0:T(1,128)}, f32[1,3840]{1,0:T(1,128)}) custom-call(s32[1,64,32]{2,1,0:T(8,128)} %copy-done.3, f32[32,128,128]{2,1,0:T(8,128)} %phase_in.1, s32[32,128,128]{2,1,0:T(8,128)} %fuel_in.1, f32[64,1,256]{2,1,0:T(1,128)} %copy-done.8, s32[8,128]{1,0:T(8,128)} %constant.8.clone.words_ref, ...), custom_call_target="tpu_custom_call" | custom-call | flops 1000000000 | bytes 8000000 | tf_op jit(solution)/shard_map/fire/pallas_call | solution.py:628
  54.6 4.6 %all-to-all-start.1 = ((f32[64,1,256]{2,1,0:T(1,128)}), f32[64,1,256]{2,1,0:T(1,128)S(1)}, u32[]{:S(2)}, u32[]{:S(2)}) async-start(f32[64,1,256]{2,1,0:T(1,128)} %get-tuple-element.35), calls=%async_computation.1 | async-start | bytes 131072 | tf_op jit(solution)/shard_map/all_to_all | solution.py:655
  59.2 1.8 %collective-permute-start.2 = (f32[1,3840]{1,0:T(1,128)}, f32[1,3840]{1,0:T(1,128)S(1)}, u32[]{:S(2)}, u32[]{:S(2)}) collective-permute-start(f32[1,3840]{1,0:T(1,128)} %get-tuple-element.32), channel_id=1, source_target_pairs={{0,1},{1,2},{2,3},{3,4},{4,5},{5,6},{6,7},{8,9},{9,10},{10,11},{11... | collective-permute-start | bytes 46088 | tf_op jit(solution)/shard_map/ppermute | solution.py:583
  61.1 1.3 %collective-permute-start.3 = (f32[1,3840]{1,0:T(1,128)}, f32[1,3840]{1,0:T(1,128)S(1)}, u32[]{:S(2)}, u32[]{:S(2)}) collective-permute-start(f32[1,3840]{1,0:T(1,128)} %get-tuple-element.33), channel_id=1, source_target_pairs={{1,0},{2,1},{3,2},{4,3},{5,4},{6,5},{7,6},{9,8},{10,9},{11,10},{12... | collective-permute-start | bytes 46088 | tf_op jit(solution)/shard_map/ppermute | solution.py:584
  62.4 6.8 %all-to-all-done.1.flux_ref = f32[64,1,256]{2,1,0:T(1,128)S(1)} async-done(((f32[64,1,256]{2,1,0:T(1,128)}), f32[64,1,256]{2,1,0:T(1,128)S(1)}, u32[]{:S(2)}, u32[]{:S(2)}) %all-to-all-start.1) | async-done | bytes 65568 | tf_op jit(solution)/shard_map/all_to_all | solution.py:655
  69.2 0.7 place.1
  69.9 2.7 %collective-permute-start.4 = (f32[1,128]{1,0:T(1,128)S(1)}, f32[1,128]{1,0:T(1,128)S(1)}, u32[]{:S(2)}, u32[]{:S(2)}) collective-permute-start(f32[1,128]{1,0:T(1,128)S(1)} %get-tuple-element.39), channel_id=1, source_target_pairs={{0,8},{8,16},{16,24},{24,32},{32,40},{40,48},{48,56},{56,64},{64,7... | collective-permute-start | bytes 1544 | tf_op jit(solution)/shard_map/ppermute | solution.py:583
  72.6 5.3 %collective-permute-start.5 = (f32[1,128]{1,0:T(1,128)S(1)}, f32[1,128]{1,0:T(1,128)S(1)}, u32[]{:S(2)}, u32[]{:S(2)}) collective-permute-start(f32[1,128]{1,0:T(1,128)S(1)} %get-tuple-element.40), channel_id=1, source_target_pairs={{8,0},{16,8},{24,16},{32,24},{40,32},{48,40},{56,48},{64,56},{72,6... | collective-permute-start | bytes 1544 | tf_op jit(solution)/shard_map/ppermute | solution.py:584
  77.9 0.0 collective-permute-done.2.left_ref
  77.9 0.0 collective-permute-done.3.right_ref
  77.9 0.0 copy-done.2
  77.9 0.0 copy-start.6
  78.0 1.3 %rims.1.part_ref = f32[240,16,128]{2,1,0:T(8,128)S(1)} custom-call(f32[244,16,128]{2,1,0:T(8,128)S(1)} %copy-done.2, f32[1,3840]{1,0:T(1,128)S(1)} %collective-permute-done.2.left_ref, f32[1,3840]{1,0:T(1,128)S(1)} %collective-permute-done.3.right_ref), custom_call_target="tpu_custom_call" | custom-call | flops 200000000 | bytes 4000000 | tf_op jit(solution)/shard_map/rims/pallas_call | solution.py:657
  79.3 0.0 collective-permute-done.4.above_ref
  79.3 0.0 collective-permute-done.5.below_ref
  79.3 0.0 copy-done.6
  79.3 1.4 %final.1 = f32[240,16,128]{2,1,0:T(8,128)} custom-call(f32[240,16,128]{2,1,0:T(8,128)S(1)} %rims.1.part_ref, f32[16,128]{1,0:T(8,128)S(1)} %get-tuple-element.36.heat_ref, f32[16,128]{1,0:T(8,128)S(1)} %get-tuple-element.37.side_ref, f32[16,128]{1,0:T(8,128)S(1)} %get-tuple-element.38.smoke_ref, f32[1,128]{1,0:T(1,128)S(1)} %collective-permute-done.4.above_ref, ...), custom_call_target="tpu_custom_call" | custom-call | flops 1000000 | bytes 4000000 | tf_op jit(solution)/shard_map/final/pallas_call | solution.py:668
Async XLA Ops:
  0.6 12.3 %copy-start = (f32[3,80,16,128]{3,2,1,0:T(8,128)S(1)}, f32[3,80,16,128]{3,2,1,0:T(8,128)}, u32[]{:S(2)}) copy-start(f32[3,80,16,128]{3,2,1,0:T(8,128)} %param.8) | copy-start | bytes 5898244
  2.5 11.9 %collective-permute-start = (f32[240,128]{1,0:T(8,128)}, f32[240,128]{1,0:T(8,128)S(1)}, u32[]{:S(2)}, u32[]{:S(2)}) collective-permute-start(f32[240,128]{1,0:T(8,128)} %get-tuple-element.22), channel_id=1, source_target_pairs={{0,8},{8,16},{16,24},{24,32},{32,40},{40,48},{48,56},{56,64},{64,7... | collective-permute-start | bytes 368648 | tf_op jit(solution)/shard_map/ppermute | solution.py:583
  6.3 8.7 %collective-permute-start.1 = (f32[240,128]{1,0:T(8,128)}, f32[240,128]{1,0:T(8,128)S(1)}, u32[]{:S(2)}, u32[]{:S(2)}) collective-permute-start(f32[240,128]{1,0:T(8,128)} %get-tuple-element.23), channel_id=1, source_target_pairs={{8,0},{16,8},{24,16},{32,24},{40,32},{48,40},{56,48},{64,56},{72,6... | collective-permute-start | bytes 368648 | tf_op jit(solution)/shard_map/ppermute | solution.py:584
  12.9 3.0 %copy-start.3 = (s32[1,64,32]{2,1,0:T(8,128)}, s32[1,64,32]{2,1,0:T(8,128)S(1)}, u32[]{:S(2)}) copy-start(s32[1,64,32]{2,1,0:T(8,128)S(1)} %copy.10.list_ref) | copy-start | bytes 24580
  14.3 21.9 %copy-start.4 = (f32[1,3840]{1,0:T(1,128)}, f32[1,3840]{1,0:T(1,128)S(1)}, u32[]{:S(2)}) copy-start(f32[1,3840]{1,0:T(1,128)S(1)} %get-tuple-element.24.left_ref.left_in) | copy-start | bytes 46084
  14.3 21.9 %copy-start.5 = (f32[1,3840]{1,0:T(1,128)}, f32[1,3840]{1,0:T(1,128)S(1)}, u32[]{:S(2)}) copy-start(f32[1,3840]{1,0:T(1,128)S(1)} %get-tuple-element.25.right_ref.right_in) | copy-start | bytes 46084
  16.0 20.3 %all-to-all-start = ((f32[64,1,256]{2,1,0:T(1,128)}), f32[64,1,256]{2,1,0:T(1,128)S(1)}, u32[]{:S(2)}, u32[]{:S(2)}) async-start(f32[64,1,256]{2,1,0:T(1,128)} %get-tuple-element.30), calls=%async_computation | async-start | bytes 131072 | tf_op jit(solution)/shard_map/all_to_all | solution.py:621
  28.1 1.3 %copy-start.1 = (f32[244,16,128]{2,1,0:T(8,128)}, f32[244,16,128]{2,1,0:T(8,128)S(1)}, u32[]{:S(2)}) copy-start(f32[244,16,128]{2,1,0:T(8,128)S(1)} %get-tuple-element.29.part_ref) | copy-start | bytes 5996548
  29.4 0.6 copy-start.7
  36.2 0.6 copy-start.8
  36.9 41.1 %copy-start.2 = (f32[244,16,128]{2,1,0:T(8,128)S(1)}, f32[244,16,128]{2,1,0:T(8,128)}, u32[]{:S(2)}) copy-start(f32[244,16,128]{2,1,0:T(8,128)} %copy-done.1) | copy-start | bytes 5996548
  54.6 14.6 %all-to-all-start.1 = ((f32[64,1,256]{2,1,0:T(1,128)}), f32[64,1,256]{2,1,0:T(1,128)S(1)}, u32[]{:S(2)}, u32[]{:S(2)}) async-start(f32[64,1,256]{2,1,0:T(1,128)} %get-tuple-element.35), calls=%async_computation.1 | async-start | bytes 131072 | tf_op jit(solution)/shard_map/all_to_all | solution.py:655
  59.2 18.7 %collective-permute-start.2 = (f32[1,3840]{1,0:T(1,128)}, f32[1,3840]{1,0:T(1,128)S(1)}, u32[]{:S(2)}, u32[]{:S(2)}) collective-permute-start(f32[1,3840]{1,0:T(1,128)} %get-tuple-element.32), channel_id=1, source_target_pairs={{0,1},{1,2},{2,3},{3,4},{4,5},{5,6},{6,7},{8,9},{9,10},{10,11},{11... | collective-permute-start | bytes 46088 | tf_op jit(solution)/shard_map/ppermute | solution.py:583
  61.1 16.8 %collective-permute-start.3 = (f32[1,3840]{1,0:T(1,128)}, f32[1,3840]{1,0:T(1,128)S(1)}, u32[]{:S(2)}, u32[]{:S(2)}) collective-permute-start(f32[1,3840]{1,0:T(1,128)} %get-tuple-element.33), channel_id=1, source_target_pairs={{1,0},{2,1},{3,2},{4,3},{5,4},{6,5},{7,6},{9,8},{10,9},{11,10},{12... | collective-permute-start | bytes 46088 | tf_op jit(solution)/shard_map/ppermute | solution.py:584
  69.9 9.3 %collective-permute-start.4 = (f32[1,128]{1,0:T(1,128)S(1)}, f32[1,128]{1,0:T(1,128)S(1)}, u32[]{:S(2)}, u32[]{:S(2)}) collective-permute-start(f32[1,128]{1,0:T(1,128)S(1)} %get-tuple-element.39), channel_id=1, source_target_pairs={{0,8},{8,16},{16,24},{24,32},{32,40},{40,48},{48,56},{56,64},{64,7... | collective-permute-start | bytes 1544 | tf_op jit(solution)/shard_map/ppermute | solution.py:583
  72.6 6.6 %collective-permute-start.5 = (f32[1,128]{1,0:T(1,128)S(1)}, f32[1,128]{1,0:T(1,128)S(1)}, u32[]{:S(2)}, u32[]{:S(2)}) collective-permute-start(f32[1,128]{1,0:T(1,128)S(1)} %get-tuple-element.40), channel_id=1, source_target_pairs={{8,0},{16,8},{24,16},{32,24},{40,32},{48,40},{56,48},{64,56},{72,6... | collective-permute-start | bytes 1544 | tf_op jit(solution)/shard_map/ppermute | solution.py:584
  77.9 1.3 %copy-start.6 = (f32[80,128]{1,0:T(8,128)S(1)}, f32[80,128]{1,0:T(8,128)}, u32[]{:S(2)}) copy-start(f32[80,128]{1,0:T(8,128)} %constant.11.clone.prof_ref) | copy-start | bytes 122884

commit v6 on v3

--- a/solution.py
+++ b/solution.py
@@ -226,15 +226,8 @@
         return slice(8 * at, 8 * at + 8)
 
     def store(target, at, values):
-        field, behind, beyond = target
-        turned = [pltpu.roll(value, 1, 1) for value in values]
         for k, value in enumerate(values):
-            field[block(at + k), :] = value
-        backs = [jnp.where(lane8 == 0, 0.0, x - y) for x, y in zip(values, turned)]
-        aheads = [pltpu.roll(back, 127, 1) for back in backs]
-        for k, (back, ahead) in enumerate(zip(backs, aheads)):
-            behind[block(at + k), :] = back
-            beyond[block(at + k), :] = ahead
+            target[block(at + k), :] = value
 
     def begin(slot, side):
         gust, rate, word = side[:3]
@@ -248,7 +241,7 @@
                 jnp.take_along_axis(words, fuel, axis=1, mode="promise_in_bounds")
                 for fuel in fuels
             ]
-            store(side[3:6], first, [phase_ref[slot, there, :] for there in places])
+            store(side[3], first, [phase_ref[slot, there, :] for there in places])
             bases = [(x & 31).astype(F32) * np.float32(0.05 * fire_time) for x in packed]
             for j, x, base in zip(blocks, packed, bases):
                 rate[block(j), :] = base
@@ -263,7 +256,7 @@
 
     def advance(side, source, keep):
         gust, rate = side[:2]
-        field, behind, beyond = source
+        field = source
         edge = field[block(0), :] - pltpu.roll(field[block(15), :], 1, 0)
         edge = jnp.where(row8 == 0, 0.0, edge)
         last = pltpu.roll(edge, 7, 0)
@@ -275,8 +268,10 @@
                 aheads.append(last)
             backs = [edge] + aheads[:-1]
             edge = aheads[-1]
-            side_backs = [behind[block(j), :] for j in blocks]
-            side_aheads = [beyond[block(j), :] for j in blocks]
+            side_backs = [
+                jnp.where(lane8 == 0, 0.0, x - pltpu.roll(x, 1, 1)) for x, _ in zip(fields, blocks)
+            ]
+            side_aheads = [pltpu.roll(x, 127, 1) for x in side_backs]
             a = [jnp.maximum(x, 0.0) for x in backs]
             b = [jnp.minimum(x, 0.0) for x in aheads]
             upwinds = [x * x + y * y for x, y in zip(a, b)]
@@ -316,7 +311,7 @@
                     terms = [x + y for x, y in zip(terms[::2], terms[1::2])]
                 total.append(terms[0])
 
-        advance(side, side[6:9], keep)
+        advance(side, side[4], keep)
         result(slot).start()
         sums_ref[slot, :, 0:128] = sum(sums[0])
         sums_ref[slot, :, 128:256] = sum(sums[1])
@@ -339,7 +334,7 @@
             begin(slot + spot, side)
         for step in range(SUB - 1):
             for side in sides:
-                pair_of = (side[3:6], side[6:9])
+                pair_of = (side[3], side[4])
                 advance(side, pair_of[step % 2], into(pair_of[1 - step % 2]))
         for spot, side in enumerate(sides):
             finish(slot + spot, side)
@@ -643,7 +638,7 @@
         + [pltpu.VMEM((256, 128), F32)] * WIDE
         + [pltpu.VMEM((128, 128), F32)] * WIDE
         + [pltpu.VMEM((128, 128), jnp.int32)] * WIDE
-        + [pltpu.VMEM((128, 128), F32)] * (6 * WIDE)
+        + [pltpu.VMEM((128, 128), F32)] * (2 * WIDE)
         + [pltpu.SemaphoreType.DMA((32,)), pltpu.SemaphoreType.DMA((6,))],
         compiler_params=room(60), name="fire", cost_estimate=cost(10**9, 8 * 10**6),
     )(

time: 80.8 us -> 80.8 us (level)
  no operation moved by 1% of the time
where the time goes in v6:
time: 80.8 us; the launch traced here: 80.4 us
  starting transfers between devices  35.6 us (44%)
  Pallas kernels  26.9 us (33%)
  waiting for transfers between devices  13.7 us (17%)
  local copies, waits for them, and re-layouts  3.33 us (4%)
  between operations  0.85 us (1%)
    pallas_call x1, Pallas kernels, on_device(): pl.pallas_call(fire_kernel, out_shape=(shape(32, 128, 128), shape(N_GX *...  17.5 us
    ppermute x3, starting transfers between devices, neighbours(): after = lax.ppermute(first, axes, [(i + 1, i) for i in range(ends)])  12.4 us
    all_to_all x1, starting transfers between devices, on_device(): lax.all_to_all(windows, ('gx', 'gy'), split_axis=0, concat_axis=0, tiled=...  10.2 us
    ppermute x3, starting transfers between devices, neighbours(): before = lax.ppermute(last, axes, [(i, i + 1) for i in range(ends)])  8.36 us
    all_to_all x1, waiting for transfers between devices, on_device(): lax.all_to_all(message, ('gx', 'gy'), split_axis=0, concat_axis=0, tiled=...  6.8 us
    all_to_all x1, waiting for transfers between devices, on_device(): lax.all_to_all(windows, ('gx', 'gy'), split_axis=0, concat_axis=0, tiled=...  6.26 us
    all_to_all x1, starting transfers between devices, on_device(): lax.all_to_all(message, ('gx', 'gy'), split_axis=0, concat_axis=0, tiled=...  4.62 us
    unnamed x19, local copies, waits for them, and re-layouts  3.33 us
  transfers between devices with their start and end apart: 8, of which 3 were waited for; matrix products, arithmetic and copies ran while one was open for 1% of the time, Pallas kernels for 7%

profile of v6, /device:TPU:2, one launch (start us, length us, event | category | flops | bytes accessed | tf_op | source)
XLA Modules:
  0.0 80.4 jit_solution(14218460222323472010)
XLA Ops:
  0.6 0.0 copy-start
  0.6 1.8 %rows.1 = (f32[240,128]{1,0:T(8,128)}, f32[240,128]{1,0:T(8,128)}) custom-call(f32[240,16,128]{2,1,0:T(8,128)} %bitcast.2), custom_call_target="tpu_custom_call" | custom-call | flops 100000 | bytes 1000000 | tf_op jit(solution)/shard_map/rows/pallas_call | solution.py:586
  2.5 3.8 %collective-permute-start = (f32[240,128]{1,0:T(8,128)}, f32[240,128]{1,0:T(8,128)S(1)}, u32[]{:S(2)}, u32[]{:S(2)}) collective-permute-start(f32[240,128]{1,0:T(8,128)} %get-tuple-element.22), channel_id=1, source_target_pairs={{0,8},{8,16},{16,24},{24,32},{32,40},{40,48},{48,56},{56,64},{64,7... | collective-permute-start | bytes 368648 | tf_op jit(solution)/shard_map/ppermute | solution.py:576
  6.3 5.8 %collective-permute-start.1 = (f32[240,128]{1,0:T(8,128)}, f32[240,128]{1,0:T(8,128)S(1)}, u32[]{:S(2)}, u32[]{:S(2)}) collective-permute-start(f32[240,128]{1,0:T(8,128)} %get-tuple-element.23), channel_id=1, source_target_pairs={{8,0},{16,8},{24,16},{32,24},{40,32},{48,40},{56,48},{64,56},{72,6... | collective-permute-start | bytes 368648 | tf_op jit(solution)/shard_map/ppermute | solution.py:577
  12.1 0.8 copy.10.list_ref
  12.9 0.0 copy-done
  12.9 0.0 copy-start.3
  13.0 0.8 table.1
  13.7 0.6 sides.1
  14.3 0.0 copy-start.4
  14.3 0.0 copy-start.5
  14.4 0.0 collective-permute-done.above_ref
  14.4 0.6 collective-permute-done.1.below_ref
  15.0 1.0 %windows.1 = (f32[64,1,256]{2,1,0:T(1,128)}, f32[8,128]{1,0:T(8,128)S(1)}) custom-call(f32[128,256]{1,0:T(8,128)S(1)} %get-tuple-element.26.table_ref, bf16[64,128]{1,0:T(8,128)(2,1)S(1)} %get-tuple-element.27.choice_ref, f32[240,128]{1,0:T(8,128)S(1)} %collective-permute-done.above_ref, f32[240,128]{1,0:T(8,128)S(1)} %collective-permute-done.1.below_ref, ...), custom_call_target="tpu_custom_call" | custom-call | flops 1000000 | bytes 1000000 | tf_op jit(solution)/shard_map/windows/pallas_call | solution.py:607
  16.0 0.0 copy-done.3
  16.0 10.2 %all-to-all-start = ((f32[64,1,256]{2,1,0:T(1,128)}), f32[64,1,256]{2,1,0:T(1,128)S(1)}, u32[]{:S(2)}, u32[]{:S(2)}) async-start(f32[64,1,256]{2,1,0:T(1,128)} %get-tuple-element.30), calls=%async_computation | async-start | bytes 131072 | tf_op jit(solution)/shard_map/all_to_all | solution.py:614
  26.2 1.9 %air.1 = (f32[244,16,128]{2,1,0:T(8,128)S(1)}, f32[8,128]{1,0:T(8,128)S(1)}) custom-call(f32[240,16,128]{2,1,0:T(8,128)S(1)} %bitcast.5, f32[240,128]{1,0:T(8,128)S(1)} %collective-permute-done.above_ref, f32[240,128]{1,0:T(8,128)S(1)} %collective-permute-done.1.below_ref, f32[1,3840]{1,0:T(1,128)S(1)} %get-tuple-element.24.left_ref.left_in, ...), custom_call_target="tpu_custom_call" | custom-call | flops 200000000 | bytes 4000000 | tf_op jit(solution)/shard_map/air/pallas_call | solution.py:615
  28.1 0.0 copy-start.1
  28.1 1.3 %copy-done.1 = f32[244,16,128]{2,1,0:T(8,128)} copy-done((f32[244,16,128]{2,1,0:T(8,128)}, f32[244,16,128]{2,1,0:T(8,128)S(1)}, u32[]{:S(2)}) %copy-start.1) | copy-done | bytes 1998872
  29.4 0.0 copy-start.7
  29.4 0.6 copy-done.7
  30.0 6.3 %all-to-all-done.recv_ref = f32[64,1,256]{2,1,0:T(1,128)S(1)} async-done(((f32[64,1,256]{2,1,0:T(1,128)}), f32[64,1,256]{2,1,0:T(1,128)S(1)}, u32[]{:S(2)}, u32[]{:S(2)}) %all-to-all-start) | async-done | bytes 65568 | tf_op jit(solution)/shard_map/all_to_all | solution.py:614
  36.2 0.0 copy-start.8
  36.2 0.0 copy-done.4
  36.2 0.0 copy-done.5
  36.3 0.6 copy-done.8
  36.9 0.0 copy-start.2
  36.9 17.5 %fire.1 = (f32[32,128,128]{2,1,0:T(8,128)}, f32[64,1,256]{2,1,0:T(1,128)}, f32[1,3840]{1,0:T(1,128)}, f32[1,3840]{1,0:T(1,128)}) custom-call(s32[1,64,32]{2,1,0:T(8,128)} %copy-done.3, f32[32,128,128]{2,1,0:T(8,128)} %phase_in.1, s32[32,128,128]{2,1,0:T(8,128)} %fuel_in.1, f32[64,1,256]{2,1,0:T(1,128)} %copy-done.8, s32[8,128]{1,0:T(8,128)} %constant.8.clone.words_ref, ...), custom_call_target="tpu_custom_call" | custom-call | flops 1000000000 | bytes 8000000 | tf_op jit(solution)/shard_map/fire/pallas_call | solution.py:621
  54.3 4.6 %all-to-all-start.1 = ((f32[64,1,256]{2,1,0:T(1,128)}), f32[64,1,256]{2,1,0:T(1,128)S(1)}, u32[]{:S(2)}, u32[]{:S(2)}) async-start(f32[64,1,256]{2,1,0:T(1,128)} %get-tuple-element.35), calls=%async_computation.1 | async-start | bytes 131072 | tf_op jit(solution)/shard_map/all_to_all | solution.py:648
  59.0 1.8 %collective-permute-start.2 = (f32[1,3840]{1,0:T(1,128)}, f32[1,3840]{1,0:T(1,128)S(1)}, u32[]{:S(2)}, u32[]{:S(2)}) collective-permute-start(f32[1,3840]{1,0:T(1,128)} %get-tuple-element.32), channel_id=1, source_target_pairs={{0,1},{1,2},{2,3},{3,4},{4,5},{5,6},{6,7},{8,9},{9,10},{10,11},{11... | collective-permute-start | bytes 46088 | tf_op jit(solution)/shard_map/ppermute | solution.py:576
  60.8 1.3 %collective-permute-start.3 = (f32[1,3840]{1,0:T(1,128)}, f32[1,3840]{1,0:T(1,128)S(1)}, u32[]{:S(2)}, u32[]{:S(2)}) collective-permute-start(f32[1,3840]{1,0:T(1,128)} %get-tuple-element.33), channel_id=1, source_target_pairs={{1,0},{2,1},{3,2},{4,3},{5,4},{6,5},{7,6},{9,8},{10,9},{11,10},{12... | collective-permute-start | bytes 46088 | tf_op jit(solution)/shard_map/ppermute | solution.py:577
  62.1 6.8 %all-to-all-done.1.flux_ref = f32[64,1,256]{2,1,0:T(1,128)S(1)} async-done(((f32[64,1,256]{2,1,0:T(1,128)}), f32[64,1,256]{2,1,0:T(1,128)S(1)}, u32[]{:S(2)}, u32[]{:S(2)}) %all-to-all-start.1) | async-done | bytes 65568 | tf_op jit(solution)/shard_map/all_to_all | solution.py:648
  68.9 0.7 place.1
  69.7 2.7 %collective-permute-start.4 = (f32[1,128]{1,0:T(1,128)S(1)}, f32[1,128]{1,0:T(1,128)S(1)}, u32[]{:S(2)}, u32[]{:S(2)}) collective-permute-start(f32[1,128]{1,0:T(1,128)S(1)} %get-tuple-element.39), channel_id=1, source_target_pairs={{0,8},{8,16},{16,24},{24,32},{32,40},{40,48},{48,56},{56,64},{64,7... | collective-permute-start | bytes 1544 | tf_op jit(solution)/shard_map/ppermute | solution.py:576
  72.4 5.3 %collective-permute-start.5 = (f32[1,128]{1,0:T(1,128)S(1)}, f32[1,128]{1,0:T(1,128)S(1)}, u32[]{:S(2)}, u32[]{:S(2)}) collective-permute-start(f32[1,128]{1,0:T(1,128)S(1)} %get-tuple-element.40), channel_id=1, source_target_pairs={{8,0},{16,8},{24,16},{32,24},{40,32},{48,40},{56,48},{64,56},{72,6... | collective-permute-start | bytes 1544 | tf_op jit(solution)/shard_map/ppermute | solution.py:577
  77.6 0.0 collective-permute-done.2.left_ref
  77.7 0.0 collective-permute-done.3.right_ref
  77.7 0.0 copy-done.2
  77.7 0.0 copy-start.6
  77.7 1.3 %rims.1.part_ref = f32[240,16,128]{2,1,0:T(8,128)S(1)} custom-call(f32[244,16,128]{2,1,0:T(8,128)S(1)} %copy-done.2, f32[1,3840]{1,0:T(1,128)S(1)} %collective-permute-done.2.left_ref, f32[1,3840]{1,0:T(1,128)S(1)} %collective-permute-done.3.right_ref), custom_call_target="tpu_custom_call" | custom-call | flops 200000000 | bytes 4000000 | tf_op jit(solution)/shard_map/rims/pallas_call | solution.py:650
  79.0 0.0 collective-permute-done.4.above_ref
  79.0 0.0 collective-permute-done.5.below_ref
  79.0 0.0 copy-done.6
  79.0 1.4 %final.1 = f32[240,16,128]{2,1,0:T(8,128)} custom-call(f32[240,16,128]{2,1,0:T(8,128)S(1)} %rims.1.part_ref, f32[16,128]{1,0:T(8,128)S(1)} %get-tuple-element.36.heat_ref, f32[16,128]{1,0:T(8,128)S(1)} %get-tuple-element.37.side_ref, f32[16,128]{1,0:T(8,128)S(1)} %get-tuple-element.38.smoke_ref, f32[1,128]{1,0:T(1,128)S(1)} %collective-permute-done.4.above_ref, ...), custom_call_target="tpu_custom_call" | custom-call | flops 1000000 | bytes 4000000 | tf_op jit(solution)/shard_map/final/pallas_call | solution.py:661
Async XLA Ops:
  0.6 12.3 %copy-start = (f32[3,80,16,128]{3,2,1,0:T(8,128)S(1)}, f32[3,80,16,128]{3,2,1,0:T(8,128)}, u32[]{:S(2)}) copy-start(f32[3,80,16,128]{3,2,1,0:T(8,128)} %param.8) | copy-start | bytes 5898244
  2.5 11.9 %collective-permute-start = (f32[240,128]{1,0:T(8,128)}, f32[240,128]{1,0:T(8,128)S(1)}, u32[]{:S(2)}, u32[]{:S(2)}) collective-permute-start(f32[240,128]{1,0:T(8,128)} %get-tuple-element.22), channel_id=1, source_target_pairs={{0,8},{8,16},{16,24},{24,32},{32,40},{40,48},{48,56},{56,64},{64,7... | collective-permute-start | bytes 368648 | tf_op jit(solution)/shard_map/ppermute | solution.py:576
  6.3 8.7 %collective-permute-start.1 = (f32[240,128]{1,0:T(8,128)}, f32[240,128]{1,0:T(8,128)S(1)}, u32[]{:S(2)}, u32[]{:S(2)}) collective-permute-start(f32[240,128]{1,0:T(8,128)} %get-tuple-element.23), channel_id=1, source_target_pairs={{8,0},{16,8},{24,16},{32,24},{40,32},{48,40},{56,48},{64,56},{72,6... | collective-permute-start | bytes 368648 | tf_op jit(solution)/shard_map/ppermute | solution.py:577
  12.9 3.0 %copy-start.3 = (s32[1,64,32]{2,1,0:T(8,128)}, s32[1,64,32]{2,1,0:T(8,128)S(1)}, u32[]{:S(2)}) copy-start(s32[1,64,32]{2,1,0:T(8,128)S(1)} %copy.10.list_ref) | copy-start | bytes 24580
  14.3 21.9 %copy-start.4 = (f32[1,3840]{1,0:T(1,128)}, f32[1,3840]{1,0:T(1,128)S(1)}, u32[]{:S(2)}) copy-start(f32[1,3840]{1,0:T(1,128)S(1)} %get-tuple-element.24.left_ref.left_in) | copy-start | bytes 46084
  14.3 21.9 %copy-start.5 = (f32[1,3840]{1,0:T(1,128)}, f32[1,3840]{1,0:T(1,128)S(1)}, u32[]{:S(2)}) copy-start(f32[1,3840]{1,0:T(1,128)S(1)} %get-tuple-element.25.right_ref.right_in) | copy-start | bytes 46084
  16.0 20.3 %all-to-all-start = ((f32[64,1,256]{2,1,0:T(1,128)}), f32[64,1,256]{2,1,0:T(1,128)S(1)}, u32[]{:S(2)}, u32[]{:S(2)}) async-start(f32[64,1,256]{2,1,0:T(1,128)} %get-tuple-element.30), calls=%async_computation | async-start | bytes 131072 | tf_op jit(solution)/shard_map/all_to_all | solution.py:614
  28.1 1.3 %copy-start.1 = (f32[244,16,128]{2,1,0:T(8,128)}, f32[244,16,128]{2,1,0:T(8,128)S(1)}, u32[]{:S(2)}) copy-start(f32[244,16,128]{2,1,0:T(8,128)S(1)} %get-tuple-element.29.part_ref) | copy-start | bytes 5996548
  29.4 0.6 copy-start.7
  36.2 0.6 copy-start.8
  36.9 40.8 %copy-start.2 = (f32[244,16,128]{2,1,0:T(8,128)S(1)}, f32[244,16,128]{2,1,0:T(8,128)}, u32[]{:S(2)}) copy-start(f32[244,16,128]{2,1,0:T(8,128)} %copy-done.1) | copy-start | bytes 5996548
  54.3 14.6 %all-to-all-start.1 = ((f32[64,1,256]{2,1,0:T(1,128)}), f32[64,1,256]{2,1,0:T(1,128)S(1)}, u32[]{:S(2)}, u32[]{:S(2)}) async-start(f32[64,1,256]{2,1,0:T(1,128)} %get-tuple-element.35), calls=%async_computation.1 | async-start | bytes 131072 | tf_op jit(solution)/shard_map/all_to_all | solution.py:648
  59.0 18.7 %collective-permute-start.2 = (f32[1,3840]{1,0:T(1,128)}, f32[1,3840]{1,0:T(1,128)S(1)}, u32[]{:S(2)}, u32[]{:S(2)}) collective-permute-start(f32[1,3840]{1,0:T(1,128)} %get-tuple-element.32), channel_id=1, source_target_pairs={{0,1},{1,2},{2,3},{3,4},{4,5},{5,6},{6,7},{8,9},{9,10},{10,11},{11... | collective-permute-start | bytes 46088 | tf_op jit(solution)/shard_map/ppermute | solution.py:576
  60.8 16.8 %collective-permute-start.3 = (f32[1,3840]{1,0:T(1,128)}, f32[1,3840]{1,0:T(1,128)S(1)}, u32[]{:S(2)}, u32[]{:S(2)}) collective-permute-start(f32[1,3840]{1,0:T(1,128)} %get-tuple-element.33), channel_id=1, source_target_pairs={{1,0},{2,1},{3,2},{4,3},{5,4},{6,5},{7,6},{9,8},{10,9},{11,10},{12... | collective-permute-start | bytes 46088 | tf_op jit(solution)/shard_map/ppermute | solution.py:577
  69.7 9.3 %collective-permute-start.4 = (f32[1,128]{1,0:T(1,128)S(1)}, f32[1,128]{1,0:T(1,128)S(1)}, u32[]{:S(2)}, u32[]{:S(2)}) collective-permute-start(f32[1,128]{1,0:T(1,128)S(1)} %get-tuple-element.39), channel_id=1, source_target_pairs={{0,8},{8,16},{16,24},{24,32},{32,40},{40,48},{48,56},{56,64},{64,7... | collective-permute-start | bytes 1544 | tf_op jit(solution)/shard_map/ppermute | solution.py:576
  72.4 6.6 %collective-permute-start.5 = (f32[1,128]{1,0:T(1,128)S(1)}, f32[1,128]{1,0:T(1,128)S(1)}, u32[]{:S(2)}, u32[]{:S(2)}) collective-permute-start(f32[1,128]{1,0:T(1,128)S(1)} %get-tuple-element.40), channel_id=1, source_target_pairs={{8,0},{16,8},{24,16},{32,24},{40,32},{48,40},{56,48},{64,56},{72,6... | collective-permute-start | bytes 1544 | tf_op jit(solution)/shard_map/ppermute | solution.py:577
  77.7 1.3 %copy-start.6 = (f32[80,128]{1,0:T(8,128)S(1)}, f32[80,128]{1,0:T(8,128)}, u32[]{:S(2)}) copy-start(f32[80,128]{1,0:T(8,128)} %constant.11.clone.prof_ref) | copy-start | bytes 122884
